TPU v7x, 32 devices: a whole 2x2x4 slice. The times are simulated.
32 devices in a mesh: dp: 1, seq: 32 (over z, y, x, core).
Axes of the slice: x: 2, y: 2, z: 4, core: 2. Of those that a mesh axis runs over, the one named last changes fastest.
Arguments:
- queries: bfloat16 [1, 8192, 2048], P('dp', 'seq'), may hold values from -40 to 40
- keys: bfloat16 [1, 8192, 2048], P('dp', 'seq'), may hold values from -40 to 40
- values: bfloat16 [1, 8192, 2048], P('dp', 'seq'), may hold values from -6 to 6
- key_gain: float32 [2048], replicated, may hold values from 0.25 to 1.75
- random_blocks: int32 [16, 128, 3], P(None, 'seq'), may hold values from 2 to 127, as said below
- out_grad: bfloat16 [1, 8192, 2048], P('dp', 'seq'), may hold values from -6 to 6
Outputs:
- attended: bfloat16 [1, 8192, 2048], P('dp', 'seq')
- query_grad: bfloat16 [1, 8192, 2048], P('dp', 'seq')
- key_grad: bfloat16 [1, 8192, 2048], P('dp', 'seq')
- value_grad: bfloat16 [1, 8192, 2048], P('dp', 'seq')
- gain_grad: float32 [2048], replicated
Inputs may be any that keep to these rules, and one draw needn't show every extreme that they name: `random_blocks`: for the 4 query blocks of one device, all heads and entries together, at most 9 entries name blocks held by any one device (blocks d * 4 to d * 4 + 3), and exactly 9 name the blocks of some device.
All inputs are finite; a program needn't handle non-finite values.
Results may differ from a plain program's by a relative error of at most 0.03.
The roundings to bfloat16 on the way count: a program that leaves them out, or rounds other values in their place, can miss the bound.
Values may be sent and summed in bfloat16 or wider, within the bound.
A program may use at most 128 MiB of HBM per device.

v0:
```python
import math

import jax
import jax.numpy as jnp
from jax import lax
from jax.sharding import PartitionSpec as P

HEADS = 16
HD = 128
BLOCK = 64
NG = 2
NR = 3
NK = 8


NEGATIVE = -1e30


def broadcast(block, axis, owner):
    block = jnp.where(lax.axis_index(axis) == owner, block, jnp.zeros_like(block))
    return lax.psum(block, axis)


def padded_2(cells, sides, width):
    for axis, dim in sides:
        count = lax.axis_size(axis)
        ends = count - 1
        head = lax.slice_in_dim(cells, 0, width, axis=dim)
        tail = lax.slice_in_dim(cells, cells.shape[dim] - width, cells.shape[dim], axis=dim)
        cells = jnp.concatenate(
            [
                lax.ppermute(tail, axis, [(i, (i + 1) % count) for i in range(ends)]),
                cells,
                lax.ppermute(head, axis, [((i + 1) % count, i) for i in range(ends)]),
            ],
            axis=dim,
        )
    return cells


def passed_along(array, axis, by):
    length = lax.axis_size(axis)
    pairs = [(i, i + by) for i in range(length) if 0 <= i + by < length]
    return lax.ppermute(array, axis, pairs)


def to_heads(rows_in):
    return rows_in.reshape(rows_in.shape[0] // BLOCK, BLOCK, HEADS, HD).transpose(2, 0, 1, 3)


def from_heads(blocks_in):
    return blocks_in.transpose(1, 2, 0, 3).reshape(1, blocks_in.shape[1] * BLOCK, HEADS * HD)


def build_list(edge_part, window_part, random_in):
    head_count = random_in.shape[0]
    block_count = random_in.shape[1]
    global_list = jnp.broadcast_to(
        edge_part[:, None], (head_count, block_count) + edge_part.shape[1:]
    )
    window_list = jnp.stack(
        [window_part[:, offset : offset + block_count] for offset in range(3)], axis=2
    )
    joined = jnp.concatenate([global_list, window_list, random_in], axis=2)
    return joined.reshape(head_count, block_count, NK * BLOCK, HD)


def spread_terms(coef, rows_in):
    head_count = rows_in.shape[0]
    block_count = rows_in.shape[1]
    coef_blocks = coef.reshape(head_count, block_count, BLOCK, NK, BLOCK)
    global_term = jnp.einsum(
        "hpbgc,hpbd->hgcd", coef_blocks[:, :, :, :NG], rows_in, preferred_element_type=jnp.float32
    )
    padded = jnp.zeros((head_count, block_count + 2, BLOCK, HD), jnp.float32)
    for offset in range(3):
        term = jnp.einsum(
            "hpbc,hpbd->hpcd",
            coef_blocks[:, :, :, NG + offset],
            rows_in,
            preferred_element_type=jnp.float32,
        )
        padded = padded + jnp.pad(term, ((0, 0), (offset, 2 - offset), (0, 0), (0, 0)))
    random_term = jnp.einsum(
        "hpbrc,hpbd->hprcd",
        coef_blocks[:, :, :, NG + 3 :],
        rows_in,
        preferred_element_type=jnp.float32,
    )
    return (global_term, padded, random_term)


def sparse_group(
    query_blk,
    edge_key,
    edge_value,
    window_key,
    window_value,
    random_key,
    random_value,
    grad_blk,
    valid_keys,
    keep_rows,
):
    score_scale = HD ** (-0.5)
    key_list = build_list(edge_key, window_key, random_key)
    value_list = build_list(edge_value, window_value, random_value)
    key_mask = jnp.repeat(valid_keys, BLOCK, axis=1)[None, :, None, :]
    scores = (
        jnp.einsum("hpbd,hpnd->hpbn", query_blk, key_list, preferred_element_type=jnp.float32)
        * score_scale
    )
    scores = jnp.where(key_mask, scores, NEGATIVE)
    row_top = jnp.max(scores, axis=3, keepdims=True)
    expo_vals = jnp.where(key_mask, jnp.exp(scores - row_top), 0.0)
    row_total = jnp.sum(expo_vals, axis=3, keepdims=True)
    numerator = jnp.einsum(
        "hpbn,hpnd->hpbd",
        expo_vals.astype(jnp.bfloat16),
        value_list,
        preferred_element_type=jnp.float32,
    )
    attended = (numerator / row_total).astype(jnp.bfloat16)
    row_delta = jnp.sum(grad_blk.astype(jnp.float32) * attended.astype(jnp.float32), axis=3)
    weights = expo_vals / row_total * keep_rows[None, :, None, None]
    dprobs = jnp.einsum("hpbd,hpnd->hpbn", grad_blk, value_list, preferred_element_type=jnp.float32)
    dscores = (weights * (dprobs - row_delta[:, :, :, None]) * score_scale).astype(jnp.bfloat16)
    dquery = jnp.einsum("hpbn,hpnd->hpbd", dscores, key_list, preferred_element_type=jnp.float32)
    key_global, key_padded, key_random = spread_terms(dscores, query_blk)
    value_global, value_padded, value_random = spread_terms(weights.astype(jnp.bfloat16), grad_blk)
    global_part = jnp.stack([key_global, value_global], axis=1)
    padded = jnp.stack([key_padded, value_padded], axis=1)
    random_part = jnp.stack([key_random, value_random], axis=1)
    return (attended, dquery, global_part, padded, random_part)


def shards(queries, keys, values, key_gain, random_blocks, out_grad):
    score_scale = HD ** (-0.5)
    tok_count = queries.shape[1]
    per_dev = tok_count // BLOCK
    owners = lax.axis_size("seq")
    seq_place = lax.axis_index("seq")
    total_blocks = owners * per_dev
    first_block = seq_place * per_dev
    key_eff = (keys[0].astype(jnp.float32) * key_gain).astype(jnp.bfloat16)
    edge_count = NG * BLOCK
    edge_rows = broadcast(
        jnp.stack(
            [
                queries[0, :edge_count],
                key_eff[:edge_count],
                values[0, :edge_count],
                out_grad[0, :edge_count],
            ]
        ),
        "seq",
        0,
    )
    window_rows = padded_2(jnp.stack([key_eff, values[0]]), (("seq", 1),), BLOCK)
    query_h = to_heads(queries[0])
    key_h = to_heads(key_eff)
    value_h = to_heads(values[0])
    grad_h = to_heads(out_grad[0])
    edge_heads = [to_heads(edge_rows[slot_pick]) for slot_pick in range(4)]
    window_key = to_heads(window_rows[0])
    window_value = to_heads(window_rows[1])
    request_count = HEADS * per_dev * NR
    capacity = (request_count + owners - 1) // owners + 3
    target = random_blocks.reshape(request_count)
    owner_dev = target // per_dev
    table_index = (
        jnp.arange(request_count, dtype=jnp.int32) // (per_dev * NR) * per_dev + target % per_dev
    )
    onehot = (owner_dev[:, None] == jnp.arange(owners, dtype=jnp.int32)[None, :]).astype(jnp.int32)
    before = jnp.cumsum(onehot, axis=0) - onehot
    slot_rank = jnp.sum(before * onehot, axis=1)
    position = owner_dev * capacity + slot_rank
    outgoing = (
        jnp.full((owners * capacity,), -1, jnp.int32)
        .at[position]
        .set(table_index)
        .reshape(owners, capacity)
    )
    kv_table = jnp.concatenate([key_h, value_h], axis=3).reshape(HEADS * per_dev, BLOCK, 2 * HD)
    index_part = lax.all_to_all(outgoing, "seq", split_axis=0, concat_axis=0, tiled=True)
    picked = kv_table[jnp.clip(index_part, 0, HEADS * per_dev - 1)]
    fetch_result = (
        lax.all_to_all(picked, "seq", split_axis=0, concat_axis=0, tiled=True),
        index_part,
    )
    arrived, served = fetch_result
    fetched = arrived.reshape(owners * capacity, BLOCK, 2 * HD)[position].reshape(
        HEADS, per_dev, NR, BLOCK, 2 * HD
    )
    fetched_key = fetched[..., :HD]
    fetched_value = fetched[..., HD:]
    block_index = first_block + jnp.arange(per_dev, dtype=jnp.int32)
    window_index = block_index[:, None] + jnp.arange(-1, 2, dtype=jnp.int32)[None, :]
    valid_keys = jnp.concatenate(
        [
            jnp.ones((per_dev, NG), bool),
            (window_index >= NG) & (window_index < total_blocks),
            jnp.ones((per_dev, NR), bool),
        ],
        axis=1,
    )
    keep_rows = (block_index >= NG).astype(jnp.float32)
    group_size = math.gcd(HEADS, 4)

    def by_group(array_in):
        return array_in.reshape((HEADS // group_size, group_size) + array_in.shape[1:])

    def merge_groups(array_in):
        return array_in.reshape((HEADS,) + array_in.shape[2:])

    def run_group(bundle):
        return sparse_group(
            bundle[0],
            bundle[1],
            bundle[2],
            bundle[3],
            bundle[4],
            bundle[5],
            bundle[6],
            bundle[7],
            valid_keys,
            keep_rows,
        )

    grouped = lax.map(
        run_group,
        (
            by_group(query_h),
            by_group(edge_heads[1]),
            by_group(edge_heads[2]),
            by_group(window_key),
            by_group(window_value),
            by_group(fetched_key),
            by_group(fetched_value),
            by_group(grad_h),
        ),
    )
    attended_h, dquery_h, global_part, padded, random_part = [
        merge_groups(piece_out) for piece_out in grouped
    ]
    edge_query = edge_heads[0].reshape(HEADS, edge_count, HD)
    edge_grad = edge_heads[3].reshape(HEADS, edge_count, HD)
    flat_key = key_h.reshape(HEADS, tok_count, HD)
    flat_value = value_h.reshape(HEADS, tok_count, HD)
    edge_scores = (
        jnp.einsum("hqd,htd->hqt", edge_query, flat_key, preferred_element_type=jnp.float32)
        * score_scale
    )
    edge_top = lax.pmax(jnp.max(edge_scores, axis=2), "seq")
    edge_expo = jnp.exp(edge_scores - edge_top[:, :, None])
    edge_total, edge_numer = lax.psum(
        (
            jnp.sum(edge_expo, axis=2),
            jnp.einsum(
                "hqt,htd->hqd",
                edge_expo.astype(jnp.bfloat16),
                flat_value,
                preferred_element_type=jnp.float32,
            ),
        ),
        "seq",
    )
    edge_out = (edge_numer / edge_total[:, :, None]).astype(jnp.bfloat16)
    edge_delta = jnp.sum(edge_grad.astype(jnp.float32) * edge_out.astype(jnp.float32), axis=2)
    edge_weights = edge_expo / edge_total[:, :, None]
    edge_dprobs = jnp.einsum(
        "hqd,htd->hqt", edge_grad, flat_value, preferred_element_type=jnp.float32
    )
    edge_dscores = (edge_weights * (edge_dprobs - edge_delta[:, :, None]) * score_scale).astype(
        jnp.bfloat16
    )
    edge_dquery = jnp.einsum(
        "hqt,htd->hqd", edge_dscores, flat_key, preferred_element_type=jnp.float32
    )
    local_dkey = jnp.einsum(
        "hqt,hqd->htd", edge_dscores, edge_query, preferred_element_type=jnp.float32
    )
    local_dvalue = jnp.einsum(
        "hqt,hqd->htd",
        edge_weights.astype(jnp.bfloat16),
        edge_grad,
        preferred_element_type=jnp.float32,
    )
    random_rounded = (
        random_part.transpose(0, 2, 3, 4, 1, 5)
        .reshape(request_count, BLOCK, 2 * HD)
        .astype(jnp.bfloat16)
    )
    sendback = (
        jnp.zeros((owners * capacity, BLOCK, 2 * HD), jnp.bfloat16)
        .at[position]
        .set(random_rounded)
        .reshape(owners, capacity, BLOCK, 2 * HD)
    )
    returned = lax.all_to_all(sendback, "seq", split_axis=0, concat_axis=0, tiled=True)
    owner_table = (
        served.reshape(1, owners * capacity)
        == jnp.arange(HEADS * per_dev, dtype=jnp.int32)[:, None]
    ).astype(jnp.bfloat16)
    summed = jnp.dot(
        owner_table,
        returned.reshape(owners * capacity, BLOCK * 2 * HD),
        preferred_element_type=jnp.float32,
    )
    summed = summed.reshape(HEADS, per_dev, BLOCK, 2, HD).transpose(0, 3, 1, 2, 4)
    from_right = passed_along(padded[:, :, 0].astype(jnp.bfloat16), "seq", -1).astype(jnp.float32)
    from_left = passed_along(padded[:, :, per_dev + 1].astype(jnp.bfloat16), "seq", 1).astype(
        jnp.float32
    )
    edge_dquery_sum, global_sum = lax.psum((edge_dquery, global_part), "seq")
    accum = padded[:, :, 1 : per_dev + 1]
    accum = accum + jnp.stack([local_dkey, local_dvalue], axis=1).reshape(
        HEADS, 2, per_dev, BLOCK, HD
    )
    accum = accum + summed
    accum = accum.at[:, :, per_dev - 1].add(from_right)
    accum = accum.at[:, :, 0].add(from_left)
    is_first = (seq_place == 0).astype(jnp.float32)
    accum = accum.at[:, :, :NG].add(global_sum * is_first)
    is_edge = (block_index < NG)[None, :, None, None]
    tail_zeros = jnp.zeros((HEADS, per_dev - NG, BLOCK, HD), jnp.float32)
    edge_dq_blocks = jnp.concatenate(
        [edge_dquery_sum.reshape(HEADS, NG, BLOCK, HD), tail_zeros], axis=1
    )
    edge_out_blocks = jnp.concatenate(
        [edge_out.reshape(HEADS, NG, BLOCK, HD), tail_zeros.astype(jnp.bfloat16)], axis=1
    )
    dquery_all = jnp.where(is_edge, edge_dq_blocks, dquery_h).astype(jnp.bfloat16)
    attended_all = jnp.where(is_edge, edge_out_blocks, attended_h)
    key_eff_grad = accum[:, 0]
    gain_heads = key_gain.reshape(HEADS, HD)
    key_grad_h = (key_eff_grad * gain_heads[:, None, None, :]).astype(jnp.bfloat16)
    value_grad_h = accum[:, 1].astype(jnp.bfloat16)
    gain_term = jnp.sum(key_eff_grad * to_heads(keys[0]).astype(jnp.float32), axis=(1, 2)).reshape(
        HEADS * HD
    )
    gain_grad = lax.psum(gain_term, ("dp", "seq"))
    return (
        from_heads(attended_all),
        from_heads(dquery_all),
        from_heads(key_grad_h),
        from_heads(value_grad_h),
        gain_grad,
    )


def solution(mesh):
    placed = (
        P("dp", "seq", None),
        P("dp", "seq", None),
        P("dp", "seq", None),
        P(),
        P(None, "seq", None),
        P("dp", "seq", None),
    )
    return jax.shard_map(
        shards,
        mesh=mesh,
        in_specs=placed,
        out_specs=(
            P("dp", "seq", None),
            P("dp", "seq", None),
            P("dp", "seq", None),
            P("dp", "seq", None),
            P(),
        ),
        check_vma=False,
    )
```

profile of v0, /device:TPU:0, one launch (start us, length us, event | category | flops | bytes accessed | tf_op | source)
XLA Modules:
  0.0 1162.1 jit_solution(12394933204315450777)
XLA Ops:
  11.2 7.3 all-to-all-start
  18.5 2.8 convert_bitcast_fusion
  27.5 10.2 gather_fusion
  37.7 5.5 all-to-all-start.1
  49.8 2.9 collective-permute-start
  63.5 214.5 %all-reduce.15.cloned.1.call-done = bf16[4,128,2048]{2,1,0:T(8,128)(2,1)} async-done(((bf16[4,128,2048]{2,1,0:T(8,128)(2,1)}), bf16[4,128,2048]{2,1,0:T(8,128)(2,1)}) %all-reduce.15.cloned.1.call-update) | async-done | bytes 2097168 | tf_op jit(solution)/shard_map/psum | solution.py:21
  281.9 11.7 %gather_fusion.1 = bf16[192,64,256]{2,1,0:T(8,128)(2,1)} fusion(bf16[288,64,256]{2,1,0:T(8,128)(2,1)} %bitcast.23, s32[1024]{0:T(1024)S(1)} %pad_clamp_fusion), kind=kCustom, calls=%fused_computation.1 | custom fusion | bytes 12583680 | tf_op jit(solution)/shard_map/gather | solution.py:192
  293.7 8.1 fusion.134
  301.7 287.5 %while.24 = (s32[]{:T(128)}, bf16[4,4,4,64,128]{4,3,2,1,0:T(8,128)(2,1)}, bf16[4,4,4,64,128]{4,3,2,1,0:T(8,128)(2,1)}, f32[4,4,2,2,64,128]{5,1,0,2,4,3:T(4,128)}...) while((s32[]{:T(128)}, ...), condition=%wide.region_14.15_spmd.clone, body=%wide.region_10.14_spmd.clone.sunk | while | flops 952370176 | bytes 142396560 | solution.py:230
  309.2 3.5 fusion.232
  318.7 3.1 fusion.233
  321.8 5.1 bitcast_dynamic-update-slice_fusion.6
  328.1 3.2 multiply_convert_fusion.4
  338.5 2.8 fusion.240
  352.4 2.8 fusion.236
  380.9 3.5 fusion.232
  390.4 3.1 fusion.233
  393.5 5.1 bitcast_dynamic-update-slice_fusion.6
  399.8 3.2 multiply_convert_fusion.4
  410.2 2.8 fusion.240
  424.1 2.8 fusion.236
  452.6 3.5 fusion.232
  462.0 3.1 fusion.233
  465.1 5.1 bitcast_dynamic-update-slice_fusion.6
  471.4 3.2 multiply_convert_fusion.4
  481.9 2.8 fusion.240
  495.8 2.8 fusion.236
  524.3 3.5 fusion.232
  533.8 3.1 fusion.233
  536.9 5.1 bitcast_dynamic-update-slice_fusion.6
  543.2 3.2 multiply_convert_fusion.4
  553.5 2.8 fusion.240
  567.5 2.8 fusion.236
  589.3 12.7 %copy.168 = bf16[16,4,3,64,2,128]{5,4,3,2,1,0:T(2,128)(2,1)} copy(bf16[16,4,3,64,2,128]{5,3,2,1,4,0:T(8,128)(2,1)} %bitcast.479) | data formatting | bytes 12582912 | tf_op jit(solution)/shard_map/convert_element_type | solution.py:292
  602.0 10.8 reshape.529
  612.9 4.8 broadcast_in_dim.167
  617.7 29.1 %scatter_fusion = bf16[288,64,256]{2,1,0:T(8,128)(2,1)} fusion(bf16[288,64,256]{2,1,0:T(8,128)(2,1)} %broadcast_in_dim.167, s32[192]{0:T(256)S(1)} %bitcast.510, bf16[192,64,256]{2,1,0:T(8,128)(2,1)} %reshape.529), kind=kCustom, calls=%fused_computation.3 | custom fusion | bytes 18875136 | tf_op jit(solution)/shard_map/scatter | solution.py:297
  646.8 12.8 %all-to-all-start.2 = ((bf16[32,9,64,256]{3,2,1,0:T(8,128)(2,1)}), bf16[32,9,64,256]{3,2,1,0:T(8,128)(2,1)}, u32[]{:S(2)}, u32[]{:S(2)}) async-start(bf16[32,9,64,256]{3,2,1,0:T(8,128)(2,1)} %bitcast.456), calls=%async_computation.2 | async-start | bytes 18874368 | tf_op jit(solution)/shard_map/all_to_all | solution.py:300
  663.6 224.5 %pmax.7 = f32[16,128]{1,0:T(8,128)S(1)} all-reduce(f32[16,128]{1,0:T(8,128)S(1)} %get-tuple-element.354), channel_id=1, replica_groups=mesh['dp'=1,'seq'=32] {'seq'}, use_global_device_ids=true, to_apply=%region_2.3 | all-reduce | flops 2048 | bytes 16384 | tf_op jit(solution)/shard_map/pmax | solution.py:254
  888.1 3.5 fusion.97
  895.4 38.4 %psum.44 = f32[16,128]{1,0:T(8,128)S(1)} all-reduce(f32[16,128]{1,0:T(8,128)S(1)} %fusion.95), channel_id=1, replica_groups=mesh['dp'=1,'seq'=32] {'seq'}, use_global_device_ids=true, to_apply=%region_5.6 | all-reduce | flops 2048 | bytes 16384 | tf_op jit(solution)/shard_map/psum | solution.py:256
  933.8 3.0 fusion.104
  942.5 4.0 collective-permute-start.3
  946.5 86.3 %all-reduce.17.cloned.1.call-done = (f32[16,128,128]{2,1,0:T(8,128)}, f32[16,2,2,64,128]{4,0,1,3,2:T(8,128)}) async-done(((f32[16,128,128]{2,1,0:T(8,128)}, f32[16,2,2,64,128]{4,0,1,3,2:T(8,128)}), (f32[16,128,128]{2,1,0:T(8,128)}, f32[16,2,2,64,128]{4,0,1,3,2:T(8,128)})) %all-reduce.17.cloned.1.call-update) | async-done | bytes 3145744 | tf_op jit(solution)/shard_map/psum | solution.py:256
  1042.5 18.9 %copy.212 = bf16[36,8,64,256]{3,1,2,0:T(8,128)(2,1)} copy(bf16[36,8,64,256]{3,2,1,0:T(8,128)(2,1)} %bitcast.182) | data formatting | bytes 18874368
  1061.4 15.9 %dot_general.116 = bf16[64,2,128,288]{2,1,0,3:T(2,128)(2,1)} reshape(bf16[16384,288]{0,1:T(8,128)(2,1)} %bitcast.459) | data formatting | bytes 18874368 | tf_op jit(solution)/shard_map/dot_general | solution.py:305
  1077.3 12.3 %fusion.85 = f32[16,2,4,64,128]{4,0,1,3,2:T(8,128)S(1)} fusion(f32[16,2,6,64,128]{4,0,1,3,2:T(8,128)} %bitcast.464, f32[16,1,4,64,128]{4,0,1,3,2:T(8,128)} %copy.166, f32[16,1,4,64,128]{4,0,1,3,2:T(8,128)} %copy.165, bf16[64,2,128,288]{2,1,0,3:T(2,128)(2,1)} %dot_general.116, s32[16,4]{0,1:T(4,128)S(1)} %multiply_add_fusion, s32[288]{0:T(512)S(1)} %eq.59), kind=kOutput, calls=%fused_computation.118 | convolution fusion | flops 607143936 | bytes 22021504 | tf_op jit(solution)/shard_map/dot_general | solution.py:305
  1095.8 50.9 %all-reduce.18 = (bf16[16,2,64,128]{3,2,1,0:T(8,128)(2,1)S(1)}, f32[2048]{0:T(1024)}) all-reduce(f32[16,2,64,128]{3,2,1,0:T(8,128)S(1)} %bitcast.484, f32[2048]{0:T(1024)S(1)} %bitcast.507), channel_id=1, replica_groups=mesh['dp'=1,'seq'=32] {'seq'}, use_global_device_ids=true, to_apply=%region_16.17 | all-reduce | flops 264192 | bytes 1589248 | tf_op jit(solution)/shard_map/psum | solution.py:315
  (456 shorter events, 271.8 us)
Async XLA Ops:
  9.3 49.5 %copy-start.33 = (s32[192,1]{0,1:T(1,128)}, s32[192,1]{0,1:T(1,128)S(1)}, u32[]{:S(2)}) copy-start(s32[192,1]{0,1:T(1,128)S(1)} %compare_select_fusion.1) | copy-start | bytes 2308
  11.2 14.4 %all-to-all-start = ((s32[32,1,9]{2,1,0:T(1,128)}), s32[32,1,9]{2,1,0:T(1,128)S(1)}, u32[]{:S(2)}, u32[]{:S(2)}) async-start(s32[32,1,9]{2,1,0:T(1,128)} %bitcast.20), calls=%async_computation | async-start | bytes 32768 | tf_op jit(solution)/shard_map/all_to_all | solution.py:185
  37.7 244.2 %all-to-all-start.1 = ((bf16[32,9,64,256]{3,2,1,0:T(8,128)(2,1)}), bf16[32,9,64,256]{3,2,1,0:T(8,128)(2,1)}, u32[]{:S(2)}, u32[]{:S(2)}) async-start(bf16[32,9,64,256]{3,2,1,0:T(8,128)(2,1)} %bitcast.458), calls=%async_computation.1 | async-start | bytes 18874368 | tf_op jit(solution)/shard_map/all_to_all | solution.py:188
  43.3 234.7 %all-reduce.15.cloned.1.call-start = ((), (), s32[]{:S(2)}) async-start(), calls=%async_computation.3 | async-start | bytes 4194304 | tf_op jit(solution)/shard_map/psum | solution.py:21
  49.8 9.1 collective-permute-start
  52.7 6.2 collective-permute-start.1
  54.4 2.8 copy-start.24
  309.1 3.7 copy-start.1
  315.8 2.9 copy-start.2
  333.3 3.8 copy-start.5
  335.6 2.9 copy-start
  363.0 2.6 copy-start.4
  369.6 2.7 copy-start.3
  369.7 2.7 copy-start.28
  380.8 3.7 copy-start.1
  387.5 2.9 copy-start.2
  405.0 3.8 copy-start.5
  407.3 2.9 copy-start
  434.6 2.6 copy-start.4
  441.3 2.6 copy-start.3
  441.4 2.6 copy-start.28
  452.4 3.7 copy-start.1
  459.1 2.9 copy-start.2
  476.6 3.8 copy-start.5
  478.9 3.0 copy-start
  506.4 2.6 copy-start.4
  513.1 2.7 copy-start.3
  513.1 2.7 copy-start.28
  524.2 3.7 copy-start.1
  530.9 2.9 copy-start.2
  548.4 3.8 copy-start.5
  550.7 2.9 copy-start
  578.0 2.6 copy-start.4
  584.8 2.7 copy-start.3
  584.8 2.7 copy-start.28
  612.9 4.8 copy-start.34
  646.8 12.9 %copy-start.7 = (f32[32,8,16,128]{3,2,1,0:T(8,128)S(1)}, f32[32,8,16,128]{3,2,1,0:T(8,128)}, u32[]{:S(2)}) copy-start(f32[32,8,16,128]{3,2,1,0:T(8,128)} %copy-done.6) | copy-start | bytes 6291460
  646.8 12.9 %copy-start.31 = (f32[2048]{0:T(1024)S(1)}, f32[2048]{0:T(1024)}, u32[]{:S(2)}) copy-start(f32[2048]{0:T(1024)} %param.17) | copy-start | bytes 24580
  646.8 395.7 %all-to-all-start.2 = ((bf16[32,9,64,256]{3,2,1,0:T(8,128)(2,1)}), bf16[32,9,64,256]{3,2,1,0:T(8,128)(2,1)}, u32[]{:S(2)}, u32[]{:S(2)}) async-start(bf16[32,9,64,256]{3,2,1,0:T(8,128)(2,1)} %bitcast.456), calls=%async_computation.2 | async-start | bytes 18874368 | tf_op jit(solution)/shard_map/all_to_all | solution.py:300
  659.6 373.3 %all-reduce.17.cloned.1.call-start = ((), (), s32[]{:S(2)}) async-start(), calls=%async_computation.4 | async-start | bytes 6291456 | tf_op jit(solution)/shard_map/psum | solution.py:256
  933.8 5.5 slice-start.1
  933.8 5.5 slice-start.2
  941.2 148.4 %collective-permute-start.2 = (bf16[16,2,64,128]{3,0,1,2:T(8,128)(2,1)}, bf16[16,2,64,128]{3,0,1,2:T(8,128)(2,1)}, u32[]{:S(2)}, u32[]{:S(2)}) collective-permute-start(bf16[16,2,64,128]{3,0,1,2:T(8,128)(2,1)} %get-tuple-element.337), channel_id=1, source_target_pairs={{1,0},{2,1},{3,2},{4,3},{5,4},{6,5},{7,6},{8,7},{9,8},{10,9},{11,1... | collective-permute-start | bytes 1572872 | tf_op jit(solution)/shard_map/ppermute | solution.py:44
  942.5 148.6 %collective-permute-start.3 = (bf16[16,2,64,128]{3,0,1,2:T(8,128)(2,1)}, bf16[16,2,64,128]{3,0,1,2:T(8,128)(2,1)}, u32[]{:S(2)}, u32[]{:S(2)}) collective-permute-start(bf16[16,2,64,128]{3,0,1,2:T(8,128)(2,1)} %get-tuple-element.336), channel_id=1, source_target_pairs={{0,1},{1,2},{2,3},{3,4},{4,5},{5,6},{6,7},{7,8},{8,9},{9,10},{10,1... | collective-permute-start | bytes 1572872 | tf_op jit(solution)/shard_map/ppermute | solution.py:44
  1032.9 2.7 copy-start.9
  1035.5 2.5 copy-start.15
  1089.6 2.8 copy-start.25
  1151.3 2.5 copy-start.20
  (43 other events, 60.4 us)
Sparse Core Ops, SparseCore 0:
  49.5 228.4 all-reduce.14
  891.7 141.1 all-reduce.16
where the time goes:
time: 1170 us; the launch traced here: 1160 us
  blocking collectives  314 us (27%)
  waiting for transfers between devices  301 us (26%)
  local copies, waits for them, and re-layouts  288 us (25%)
  matrix products  154 us (13%)
  other arithmetic  53.4 us (5%)
  starting transfers between devices  35.5 us (3%)
  between operations  14.8 us (1%)
    pmax x1, blocking collectives, shards(): edge_top = lax.pmax(jnp.max(edge_scores, axis=2), 'seq')  224 us
    psum x1, waiting for transfers between devices, broadcast(): return lax.psum(block, axis)  214 us
    psum x1, waiting for transfers between devices, shards(): lax.psum((jnp.sum(edge_expo, axis=2), jnp.einsum('hqt,htd->hqd', edge_exp...  86.3 us
    psum x1, blocking collectives, shards(): edge_dquery_sum, global_sum = lax.psum((edge_dquery, global_part), 'seq')  50.9 us
    while x160, local copies, waits for them, and re-layouts  46.7 us
    dot_general x24, matrix products, spread_terms(): jnp.einsum('hpbc,hpbd->hpcd', coef_blocks[:, :, :, NG + offset], rows_in,...  41.2 us
    psum x1, blocking collectives, shards(): lax.psum((jnp.sum(edge_expo, axis=2), jnp.einsum('hqt,htd->hqd', edge_exp...  38.4 us
    unnamed x62, local copies, waits for them, and re-layouts  34 us
  transfers between devices with their start and end apart: 9, of which 3 were waited for; matrix products, arithmetic and copies ran while one was open for 8% of the time, Pallas kernels for 0%

commit v1 on v0

v1 whole, which is shorter than its diff:
```python
import functools

import jax
import jax.numpy as jnp
from jax import lax
from jax.experimental import pallas as pl
from jax.experimental.pallas import tpu as pltpu
from jax.sharding import PartitionSpec as P

HEADS = 16
HD = 128
BLOCK = 64
NG = 2
NR = 3
NK = 8
EDGE = NG * BLOCK
SCALE = HD ** (-0.5)
NEGATIVE = -1e30
VMEM = pltpu.CompilerParams(vmem_limit_bytes=56 * 1024 * 1024)
WHOLE = pl.BlockSpec(memory_space=pltpu.VMEM)


def dot_nt(a, b):
    return lax.dot_general(a, b, (((1,), (1,)), ((), ())), preferred_element_type=jnp.float32)


def dot_nn(a, b):
    return lax.dot_general(a, b, (((1,), (0,)), ((), ())), preferred_element_type=jnp.float32)


def dot_tn(a, b):
    return lax.dot_general(a, b, (((0,), (0,)), ((), ())), preferred_element_type=jnp.float32)


def passed_along(array, axis, by):
    length = lax.axis_size(axis)
    pairs = [(i, i + by) for i in range(length) if 0 <= i + by < length]
    return lax.ppermute(array, axis, pairs)


def pick_kernel(per_dev, slots, index_ref, key_ref, value_ref, out_ref):
    def step(s, carry):
        table = jnp.maximum(index_ref[s], 0)
        rows = pl.ds(pl.multiple_of(lax.rem(table, per_dev) * BLOCK, BLOCK), BLOCK)
        cols = pl.ds(pl.multiple_of(lax.div(table, per_dev) * HD, HD), HD)
        out_ref[s, :, :HD] = key_ref[rows, cols]
        out_ref[s, :, HD:] = value_ref[rows, cols]
        return carry

    lax.fori_loop(0, slots, step, 0)


def pick(index, key_eff, values, per_dev):
    slots = index.shape[0]
    return pl.pallas_call(
        functools.partial(pick_kernel, per_dev, slots),
        grid_spec=pltpu.PrefetchScalarGridSpec(
            num_scalar_prefetch=1, grid=(), in_specs=[WHOLE, WHOLE], out_specs=WHOLE
        ),
        out_shape=jax.ShapeDtypeStruct((slots, BLOCK, 2 * HD), jnp.bfloat16),
        compiler_params=VMEM,
        name="pick",
    )(index, key_eff, values)


def sparse_kernel(
    per_dev, place_ref, pos_ref, q_ref, k_ref, v_ref, g_ref, left_ref, right_ref, edge_ref,
    arrived_ref, att_ref, dq_ref, global_ref, padded_ref, send_ref,
):
    head = pl.program_id(0)
    first_block = place_ref[0]
    total_blocks = place_ref[1]

    @pl.when(head == 0)
    def _():
        send_ref[...] = jnp.zeros_like(send_ref)

    k_window = jnp.concatenate([left_ref[0], k_ref[...], right_ref[0]], axis=0)
    v_window = jnp.concatenate([left_ref[1], v_ref[...], right_ref[1]], axis=0)
    global_ref[...] = jnp.zeros_like(global_ref)
    padded_ref[...] = jnp.zeros_like(padded_ref)
    column = lax.broadcasted_iota(jnp.int32, (1, NK * BLOCK), 1)
    for p in range(per_dev):
        rows = slice(p * BLOCK, (p + 1) * BLOCK)
        block = first_block + p
        slots = [pos_ref[(head * per_dev + p) * NR + r] for r in range(NR)]
        picked = [arrived_ref[s] for s in slots]
        window = slice(p * BLOCK, (p + 3) * BLOCK)
        keys = jnp.concatenate(
            [edge_ref[1], k_window[window]] + [x[:, :HD] for x in picked], axis=0
        )
        values = jnp.concatenate(
            [edge_ref[2], v_window[window]] + [x[:, HD:] for x in picked], axis=0
        )
        listed = block - 1 - NG + column // BLOCK
        mask = (column < EDGE) | (column >= EDGE + 3 * BLOCK)
        mask = mask | ((listed >= NG) & (listed < total_blocks))
        q = q_ref[rows, :]
        g = g_ref[rows, :]
        scores = jnp.where(mask, dot_nt(q, keys) * SCALE, NEGATIVE)
        top = jnp.max(scores, axis=1, keepdims=True)
        expo = jnp.where(mask, jnp.exp(scores - top), 0.0)
        total = jnp.sum(expo, axis=1, keepdims=True)
        attended = (dot_nn(expo.astype(jnp.bfloat16), values) / total).astype(jnp.bfloat16)
        delta = jnp.sum(
            g.astype(jnp.float32) * attended.astype(jnp.float32), axis=1, keepdims=True
        )
        keep = jnp.where(block >= NG, 1.0, 0.0).astype(jnp.float32)
        weights = expo * (keep / total)
        dprobs = dot_nt(g, values)
        dscores = (weights * (dprobs - delta) * SCALE).astype(jnp.bfloat16)
        weights_b = weights.astype(jnp.bfloat16)
        att_ref[rows, :] = attended
        dq_ref[rows, :] = dot_nn(dscores, keys).astype(jnp.bfloat16)
        for part, terms in ((0, dot_tn(dscores, q)), (1, dot_tn(weights_b, g))):
            global_ref[part] += terms[:EDGE]
            padded_ref[part, window, :] += terms[EDGE : EDGE + 3 * BLOCK]
            for r in range(NR):
                start = EDGE + (3 + r) * BLOCK
                send_ref[slots[r], :, part * HD : (part + 1) * HD] = terms[
                    start : start + BLOCK
                ].astype(jnp.bfloat16)


def head_spec(rows):
    return pl.BlockSpec((rows, HD), lambda h, *_: (0, h))


def head_spec_3(parts, rows):
    return pl.BlockSpec((parts, rows, HD), lambda h, *_: (0, 0, h))


def row_spec():
    return pl.BlockSpec((1, 1, EDGE), lambda h, *_: (h, 0, 0))


def sparse(place, position, q, k, v, g, left, right, edge, arrived, per_dev):
    tok = q.shape[0]
    width = q.shape[1]
    wide = tok + 2 * BLOCK
    return pl.pallas_call(
        functools.partial(sparse_kernel, per_dev),
        grid_spec=pltpu.PrefetchScalarGridSpec(
            num_scalar_prefetch=2,
            grid=(HEADS,),
            in_specs=[head_spec(tok)] * 4
            + [head_spec_3(2, BLOCK)] * 2
            + [head_spec_3(4, EDGE), WHOLE],
            out_specs=[
                head_spec(tok),
                head_spec(tok),
                head_spec_3(2, EDGE),
                head_spec_3(2, wide),
                WHOLE,
            ],
        ),
        out_shape=[
            jax.ShapeDtypeStruct((tok, width), jnp.bfloat16),
            jax.ShapeDtypeStruct((tok, width), jnp.bfloat16),
            jax.ShapeDtypeStruct((2, EDGE, width), jnp.float32),
            jax.ShapeDtypeStruct((2, wide, width), jnp.float32),
            jax.ShapeDtypeStruct(arrived.shape, jnp.bfloat16),
        ],
        compiler_params=VMEM,
        name="sparse",
    )(place, position, q, k, v, g, left, right, edge, arrived)


def edge_top_kernel(edge_ref, k_ref, top_ref):
    scores = dot_nt(k_ref[...], edge_ref[0]) * SCALE
    top_ref[0] = jnp.max(scores, axis=0, keepdims=True)


def edge_sum_kernel(edge_ref, k_ref, v_ref, top_ref, total_ref, numer_ref):
    scores = dot_nt(k_ref[...], edge_ref[0]) * SCALE
    expo = jnp.exp(scores - top_ref[0])
    total_ref[0] = jnp.sum(expo, axis=0, keepdims=True)
    numer_ref[...] = dot_tn(expo.astype(jnp.bfloat16), v_ref[...])


def edge_grad_kernel(edge_ref, k_ref, v_ref, top_ref, total_ref, delta_ref, dq_ref, dkv_ref):
    q = edge_ref[0]
    g = edge_ref[3]
    scores = dot_nt(k_ref[...], q) * SCALE
    weights = jnp.exp(scores - top_ref[0]) / total_ref[0]
    dprobs = dot_nt(v_ref[...], g)
    dscores = (weights * (dprobs - delta_ref[0]) * SCALE).astype(jnp.bfloat16)
    dq_ref[...] = dot_tn(dscores, k_ref[...])
    dkv_ref[0] = dot_nn(dscores, q)
    dkv_ref[1] = dot_nn(weights.astype(jnp.bfloat16), g)


def edge_call(kernel, inputs, specs, outs, out_specs, name):
    return pl.pallas_call(
        kernel,
        grid=(HEADS,),
        in_specs=specs,
        out_specs=out_specs,
        out_shape=[jax.ShapeDtypeStruct(s, jnp.float32) for s in outs],
        compiler_params=VMEM,
        name=name,
    )(*inputs)


def final_kernel(
    per_dev, slots, place_ref, served_ref, returned_ref, padded_ref, local_ref, next_ref,
    prev_ref, global_ref, keys_ref, gain_ref, edq_ref, eout_ref, att_ref, dq_ref,
    att_out, dq_out, dk_out, dv_out, gain_out, acc_ref,
):
    head = pl.program_id(0)
    first_block = place_ref[0]

    @pl.when(head == 0)
    def _():
        acc_ref[...] = jnp.zeros_like(acc_ref)

        def step(s, carry):
            table = served_ref[s]

            @pl.when(table >= 0)
            def _():
                acc_ref[table] += returned_ref[s].astype(jnp.float32)

            return carry

        lax.fori_loop(0, slots, step, 0)

    gain_sum = jnp.zeros((1, HD), jnp.float32)
    for p in range(per_dev):
        rows = slice(p * BLOCK, (p + 1) * BLOCK)
        shifted = slice((p + 1) * BLOCK, (p + 2) * BLOCK)
        summed = acc_ref[head * per_dev + p]
        sums = []
        for part in range(2):
            term = padded_ref[part, shifted, :] + local_ref[part, rows, :]
            term = term + summed[:, part * HD : (part + 1) * HD]
            if p == per_dev - 1:
                term = term + next_ref[part].astype(jnp.float32)
            if p == 0:
                term = term + prev_ref[part].astype(jnp.float32)
            if p < NG:
                term = term + jnp.where(
                    first_block == 0, global_ref[part, rows, :].astype(jnp.float32), 0.0
                )
            sums.append(term)
        dk_out[rows, :] = (sums[0] * gain_ref[...]).astype(jnp.bfloat16)
        dv_out[rows, :] = sums[1].astype(jnp.bfloat16)
        gain_sum = gain_sum + jnp.sum(
            sums[0] * keys_ref[rows, :].astype(jnp.float32), axis=0, keepdims=True
        )
        if p < NG:
            is_edge = first_block == 0
            att_out[rows, :] = jnp.where(is_edge, eout_ref[rows, :], att_ref[rows, :])
            dq_out[rows, :] = jnp.where(
                is_edge, edq_ref[rows, :].astype(jnp.bfloat16), dq_ref[rows, :]
            )
        else:
            att_out[rows, :] = att_ref[rows, :]
            dq_out[rows, :] = dq_ref[rows, :]
    gain_out[...] = gain_sum


def final(place, served, returned, padded, local, nxt, prev, glob, keys, gain, edq, eout, att, dq,
          per_dev):
    tok = keys.shape[0]
    width = keys.shape[1]
    slots = served.shape[0]
    return pl.pallas_call(
        functools.partial(final_kernel, per_dev, slots),
        grid_spec=pltpu.PrefetchScalarGridSpec(
            num_scalar_prefetch=2,
            grid=(HEADS,),
            in_specs=[
                WHOLE,
                head_spec_3(2, tok + 2 * BLOCK),
                head_spec_3(2, tok),
                head_spec_3(2, BLOCK),
                head_spec_3(2, BLOCK),
                head_spec_3(2, EDGE),
                head_spec(tok),
                head_spec(1),
                head_spec(EDGE),
                head_spec(EDGE),
                head_spec(tok),
                head_spec(tok),
            ],
            out_specs=[head_spec(tok)] * 4 + [head_spec(1)],
            scratch_shapes=[pltpu.VMEM((HEADS * per_dev, BLOCK, 2 * HD), jnp.float32)],
        ),
        out_shape=[jax.ShapeDtypeStruct((tok, width), jnp.bfloat16)] * 4
        + [jax.ShapeDtypeStruct((1, width), jnp.float32)],
        compiler_params=VMEM,
        name="final",
    )(place, served, returned, padded, local, nxt, prev, glob, keys, gain, edq, eout, att, dq)


def shards(queries, keys, values, key_gain, random_blocks, out_grad):
    tok = queries.shape[1]
    width = queries.shape[2]
    per_dev = tok // BLOCK
    owners = lax.axis_size("seq")
    seq_place = lax.axis_index("seq")
    first_block = seq_place * per_dev
    place = jnp.stack([first_block, jnp.int32(owners * per_dev)]).astype(jnp.int32)
    q, v, g = queries[0], values[0], out_grad[0]
    key_eff = (keys[0].astype(jnp.float32) * key_gain).astype(jnp.bfloat16)

    request_count = HEADS * per_dev * NR
    capacity = (request_count + owners - 1) // owners + 3
    target = random_blocks.reshape(request_count)
    owner_dev = target // per_dev
    table_index = (
        jnp.arange(request_count, dtype=jnp.int32) // (per_dev * NR) * per_dev + target % per_dev
    )
    onehot = (owner_dev[:, None] == jnp.arange(owners, dtype=jnp.int32)[None, :]).astype(jnp.int32)
    before = jnp.cumsum(onehot, axis=0) - onehot
    slot_rank = jnp.sum(before * onehot, axis=1)
    position = (owner_dev * capacity + slot_rank).astype(jnp.int32)
    hit = position[:, None] == jnp.arange(owners * capacity, dtype=jnp.int32)[None, :]
    outgoing = (
        jnp.sum(jnp.where(hit, table_index[:, None] + 1, 0), axis=0).astype(jnp.int32) - 1
    ).reshape(owners, capacity)
    served = lax.all_to_all(outgoing, "seq", split_axis=0, concat_axis=0, tiled=True)
    served = served.reshape(owners * capacity)
    picked = pick(served, key_eff, v, per_dev)

    def exchange(slots):
        shaped = slots.reshape(owners, capacity, BLOCK, 2 * HD)
        moved = lax.all_to_all(shaped, "seq", split_axis=0, concat_axis=0, tiled=True)
        return moved.reshape(owners * capacity, BLOCK, 2 * HD)

    edge = jnp.stack([q[:EDGE], key_eff[:EDGE], v[:EDGE], g[:EDGE]])
    edge = lax.psum(jnp.where(seq_place == 0, edge, jnp.zeros_like(edge)), "seq")
    tails = jnp.stack([key_eff[tok - BLOCK :], v[tok - BLOCK :]])
    heads = jnp.stack([key_eff[:BLOCK], v[:BLOCK]])
    left = passed_along(tails, "seq", 1)
    right = passed_along(heads, "seq", -1)
    arrived = exchange(picked)

    rows = (HEADS, 1, EDGE)
    edge_in = head_spec_3(4, EDGE)
    (local_top,) = edge_call(
        edge_top_kernel, (edge, key_eff), [edge_in, head_spec(tok)], [rows], [row_spec()], "top"
    )
    top = lax.pmax(local_top, "seq")
    total, numer = lax.psum(
        tuple(
            edge_call(
                edge_sum_kernel,
                (edge, key_eff, v, top),
                [edge_in, head_spec(tok), head_spec(tok), row_spec()],
                [rows, (EDGE, width)],
                [row_spec(), head_spec(EDGE)],
                "sums",
            )
        ),
        "seq",
    )
    numer = numer.reshape(EDGE, HEADS, HD)
    edge_out = (numer / total[:, 0].T[:, :, None]).astype(jnp.bfloat16)
    edge_delta = jnp.sum(
        edge[3].reshape(EDGE, HEADS, HD).astype(jnp.float32) * edge_out.astype(jnp.float32), axis=2
    ).T[:, None]
    edge_out = edge_out.reshape(EDGE, width)
    edge_dq, local = edge_call(
        edge_grad_kernel,
        (edge, key_eff, v, top, total, edge_delta),
        [edge_in, head_spec(tok), head_spec(tok), row_spec(), row_spec(), row_spec()],
        [(EDGE, width), (2, tok, width)],
        [head_spec(EDGE), head_spec_3(2, tok)],
        "grads",
    )
    arrived, edge_dq, local = lax.optimization_barrier((arrived, edge_dq, local))

    att, dq, global_part, padded, send = sparse(
        place, position, q, key_eff, v, g, left, right, edge, arrived, per_dev
    )
    returned = exchange(send)
    nxt = passed_along(padded[:, :BLOCK].astype(jnp.bfloat16), "seq", -1)
    prev = passed_along(padded[:, tok + BLOCK :].astype(jnp.bfloat16), "seq", 1)
    edge_dq, global_sum = lax.psum((edge_dq, global_part), "seq")
    att, dq, dk, dv, gain_term = final(
        place, served, returned, padded, local, nxt, prev, global_sum, keys[0],
        key_gain[None], edge_dq, edge_out, att, dq, per_dev,
    )
    gain_grad = lax.psum(gain_term[0], ("dp", "seq"))
    return att[None], dq[None], dk[None], dv[None], gain_grad


def solution(mesh):
    placed = (
        P("dp", "seq", None),
        P("dp", "seq", None),
        P("dp", "seq", None),
        P(),
        P(None, "seq", None),
        P("dp", "seq", None),
    )
    return jax.shard_map(
        shards,
        mesh=mesh,
        in_specs=placed,
        out_specs=(
            P("dp", "seq", None),
            P("dp", "seq", None),
            P("dp", "seq", None),
            P("dp", "seq", None),
            P(),
        ),
        check_vma=False,
    )
```

time: 1170 us -> 860 us (0.74)
  local copies, waits for them, and re-layouts: 288 us -> 8.84 us
  waiting for transfers between devices: 301 us -> 555 us
  blocking collectives: 314 us -> 128 us
  matrix products: 154 us -> 0 us
  Pallas kernels: 0 us -> 118 us
  other arithmetic: 53.4 us -> 12.6 us
  starting transfers between devices: 35.5 us -> 21.8 us
    psum x2 -> x3, waiting for transfers between devices: 301 us -> 547 us  [the longest x1 235 us: shards(): edge_dq, global_sum = lax.psum((edge_dq, global_part), 'seq')]
    pmax x1, blocking collectives: 224 us -> 39.2 us  [shards(): top = lax.pmax(local_top, 'seq')]
    dot_general x63 -> x0, matrix products: 140 us -> none  [the longest x24 41.2 us: spread_terms(): jnp.einsum('hpbc,hpbd->hpcd', coef_blocks[:, :, :, NG + offset], rows_in,...]
    pallas_call x0 -> x6, Pallas kernels: none -> 118 us  [the longest x1 49.4 us: sparse(): pl.pallas_call(functools.partial(sparse_kernel, per_dev), grid_spec=pltpu...]
    while x160 -> x0, local copies, waits for them, and re-layouts: 46.7 us -> none
    slice x34 -> x8, local copies, waits for them, and re-layouts: 45.4 us -> 1.4 us  [the longest x5 1.11 us: shards(): edge = jnp.stack([q[:EDGE], key_eff[:EDGE], v[:EDGE], g[:EDGE]])]
    scatter x2 -> x0, local copies, waits for them, and re-layouts: 30.3 us -> none  [the longest x1 29.1 us: shards(): sendback = jnp.zeros((owners * capacity, BLOCK, 2 * HD), jnp.bfloat16).at...]
    unnamed x62 -> x25, local copies, waits for them, and re-layouts: 34 us -> 4.26 us
  transfers between devices with their start and end apart: 9 -> 10, of which waited for: 3 -> 5; matrix products, arithmetic and copies ran while one was open for 8% -> 2% of each run, Pallas kernels for 0% -> 4%
where the time goes in v1:
time: 860 us; the launch traced here: 858 us
  waiting for transfers between devices  555 us (65%)
  blocking collectives  128 us (15%)
  Pallas kernels  118 us (14%)
  starting transfers between devices  21.8 us (3%)
  between operations  14.1 us (2%)
  other arithmetic  12.6 us (1%)
  local copies, waits for them, and re-layouts  8.84 us (1%)
    psum x1, waiting for transfers between devices, shards(): edge_dq, global_sum = lax.psum((edge_dq, global_part), 'seq')  235 us
    psum x1, waiting for transfers between devices, shards(): lax.psum(jnp.where(seq_place == 0, edge, jnp.zeros_like(edge)), 'seq')  226 us
    psum x1, waiting for transfers between devices, shards(): lax.psum(tuple(edge_call(edge_sum_kernel, (edge, key_eff, v, top), [edge_...  86.5 us
    pallas_call x1, Pallas kernels, sparse(): pl.pallas_call(functools.partial(sparse_kernel, per_dev), grid_spec=pltpu...  49.4 us
    psum x1, blocking collectives, shards(): gain_grad = lax.psum(gain_term[0], ('dp', 'seq'))  45 us
    psum x1, blocking collectives, shards(): lax.psum(tuple(edge_call(edge_sum_kernel, (edge, key_eff, v, top), [edge_...  43.3 us
    pmax x1, blocking collectives, shards(): top = lax.pmax(local_top, 'seq')  39.2 us
    pallas_call x3, Pallas kernels, edge_call(): pl.pallas_call(kernel, grid=(HEADS,), in_specs=specs, out_specs=out_specs...  36.2 us
  transfers between devices with their start and end apart: 10, of which 5 were waited for; matrix products, arithmetic and copies ran while one was open for 2% of the time, Pallas kernels for 4%

profile of v1, /device:TPU:0, one launch (start us, length us, event | category | flops | bytes accessed | tf_op | source)
XLA Modules:
  0.0 857.9 jit_solution(5562942633640766044)
XLA Ops:
  7.2 0.8 copy.22
  8.0 0.1 reshape.162
  8.2 0.6 reduce-window.6
  8.8 0.2 slice_reduce_fusion
  9.3 0.7 sub.23
  10.0 7.3 all-to-all-start
  17.3 2.4 multiply_convert_fusion.key_ref.k_ref
  19.7 4.6 all-to-all-done
  24.4 0.5 broadcast.180
  24.9 0.7 reduce.5
  25.6 0.6 reshape.165.index_ref.served_ref
  26.2 10.9 %pick.1 = bf16[288,64,256]{2,1,0:T(8,128)(2,1)} custom-call(s32[288]{0:T(512)} %reshape.165.index_ref.served_ref, bf16[256,2048]{1,0:T(8,128)(2,1)} %multiply_convert_fusion.key_ref.k_ref, bf16[256,2048]{1,0:T(8,128)(2,1)} %bitcast.56), custom_call_target="tpu_custom_call" | custom-call | tf_op jit(solution)/shard_map/pick/pallas_call | solution.py:55
  37.1 3.8 all-to-all-start.1
  41.0 0.8 slice.58
  41.8 0.5 copy-done
  42.4 0.2 slice-done.1
  42.6 0.4 copy-done.3
  43.0 1.6 maximum_select_fusion
  44.8 2.0 collective-permute-start
  46.8 225.8 %all-reduce.6.cloned.1.call-done.edge_ref = bf16[4,128,2048]{2,1,0:T(8,128)(2,1)} async-done(((bf16[4,128,2048]{2,1,0:T(8,128)(2,1)}), bf16[4,128,2048]{2,1,0:T(8,128)(2,1)}) %all-reduce.6.cloned.1.call-update) | async-done | bytes 2097168 | tf_op jit(solution)/shard_map/psum | solution.py:333
  272.6 9.9 %top.1 = f32[16,1,128]{2,1,0:T(1,128)} custom-call(bf16[4,128,2048]{2,1,0:T(8,128)(2,1)} %all-reduce.6.cloned.1.call-done.edge_ref, bf16[256,2048]{1,0:T(8,128)(2,1)} %multiply_convert_fusion.key_ref.k_ref), custom_call_target="tpu_custom_call" | custom-call | tf_op jit(solution)/shard_map/top/pallas_call | solution.py:194
  282.5 39.2 %pmax.7.top_ref = f32[16,1,128]{2,1,0:T(1,128)} all-reduce(f32[16,1,128]{2,1,0:T(1,128)} %top.1), channel_id=1, replica_groups=mesh['dp'=1,'seq'=32] {'seq'}, use_global_device_ids=true, to_apply=%region_5.6 | all-reduce | flops 2048 | bytes 16384 | tf_op jit(solution)/shard_map/pmax | solution.py:345
  321.7 12.5 %sums.1 = (f32[16,1,128]{2,1,0:T(1,128)}, f32[128,2048]{1,0:T(8,128)}) custom-call(bf16[4,128,2048]{2,1,0:T(8,128)(2,1)} %all-reduce.6.cloned.1.call-done.edge_ref, bf16[256,2048]{1,0:T(8,128)(2,1)} %multiply_convert_fusion.key_ref.k_ref, bf16[256,2048]{1,0:T(8,128)(2,1)} %bitcast.57, f32[16,1,128]{2,1,0:T(1,128)} %pmax.7.top_ref), custom_call_target="tpu_custom_call" | custom-call | tf_op jit(solution)/shard_map/sums/pallas_call | solution.py:194
  334.4 1.3 collective-permute-start.1
  335.7 0.6 pad_add_fusion.place_ref
  336.3 1.1 convert_bitcast_fusion
  337.4 0.2 copy.30
  337.6 43.3 %psum.43.total_ref = f32[16,1,128]{2,1,0:T(1,128)S(1)} all-reduce(f32[16,1,128]{2,1,0:T(1,128)S(1)} %copy-done.10), channel_id=1, replica_groups=mesh['dp'=1,'seq'=32] {'seq'}, use_global_device_ids=true, to_apply=%region_6.7 | all-reduce | flops 2048 | bytes 16384 | tf_op jit(solution)/shard_map/psum | solution.py:346
  381.0 86.5 %all-reduce.8.cloned.1.call-done = f32[128,2048]{1,0:T(8,128)} async-done(((f32[128,2048]{1,0:T(8,128)}), f32[128,2048]{1,0:T(8,128)}) %all-reduce.8.cloned.1.call-update) | async-done | bytes 1048592 | tf_op jit(solution)/shard_map/psum | solution.py:346
  467.5 1.4 copy.31
  468.9 0.3 fusion.1
  469.3 0.3 multiply_reduce_fusion
  469.6 0.7 copy.27
  470.3 13.7 %grads.1 = (f32[128,2048]{1,0:T(8,128)}, f32[2,256,2048]{2,1,0:T(8,128)}) custom-call(bf16[4,128,2048]{2,1,0:T(8,128)(2,1)} %all-reduce.6.cloned.1.call-done.edge_ref, bf16[256,2048]{1,0:T(8,128)(2,1)} %multiply_convert_fusion.key_ref.k_ref, bf16[256,2048]{1,0:T(8,128)(2,1)} %bitcast.58, f32[16,1,128]{2,1,0:T(1,128)} %pmax.7.top_ref, ...), custom_call_target="tpu_custom_call" | custom-call | tf_op jit(solution)/shard_map/grads/pallas_call | solution.py:194
  484.1 0.8 copy-done.4
  484.9 0.2 copy-done.5
  485.0 49.4 %sparse.1 = (bf16[256,2048]{1,0:T(8,128)(2,1)}, bf16[256,2048]{1,0:T(8,128)(2,1)}, f32[2,128,2048]{2,1,0:T(8,128)}, f32[2,384,2048]{2,1,0:T(8,128)}, bf16[288,64,256]{2,1,0:T(8,128)(2,1)}) custom-call(s32[2]{0:T(128)} %pad_add_fusion.place_ref, s32[192]{0:T(256)} %copy-done.9, bf16[256,2048]{1,0:T(8,128)(2,1)} %bitcast.65, ...), custom_call_target="tpu_custom_call" | custom-call | tf_op jit(solution)/shard_map/sparse/pallas_call | solution.py:141
  534.4 3.7 all-to-all-start.2
  538.2 0.7 all-reduce.10.cloned.1.call-update
  538.9 3.3 convert.11
  542.2 2.2 collective-permute-start.3
  544.5 1.3 collective-permute-start.2
  545.8 0.3 div.42
  546.1 1.2 fusion.eout_ref
  547.3 2.1 collective-permute-done.2.next_ref
  549.4 235.2 %all-reduce.10.cloned.1.call-done = (f32[2,128,2048]{2,1,0:T(8,128)}, f32[128,2048]{1,0:T(8,128)}) async-done(((f32[2,128,2048]{2,1,0:T(8,128)}, f32[128,2048]{1,0:T(8,128)}), (f32[2,128,2048]{2,1,0:T(8,128)}, f32[128,2048]{1,0:T(8,128)})) %all-reduce.10.cloned.1.call-update) | async-done | bytes 3145744 | tf_op jit(solution)/shard_map/psum | solution.py:381
  784.5 21.8 %final.1 = (bf16[256,2048]{1,0:T(8,128)(2,1)}, bf16[256,2048]{1,0:T(8,128)(2,1)}, bf16[256,2048]{1,0:T(8,128)(2,1)}, bf16[256,2048]{1,0:T(8,128)(2,1)}, f32[1,2048]{1,0:T(1,128)}) custom-call(s32[2]{0:T(128)} %pad_add_fusion.place_ref, s32[288]{0:T(512)} %reshape.165.index_ref.served_ref, bf16[288,64,256]{2,1,0:T(8,128)(2,1)} %bitcast.17.returned_ref, ...), custom_call_target="tpu_custom_call" | custom-call | tf_op jit(solution)/shard_map/final/pallas_call | solution.py:268
  806.3 45.0 %psum.47 = f32[2048]{0:T(1024)} all-reduce(f32[2048]{0:T(1024)} %bitcast.70), channel_id=1, replica_groups=mesh['dp'=1,'seq'=32] {'dp','seq'}, use_global_device_ids=true, to_apply=%region_11.12 | all-reduce | flops 2048 | bytes 16384 | tf_op jit(solution)/shard_map/psum | solution.py:386
  (48 shorter events, 1.0 us)
Async XLA Ops:
  9.1 27.9 %copy-start.9 = (s32[192]{0:T(256)}, s32[192]{0:T(256)S(1)}, u32[]{:S(2)}) copy-start(s32[192]{0:T(256)S(1)} %multiply_add_fusion.pos_ref) | copy-start | bytes 2308
  10.0 14.4 %all-to-all-start = ((s32[32,1,9]{2,1,0:T(1,128)}), s32[32,1,9]{2,1,0:T(1,128)S(1)}, u32[]{:S(2)}, u32[]{:S(2)}) async-start(s32[32,1,9]{2,1,0:T(1,128)} %bitcast.2), calls=%async_computation | async-start | bytes 32768 | tf_op jit(solution)/shard_map/all_to_all | solution.py:323
  37.1 3.9 copy-start.1
  37.1 447.0 %all-to-all-start.1 = ((bf16[32,9,64,256]{3,2,1,0:T(8,128)(2,1)}), bf16[32,9,64,256]{3,2,1,0:T(8,128)(2,1)}, u32[]{:S(2)}, u32[]{:S(2)}) async-start(bf16[32,9,64,256]{3,2,1,0:T(8,128)(2,1)} %bitcast.55), calls=%async_computation.1 | async-start | bytes 18874368 | tf_op jit(solution)/shard_map/all_to_all | solution.py:329
  40.9 1.4 copy-start
  40.9 231.7 %all-reduce.6.cloned.1.call-start = ((), (), s32[]{:S(2)}) async-start(), calls=%async_computation.3 | async-start | bytes 4194304 | tf_op jit(solution)/shard_map/psum | solution.py:333
  41.0 1.5 slice-start
  41.0 1.6 slice-start.1
  41.8 1.2 copy-start.3
  44.6 422.9 %all-reduce.8.cloned.1.call-start = ((), (), s32[]{:S(2)}) async-start(), calls=%async_computation.4 | async-start | bytes 2097152 | tf_op jit(solution)/shard_map/psum | solution.py:346
  44.8 439.2 %collective-permute-start = (bf16[2,64,2048]{2,1,0:T(8,128)(2,1)S(1)}, bf16[2,64,2048]{2,1,0:T(8,128)(2,1)S(1)}, u32[]{:S(2)}, u32[]{:S(2)}) collective-permute-start(bf16[2,64,2048]{2,1,0:T(8,128)(2,1)S(1)} %pad_maximum_fusion), channel_id=1, source_target_pairs={{0,1},{1,2},{2,3},{3,4},{4,5},{5,6},{6,7},{7,8},{8,9},{9,10},{10,1... | collective-permute-start | bytes 1572872 | tf_op jit(solution)/shard_map/ppermute | solution.py:38
  334.4 3.2 copy-start.10
  334.4 149.7 %collective-permute-start.1 = (bf16[2,64,2048]{2,1,0:T(8,128)(2,1)S(1)}, bf16[2,64,2048]{2,1,0:T(8,128)(2,1)S(1)}, u32[]{:S(2)}, u32[]{:S(2)}) collective-permute-start(bf16[2,64,2048]{2,1,0:T(8,128)(2,1)S(1)} %pad_maximum_fusion.1), channel_id=1, source_target_pairs={{1,0},{2,1},{3,2},{4,3},{5,4},{6,5},{7,6},{8,7},{9,8},{10,9},{11,1... | collective-permute-start | bytes 1572872 | tf_op jit(solution)/shard_map/ppermute | solution.py:38
  380.9 88.7 %copy-start.8 = (f32[16,1,128]{2,1,0:T(1,128)}, f32[16,1,128]{2,1,0:T(1,128)S(1)}, u32[]{:S(2)}) copy-start(f32[16,1,128]{2,1,0:T(1,128)S(1)} %psum.43.total_ref) | copy-start | bytes 24580
  484.1 0.8 copy-start.4
  484.1 0.9 copy-start.5
  534.4 250.1 %all-to-all-start.2 = ((bf16[32,9,64,256]{3,2,1,0:T(8,128)(2,1)}), bf16[32,9,64,256]{3,2,1,0:T(8,128)(2,1)}, u32[]{:S(2)}, u32[]{:S(2)}) async-start(bf16[32,9,64,256]{3,2,1,0:T(8,128)(2,1)} %bitcast.60), calls=%async_computation.2 | async-start | bytes 18874368 | tf_op jit(solution)/shard_map/all_to_all | solution.py:329
  538.1 246.4 %all-reduce.10.cloned.1.call-start = ((), (), s32[]{:S(2)}) async-start(), calls=%async_computation.5 | async-start | bytes 6291456 | tf_op jit(solution)/shard_map/psum | solution.py:381
  542.1 4.0 copy-start.2
  542.2 5.1 collective-permute-start.3
  544.5 4.9 collective-permute-start.2
  547.3 237.2 %copy-start.6 = (bf16[2,64,2048]{2,1,0:T(8,128)(2,1)}, bf16[2,64,2048]{2,1,0:T(8,128)(2,1)S(1)}, u32[]{:S(2)}) copy-start(bf16[2,64,2048]{2,1,0:T(8,128)(2,1)S(1)} %collective-permute-done.3.prev_ref) | copy-start | bytes 1572868
  549.4 235.2 %copy-start.7 = (bf16[2,64,2048]{2,1,0:T(8,128)(2,1)}, bf16[2,64,2048]{2,1,0:T(8,128)(2,1)S(1)}, u32[]{:S(2)}) copy-start(bf16[2,64,2048]{2,1,0:T(8,128)(2,1)S(1)} %collective-permute-done.2.next_ref) | copy-start | bytes 1572868
Sparse Core Ops, SparseCore 0:
  47.1 225.4 all-reduce.5
  334.4 133.0 all-reduce.7
  545.1 239.3 all-reduce.9

commit v2 on v1

v2 whole, which is shorter than its diff:
```python
import functools

import jax
import jax.numpy as jnp
from jax import lax
from jax.experimental import pallas as pl
from jax.experimental.pallas import tpu as pltpu
from jax.sharding import PartitionSpec as P

HEADS = 16
HD = 128
BLOCK = 64
NG = 2
NR = 3
NK = 8
EDGE = NG * BLOCK
SCALE = HD ** (-0.5)
NEGATIVE = -1e30
VMEM = pltpu.CompilerParams(vmem_limit_bytes=56 * 1024 * 1024)
WHOLE = pl.BlockSpec(memory_space=pltpu.VMEM)


def dot_nt(a, b):
    return lax.dot_general(a, b, (((1,), (1,)), ((), ())), preferred_element_type=jnp.float32)


def dot_nn(a, b):
    return lax.dot_general(a, b, (((1,), (0,)), ((), ())), preferred_element_type=jnp.float32)


def dot_tn(a, b):
    return lax.dot_general(a, b, (((0,), (0,)), ((), ())), preferred_element_type=jnp.float32)


def passed_along(array, axis, by):
    length = lax.axis_size(axis)
    pairs = [(i, i + by) for i in range(length) if 0 <= i + by < length]
    return lax.ppermute(array, axis, pairs)


def pick_kernel(per_dev, slots, index_ref, key_ref, value_ref, key_out, value_out):
    def step(s, carry):
        table = jnp.maximum(index_ref[s], 0)
        rows = pl.ds(pl.multiple_of(lax.rem(table, per_dev) * BLOCK, BLOCK), BLOCK)
        cols = pl.ds(pl.multiple_of(lax.div(table, per_dev) * HD, HD), HD)
        key_out[s] = key_ref[rows, cols]
        value_out[s] = value_ref[rows, cols]
        return carry

    lax.fori_loop(0, slots, step, 0)


def pick(index, key_eff, values, per_dev):
    slots = index.shape[0]
    return pl.pallas_call(
        functools.partial(pick_kernel, per_dev, slots),
        grid_spec=pltpu.PrefetchScalarGridSpec(
            num_scalar_prefetch=1, grid=(), in_specs=[WHOLE, WHOLE], out_specs=[WHOLE, WHOLE]
        ),
        out_shape=[jax.ShapeDtypeStruct((slots, BLOCK, HD), jnp.bfloat16)] * 2,
        compiler_params=VMEM,
        name="pick",
    )(index, key_eff, values)


def listed_rows(edge_rows, window_rows, p, arrived_ref, slots):
    window = window_rows[p * BLOCK : (p + 3) * BLOCK]
    return jnp.concatenate([edge_rows, window] + [arrived_ref[s] for s in slots], axis=0)


def softmax_parts(q, keys, block, total_blocks):
    column = lax.broadcasted_iota(jnp.int32, (1, NK * BLOCK), 1)
    listed = block - 1 - NG + column // BLOCK
    mask = (column < EDGE) | (column >= EDGE + 3 * BLOCK)
    mask = mask | ((listed >= NG) & (listed < total_blocks))
    scores = jnp.where(mask, dot_nt(q, keys) * SCALE, NEGATIVE)
    top = jnp.max(scores, axis=1, keepdims=True)
    expo = jnp.where(mask, jnp.exp(scores - top), 0.0)
    total = jnp.sum(expo, axis=1, keepdims=True)
    keep = jnp.where(block >= NG, 1.0, 0.0).astype(jnp.float32)
    return expo, total, expo * (keep / total)


def scatter_terms(terms, p, slots, global_ref, padded_ref, send_ref):
    global_ref[...] += terms[:EDGE]
    padded_ref[p * BLOCK : (p + 3) * BLOCK, :] += terms[EDGE : EDGE + 3 * BLOCK]
    for r in range(NR):
        start = EDGE + (3 + r) * BLOCK
        send_ref[slots[r]] = terms[start : start + BLOCK].astype(jnp.bfloat16)


def clear(head, global_ref, padded_ref, send_ref):
    @pl.when(head == 0)
    def _():
        send_ref[...] = jnp.zeros_like(send_ref)

    global_ref[...] = jnp.zeros_like(global_ref)
    padded_ref[...] = jnp.zeros_like(padded_ref)


def value_kernel(
    per_dev, place_ref, pos_ref, q_ref, g_ref, k_ref, left_ref, right_ref, edge_ref,
    arrived_ref, global_ref, padded_ref, send_ref,
):
    head = pl.program_id(0)
    clear(head, global_ref, padded_ref, send_ref)
    k_window = jnp.concatenate([left_ref[0], k_ref[...], right_ref[0]], axis=0)
    for p in range(per_dev):
        rows = slice(p * BLOCK, (p + 1) * BLOCK)
        slots = [pos_ref[(head * per_dev + p) * NR + r] for r in range(NR)]
        keys = listed_rows(edge_ref[1], k_window, p, arrived_ref, slots)
        _, _, weights = softmax_parts(q_ref[rows, :], keys, place_ref[0] + p, place_ref[1])
        terms = dot_tn(weights.astype(jnp.bfloat16), g_ref[rows, :])
        scatter_terms(terms, p, slots, global_ref, padded_ref, send_ref)


def key_kernel(
    per_dev, place_ref, pos_ref, q_ref, g_ref, k_ref, left_ref, right_ref, edge_ref,
    arrived_ref, v_ref, arrived_v_ref, global_ref, padded_ref, send_ref, att_ref, dq_ref,
):
    head = pl.program_id(0)
    clear(head, global_ref, padded_ref, send_ref)
    k_window = jnp.concatenate([left_ref[0], k_ref[...], right_ref[0]], axis=0)
    v_window = jnp.concatenate([left_ref[1], v_ref[...], right_ref[1]], axis=0)
    for p in range(per_dev):
        rows = slice(p * BLOCK, (p + 1) * BLOCK)
        slots = [pos_ref[(head * per_dev + p) * NR + r] for r in range(NR)]
        keys = listed_rows(edge_ref[1], k_window, p, arrived_ref, slots)
        values = listed_rows(edge_ref[2], v_window, p, arrived_v_ref, slots)
        q = q_ref[rows, :]
        g = g_ref[rows, :]
        expo, total, weights = softmax_parts(q, keys, place_ref[0] + p, place_ref[1])
        attended = (dot_nn(expo.astype(jnp.bfloat16), values) / total).astype(jnp.bfloat16)
        delta = jnp.sum(
            g.astype(jnp.float32) * attended.astype(jnp.float32), axis=1, keepdims=True
        )
        dscores = (weights * (dot_nt(g, values) - delta) * SCALE).astype(jnp.bfloat16)
        att_ref[rows, :] = attended
        dq_ref[rows, :] = dot_nn(dscores, keys).astype(jnp.bfloat16)
        scatter_terms(dot_tn(dscores, q), p, slots, global_ref, padded_ref, send_ref)


def head_spec(rows):
    return pl.BlockSpec((rows, HD), lambda h, *_: (0, h))


def head_spec_3(parts, rows):
    return pl.BlockSpec((parts, rows, HD), lambda h, *_: (0, 0, h))


def row_spec():
    return pl.BlockSpec((1, 1, EDGE), lambda h, *_: (h, 0, 0))


def sparse(kernel, place, position, inputs, more, per_dev, outs, name):
    q = inputs[0]
    tok = q.shape[0]
    width = q.shape[1]
    wide = tok + 2 * BLOCK
    slots = inputs[6].shape
    return pl.pallas_call(
        functools.partial(kernel, per_dev),
        grid_spec=pltpu.PrefetchScalarGridSpec(
            num_scalar_prefetch=2,
            grid=(HEADS,),
            in_specs=[head_spec(tok)] * 3
            + [head_spec_3(2, BLOCK)] * 2
            + [head_spec_3(4, EDGE), WHOLE]
            + [head_spec(tok), WHOLE][: len(more)],
            out_specs=[head_spec(EDGE), head_spec(wide), WHOLE] + [head_spec(tok)] * outs,
        ),
        out_shape=[
            jax.ShapeDtypeStruct((EDGE, width), jnp.float32),
            jax.ShapeDtypeStruct((wide, width), jnp.float32),
            jax.ShapeDtypeStruct(slots, jnp.bfloat16),
        ]
        + [jax.ShapeDtypeStruct((tok, width), jnp.bfloat16)] * outs,
        compiler_params=VMEM,
        name=name,
    )(place, position, *inputs, *more)


def edge_sum_kernel(edge_ref, k_ref, v_ref, top_ref, total_ref, numer_ref):
    scores = dot_nt(k_ref[...], edge_ref[0]) * SCALE
    top = jnp.max(scores, axis=0, keepdims=True)
    expo = jnp.exp(scores - top)
    top_ref[0] = top
    total_ref[0] = jnp.sum(expo, axis=0, keepdims=True)
    numer_ref[...] = dot_tn(expo.astype(jnp.bfloat16), v_ref[...])


def edge_grad_kernel(edge_ref, k_ref, v_ref, top_ref, total_ref, delta_ref, dq_ref, dkv_ref):
    q = edge_ref[0]
    g = edge_ref[3]
    scores = dot_nt(k_ref[...], q) * SCALE
    weights = jnp.exp(scores - top_ref[0]) / total_ref[0]
    dprobs = dot_nt(v_ref[...], g)
    dscores = (weights * (dprobs - delta_ref[0]) * SCALE).astype(jnp.bfloat16)
    dq_ref[...] = dot_tn(dscores, k_ref[...])
    dkv_ref[0] = dot_nn(dscores, q)
    dkv_ref[1] = dot_nn(weights.astype(jnp.bfloat16), g)


def edge_call(kernel, inputs, specs, outs, out_specs, name):
    return pl.pallas_call(
        kernel,
        grid=(HEADS,),
        in_specs=specs,
        out_specs=out_specs,
        out_shape=[jax.ShapeDtypeStruct(s, jnp.float32) for s in outs],
        compiler_params=VMEM,
        name=name,
    )(*inputs)


def sum_terms(
    per_dev, place_ref, served_ref, returned_ref, padded_ref, local_ref, next_ref, prev_ref,
    global_ref, acc_ref,
):
    head = pl.program_id(0)

    @pl.when(head == 0)
    def _():
        acc_ref[...] = jnp.zeros_like(acc_ref)

        def step(s, carry):
            table = served_ref[s]

            @pl.when(table >= 0)
            def _():
                acc_ref[table] += returned_ref[s].astype(jnp.float32)

            return carry

        lax.fori_loop(0, returned_ref.shape[0], step, 0)

    sums = []
    for p in range(per_dev):
        rows = slice(p * BLOCK, (p + 1) * BLOCK)
        shifted = slice((p + 1) * BLOCK, (p + 2) * BLOCK)
        term = padded_ref[shifted, :] + local_ref[0, rows, :] + acc_ref[head * per_dev + p]
        if p == per_dev - 1:
            term = term + next_ref[...].astype(jnp.float32)
        if p == 0:
            term = term + prev_ref[...].astype(jnp.float32)
        if p < NG:
            term = term + jnp.where(place_ref[0] == 0, global_ref[rows, :], 0.0)
        sums.append(term)
    return sums


def final_value_kernel(
    per_dev, place_ref, served_ref, returned_ref, padded_ref, local_ref, next_ref, prev_ref,
    global_ref, dv_out, acc_ref,
):
    sums = sum_terms(
        per_dev, place_ref, served_ref, returned_ref, padded_ref, local_ref, next_ref, prev_ref,
        global_ref, acc_ref,
    )
    for p in range(per_dev):
        dv_out[p * BLOCK : (p + 1) * BLOCK, :] = sums[p].astype(jnp.bfloat16)


def final_key_kernel(
    per_dev, place_ref, served_ref, returned_ref, padded_ref, local_ref, next_ref, prev_ref,
    global_ref, keys_ref, gain_ref, edq_ref, eout_ref, att_ref, dq_ref,
    dk_out, att_out, dq_out, gain_out, acc_ref,
):
    sums = sum_terms(
        per_dev, place_ref, served_ref, returned_ref, padded_ref, local_ref, next_ref, prev_ref,
        global_ref, acc_ref,
    )
    is_edge = place_ref[0] == 0
    gain_sum = jnp.zeros((1, HD), jnp.float32)
    for p in range(per_dev):
        rows = slice(p * BLOCK, (p + 1) * BLOCK)
        dk_out[rows, :] = (sums[p] * gain_ref[...]).astype(jnp.bfloat16)
        gain_sum = gain_sum + jnp.sum(
            sums[p] * keys_ref[rows, :].astype(jnp.float32), axis=0, keepdims=True
        )
        if p < NG:
            att_out[rows, :] = jnp.where(is_edge, eout_ref[rows, :], att_ref[rows, :])
            dq_out[rows, :] = jnp.where(
                is_edge, edq_ref[rows, :].astype(jnp.bfloat16), dq_ref[rows, :]
            )
        else:
            att_out[rows, :] = att_ref[rows, :]
            dq_out[rows, :] = dq_ref[rows, :]
    gain_out[...] = gain_sum


def final(kernel, part, place, served, inputs, more, per_dev, name):
    tok = inputs[2].shape[1]
    width = inputs[2].shape[2]
    more_specs = [
        head_spec(tok), head_spec(1), head_spec(EDGE), head_spec(EDGE), head_spec(tok),
        head_spec(tok),
    ]
    full = jax.ShapeDtypeStruct((tok, width), jnp.bfloat16)
    outs = [full] if not more else [full] * 3 + [jax.ShapeDtypeStruct((1, width), jnp.float32)]
    return pl.pallas_call(
        functools.partial(kernel, per_dev),
        grid_spec=pltpu.PrefetchScalarGridSpec(
            num_scalar_prefetch=2,
            grid=(HEADS,),
            in_specs=[
                WHOLE,
                head_spec(tok + 2 * BLOCK),
                pl.BlockSpec((1, tok, HD), lambda h, *_: (part, 0, h)),
                head_spec(BLOCK),
                head_spec(BLOCK),
                head_spec(EDGE),
            ]
            + more_specs[: len(more)],
            out_specs=[head_spec(x.shape[0]) for x in outs],
            scratch_shapes=[pltpu.VMEM((HEADS * per_dev, BLOCK, HD), jnp.float32)],
        ),
        out_shape=outs,
        compiler_params=VMEM,
        name=name,
    )(place, served, *inputs, *more)


def shards(queries, keys, values, key_gain, random_blocks, out_grad):
    tok = queries.shape[1]
    width = queries.shape[2]
    per_dev = tok // BLOCK
    owners = lax.axis_size("seq")
    seq_place = lax.axis_index("seq")
    first_block = seq_place * per_dev
    place = jnp.stack([first_block, jnp.int32(owners * per_dev)]).astype(jnp.int32)
    q, v, g = queries[0], values[0], out_grad[0]
    key_eff = (keys[0].astype(jnp.float32) * key_gain).astype(jnp.bfloat16)

    request_count = HEADS * per_dev * NR
    capacity = (request_count + owners - 1) // owners + 3
    target = random_blocks.reshape(request_count)
    owner_dev = target // per_dev
    table_index = (
        jnp.arange(request_count, dtype=jnp.int32) // (per_dev * NR) * per_dev + target % per_dev
    )
    onehot = (owner_dev[:, None] == jnp.arange(owners, dtype=jnp.int32)[None, :]).astype(jnp.int32)
    before = jnp.cumsum(onehot, axis=0) - onehot
    slot_rank = jnp.sum(before * onehot, axis=1)
    position = (owner_dev * capacity + slot_rank).astype(jnp.int32)
    hit = position[:, None] == jnp.arange(owners * capacity, dtype=jnp.int32)[None, :]
    outgoing = (
        jnp.sum(jnp.where(hit, table_index[:, None] + 1, 0), axis=0).astype(jnp.int32) - 1
    ).reshape(owners, capacity)
    served = lax.all_to_all(outgoing, "seq", split_axis=0, concat_axis=0, tiled=True)
    served = served.reshape(owners * capacity)
    picked_k, picked_v = pick(served, key_eff, v, per_dev)

    def exchange(slots):
        shaped = slots.reshape(owners, capacity, BLOCK, HD)
        moved = lax.all_to_all(shaped, "seq", split_axis=0, concat_axis=0, tiled=True)
        return moved.reshape(owners * capacity, BLOCK, HD)

    def to_all(array):
        spread = jnp.broadcast_to(array[None], (owners,) + array.shape)
        return lax.all_to_all(spread, "seq", split_axis=0, concat_axis=0, tiled=True)

    edge = jnp.stack([q[:EDGE], key_eff[:EDGE], v[:EDGE], g[:EDGE]])
    edge = lax.psum(jnp.where(seq_place == 0, edge, jnp.zeros_like(edge)), "seq")
    tails = jnp.stack([key_eff[tok - BLOCK :], v[tok - BLOCK :]])
    heads = jnp.stack([key_eff[:BLOCK], v[:BLOCK]])
    left = passed_along(tails, "seq", 1)
    right = passed_along(heads, "seq", -1)
    arrived_k = exchange(picked_k)
    picked_v, arrived_k = lax.optimization_barrier((picked_v, arrived_k))
    arrived_v = exchange(picked_v)

    stat = (HEADS, 1, EDGE)
    edge_in = head_spec_3(4, EDGE)
    top, total, numer = edge_call(
        edge_sum_kernel,
        (edge, key_eff, v),
        [edge_in, head_spec(tok), head_spec(tok)],
        [stat, stat, (EDGE, width)],
        [row_spec(), row_spec(), head_spec(EDGE)],
        "sums",
    )
    share = EDGE // owners
    stats = jnp.concatenate([top[:, 0].T, total[:, 0].T], axis=1)
    stats = jnp.pad(stats, ((0, 0), (0, HD - 2 * HEADS)))
    parts = jnp.concatenate([numer, stats], axis=1).reshape(owners, share, width + HD)

    base = [q, g, key_eff, left, right, edge, arrived_k]
    value_global, value_padded, send_v = sparse(
        value_kernel, place, position, base, [], per_dev, 0, "value_terms"
    )

    parts = lax.all_to_all(parts, "seq", split_axis=0, concat_axis=0, tiled=True)
    parts, send_v = lax.optimization_barrier((parts, send_v))
    tops = parts[:, :, width : width + HEADS]
    top_row = jnp.max(tops, axis=0)
    factor = jnp.exp(tops - top_row[None])
    total_row = jnp.sum(factor * parts[:, :, width + HEADS : width + 2 * HEADS], axis=0)
    numer_row = jnp.sum(
        parts[:, :, :width].reshape(owners, share, HEADS, HD) * factor[..., None], axis=0
    )
    out_row = (numer_row / total_row[..., None]).astype(jnp.bfloat16)
    grad_row = lax.dynamic_slice_in_dim(edge[3], seq_place * share, share, axis=0)
    grad_row = grad_row.reshape(share, HEADS, HD).astype(jnp.float32)
    delta_row = jnp.sum(grad_row * out_row.astype(jnp.float32), axis=2)
    row_stats = to_all(jnp.concatenate([top_row, total_row, delta_row], axis=1))
    row_stats = row_stats.reshape(EDGE, 3, HEADS).transpose(1, 2, 0)[:, :, None]
    edge_out = lax.all_gather(out_row.reshape(share, width), "seq", axis=0, tiled=True)

    arrived_v, send_v = lax.optimization_barrier((arrived_v, send_v))
    returned_v = exchange(send_v)
    key_global, key_padded, send_k, att, dq = sparse(
        key_kernel, place, position, base, [v, arrived_v], per_dev, 2, "key_terms"
    )
    row_stats, send_k = lax.optimization_barrier((row_stats, send_k))
    value_global = lax.psum(value_global, "seq")
    edge_dq, local = edge_call(
        edge_grad_kernel,
        (edge, key_eff, v, row_stats[0], row_stats[1], row_stats[2]),
        [edge_in, head_spec(tok), head_spec(tok), row_spec(), row_spec(), row_spec()],
        [(EDGE, width), (2, tok, width)],
        [head_spec(EDGE), head_spec_3(2, tok)],
        "grads",
    )
    send_k, returned_v, value_global = lax.optimization_barrier((send_k, returned_v, value_global))
    returned_k = exchange(send_k)

    def neighbours(padded):
        nxt = passed_along(padded[:BLOCK].astype(jnp.bfloat16), "seq", -1)
        prev = passed_along(padded[tok + BLOCK :].astype(jnp.bfloat16), "seq", 1)
        return nxt, prev

    edge_dq, key_global = lax.psum((edge_dq, key_global), "seq")
    (dv,) = final(
        final_value_kernel, 1, place, served,
        (returned_v, value_padded, local, *neighbours(value_padded), value_global), (),
        per_dev, "final_value",
    )
    returned_k, dv = lax.optimization_barrier((returned_k, dv))
    dk, att, dq, gain_term = final(
        final_key_kernel, 0, place, served,
        (returned_k, key_padded, local, *neighbours(key_padded), key_global),
        (keys[0], key_gain[None], edge_dq, edge_out, att, dq), per_dev, "final_key",
    )
    gain_grad = lax.psum(jnp.sum(to_all(gain_term), axis=(0, 1)), "dp")
    return att[None], dq[None], dk[None], dv[None], gain_grad


def solution(mesh):
    placed = (
        P("dp", "seq", None),
        P("dp", "seq", None),
        P("dp", "seq", None),
        P(),
        P(None, "seq", None),
        P("dp", "seq", None),
    )
    return jax.shard_map(
        shards,
        mesh=mesh,
        in_specs=placed,
        out_specs=(
            P("dp", "seq", None),
            P("dp", "seq", None),
            P("dp", "seq", None),
            P("dp", "seq", None),
            P(),
        ),
        check_vma=False,
    )
```

time: 860 us -> 845 us (0.983)
  waiting for transfers between devices: 555 us -> 438 us
  starting transfers between devices: 21.8 us -> 78.1 us
  Pallas kernels: 118 us -> 146 us
  blocking collectives: 128 us -> 140 us
    psum x2 -> x1, waiting for transfers between devices: 322 us -> 154 us  [shards(): value_global = lax.psum(value_global, 'seq')]
    all_gather x0 -> x1, blocking collectives: none -> 111 us  [shards(): lax.all_gather(out_row.reshape(share, width), 'seq', axis=0, tiled=True)]
    psum x2 -> x0, blocking collectives: 88.4 us -> none  [the longest x1 45 us: shards(): gain_grad = lax.psum(gain_term[0], ('dp', 'seq'))]
    all_to_all x2 -> x4, waiting for transfers between devices: 0.01 us -> 68 us  [exchange(): lax.all_to_all(shaped, 'seq', split_axis=0, concat_axis=0, tiled=True)]
    psum x1, waiting for transfers between devices: 226 us -> 174 us  [shards(): lax.psum(jnp.where(seq_place == 0, edge, jnp.zeros_like(edge)), 'seq')]
    all_to_all x0 -> x2, starting transfers between devices: none -> 42.5 us  [the longest x1 39 us: to_all(): lax.all_to_all(spread, 'seq', split_axis=0, concat_axis=0, tiled=True)]
    pmax x1 -> x0, blocking collectives: 39.2 us -> none  [shards(): top = lax.pmax(local_top, 'seq')]
    pallas_call x2 -> x4, Pallas kernels: 71.2 us -> 109 us  [the longest x2 73.7 us: sparse(): pl.pallas_call(functools.partial(kernel, per_dev), grid_spec=pltpu.Prefet...]
  transfers between devices with their start and end apart: 10 -> 15, of which waited for: 5 -> 7; matrix products, arithmetic and copies ran while one was open for 2% -> 2% of each run, Pallas kernels for 4% -> 14%
where the time goes in v2:
time: 845 us; the launch traced here: 843 us
  waiting for transfers between devices  438 us (52%)
  Pallas kernels  146 us (17%)
  blocking collectives  140 us (17%)
  starting transfers between devices  78.1 us (9%)
  local copies, waits for them, and re-layouts  14.8 us (2%)
  between operations  14.5 us (2%)
  other arithmetic  11 us (1%)
    psum x1, waiting for transfers between devices, shards(): lax.psum(jnp.where(seq_place == 0, edge, jnp.zeros_like(edge)), 'seq')  174 us
    psum x1, waiting for transfers between devices, shards(): value_global = lax.psum(value_global, 'seq')  154 us
    all_gather x1, blocking collectives, shards(): lax.all_gather(out_row.reshape(share, width), 'seq', axis=0, tiled=True)  111 us
    pallas_call x2, Pallas kernels, sparse(): pl.pallas_call(functools.partial(kernel, per_dev), grid_spec=pltpu.Prefet...  73.7 us
    all_to_all x4, waiting for transfers between devices, exchange(): lax.all_to_all(shaped, 'seq', split_axis=0, concat_axis=0, tiled=True)  68 us
    all_to_all x1, starting transfers between devices, to_all(): lax.all_to_all(spread, 'seq', split_axis=0, concat_axis=0, tiled=True)  39 us
    pallas_call x2, Pallas kernels, final(): pl.pallas_call(functools.partial(kernel, per_dev), grid_spec=pltpu.Prefet...  35.3 us
    all_to_all x1, blocking collectives, to_all(): lax.all_to_all(spread, 'seq', split_axis=0, concat_axis=0, tiled=True)  29.2 us
  transfers between devices with their start and end apart: 15, of which 7 were waited for; matrix products, arithmetic and copies ran while one was open for 2% of the time, Pallas kernels for 14%

profile of v2, /device:TPU:0, one launch (start us, length us, event | category | flops | bytes accessed | tf_op | source)
XLA Modules:
  0.0 843.4 jit_solution(2978955494166914902)
XLA Ops:
  7.2 0.8 copy.40
  9.3 0.7 sub.31
  10.0 7.3 all-to-all-start
  17.3 2.4 multiply_convert_fusion.k_ref.key_ref
  19.7 4.6 all-to-all-done
  24.9 0.7 reduce.6
  25.6 0.7 reshape.194.index_ref.served_ref
  26.3 10.9 %pick.1 = (bf16[288,64,128]{2,1,0:T(8,128)(2,1)}, bf16[288,64,128]{2,1,0:T(8,128)(2,1)}) custom-call(s32[288]{0:T(512)} %reshape.194.index_ref.served_ref, bf16[256,2048]{1,0:T(8,128)(2,1)} %multiply_convert_fusion.k_ref.key_ref, bf16[256,2048]{1,0:T(8,128)(2,1)} %bitcast.81), custom_call_target="tpu_custom_call" | custom-call | tf_op jit(solution)/shard_map/pick/pallas_call | solution.py:55
  37.2 3.7 all-to-all-start.2
  41.0 0.8 slice.80
  43.1 1.6 maximum_select_fusion
  44.7 174.2 %all-reduce.6.cloned.1.call-done.edge_ref = bf16[4,128,2048]{2,1,0:T(8,128)(2,1)} async-done(((bf16[4,128,2048]{2,1,0:T(8,128)(2,1)}), bf16[4,128,2048]{2,1,0:T(8,128)(2,1)}) %all-reduce.6.cloned.1.call-update) | async-done | bytes 2097168 | tf_op jit(solution)/shard_map/psum | solution.py:364
  218.9 12.5 %sums.1 = (f32[16,1,128]{2,1,0:T(1,128)}, f32[16,1,128]{2,1,0:T(1,128)}, f32[128,2048]{1,0:T(8,128)}) custom-call(bf16[4,128,2048]{2,1,0:T(8,128)(2,1)} %all-reduce.6.cloned.1.call-done.edge_ref, bf16[256,2048]{1,0:T(8,128)(2,1)} %multiply_convert_fusion.k_ref.key_ref, bf16[256,2048]{1,0:T(8,128)(2,1)} %bitcast.82), custom_call_target="tpu_custom_call" | custom-call | tf_op jit(solution)/shard_map/sums/pallas_call | solution.py:205
  231.4 0.7 pad_maximum_fusion.2
  232.2 1.3 select_maximum_fusion
  233.5 1.4 reshape.195
  234.9 3.5 all-to-all-start.1
  238.4 27.6 %all-to-all-done.1 = f32[32,4,2176]{2,1,0:T(4,128)S(1)} async-done(((f32[32,4,2176]{2,1,0:T(4,128)}), f32[32,4,2176]{2,1,0:T(4,128)S(1)}, u32[]{:S(2)}, u32[]{:S(2)}) %all-to-all-start.1) | async-done | bytes 1114144 | tf_op jit(solution)/shard_map/all_to_all | solution.py:393
  266.0 1.0 copy-done.6
  267.0 3.7 all-to-all-start.4
  271.0 2.3 collective-permute-start
  273.3 1.3 collective-permute-start.1
  275.3 2.9 collective-permute-done.1.right_ref
  278.2 0.8 copy-done.9
  279.0 27.5 %value_terms.1 = (f32[128,2048]{1,0:T(8,128)}, f32[384,2048]{1,0:T(8,128)}, bf16[288,64,128]{2,1,0:T(8,128)(2,1)}) custom-call(s32[2]{0:T(128)} %pad_add_fusion.place_ref, s32[192]{0:T(256)} %copy-done.15, bf16[256,2048]{1,0:T(8,128)(2,1)} %bitcast.85, bf16[256,2048]{1,0:T(8,128)(2,1)} %bitcast.87, bf16[256,2048]{1,0:T(8,128)(2,1)} %multiply_convert_fusion.k_ref.key_ref, ...), custom_call_target="tpu_custom_call" | custom-call | tf_op jit(solution)/shard_map/value_terms/pallas_call | solution.py:161
  308.0 0.7 reshape.219
  308.7 68.0 %all-to-all-done.4 = bf16[32,9,64,128]{3,2,1,0:T(8,128)(2,1)} async-done(((bf16[32,9,64,128]{3,2,1,0:T(8,128)(2,1)}), bf16[32,9,64,128]{3,2,1,0:T(8,128)(2,1)}, u32[]{:S(2)}, u32[]{:S(2)}) %all-to-all-start.4) | async-done | bytes 4718624 | tf_op jit(solution)/shard_map/all_to_all | solution.py:356
  376.7 39.0 %all-to-all-start.3 = ((f32[32,1,192]{2,1,0:T(1,128)}), f32[32,1,192]{2,1,0:T(1,128)S(1)}, u32[]{:S(2)}, u32[]{:S(2)}) async-start(f32[32,1,192]{2,1,0:T(1,128)} %reshape.219), calls=%async_computation.3 | async-start | bytes 65536 | tf_op jit(solution)/shard_map/all_to_all | solution.py:361
  415.8 7.2 all-to-all-done.3
  423.0 3.6 all-to-all-start.5
  427.2 0.7 reduce.7
  428.3 46.2 %key_terms.1 = (f32[128,2048]{1,0:T(8,128)}, f32[384,2048]{1,0:T(8,128)}, bf16[288,64,128]{2,1,0:T(8,128)(2,1)}, bf16[256,2048]{1,0:T(8,128)(2,1)}, bf16[256,2048]{1,0:T(8,128)(2,1)}) custom-call(s32[2]{0:T(128)} %pad_add_fusion.place_ref, s32[192]{0:T(256)} %copy-done.15, bf16[256,2048]{1,0:T(8,128)(2,1)} %bitcast.86, bf16[256,2048]{1,0:T(8,128)(2,1)} %bitcast.88, ...), custom_call_target="tpu_custom_call" | custom-call | tf_op jit(solution)/shard_map/key_terms/pallas_call | solution.py:161
  475.1 13.7 %grads.1 = (f32[128,2048]{1,0:T(8,128)}, f32[2,256,2048]{2,1,0:T(8,128)}) custom-call(bf16[4,128,2048]{2,1,0:T(8,128)(2,1)} %all-reduce.6.cloned.1.call-done.edge_ref, bf16[256,2048]{1,0:T(8,128)(2,1)} %multiply_convert_fusion.k_ref.key_ref, bf16[256,2048]{1,0:T(8,128)(2,1)} %bitcast.84, f32[16,1,128]{2,1,0:T(1,128)} %bitcast.100, f32[16,1,128]{2,1,0:T(1,128)} %bitcast.99, ...), custom_call_target="tpu_custom_call" | custom-call | tf_op jit(solution)/shard_map/grads/pallas_call | solution.py:205
  488.7 153.7 %all-reduce.8.cloned.1.call-done = (f32[128,2048]{1,0:T(8,128)}, f32[128,2048]{1,0:T(8,128)}, f32[128,2048]{1,0:T(8,128)}) async-done(((f32[128,2048]{1,0:T(8,128)}, f32[128,2048]{1,0:T(8,128)}, f32[128,2048]{1,0:T(8,128)}), (f32[128,2048]{1,0:T(8,128)}, f32[128,2048]{1,0:T(8,128)}, f32[128,2048]{1,0:T(8,128)})) %all-reduce.8.cloned.1.call-update) | async-done | bytes 3145744 | tf_op jit(solution)/shard_map/psum | solution.py:416
  642.4 3.9 all-to-all-start.6
  646.6 1.4 collective-permute-start.2
  648.1 3.0 collective-permute-start.3
  651.4 1.3 collective-permute-start.4
  652.7 3.9 collective-permute-start.5
  656.7 111.2 %all-gather = bf16[32,4,2048]{2,1,0:T(4,128)(2,1)S(1)} all-gather(bf16[1,4,2048]{2,1,0:T(4,128)(2,1)S(1)} %fusion.5), channel_id=1, replica_groups=mesh['dp'=1,'seq'=32] {'seq'}, dimensions={0}, use_global_device_ids=true | all-gather | bytes 540672 | tf_op jit(solution)/shard_map/all_gather | solution.py:408
  767.9 0.9 reshape.208.eout_ref
  768.9 0.7 copy-done.11
  769.6 17.0 %final_value.1 = bf16[256,2048]{1,0:T(8,128)(2,1)} custom-call(s32[2]{0:T(128)} %pad_add_fusion.place_ref, s32[288]{0:T(512)} %reshape.194.index_ref.served_ref, bf16[288,64,128]{2,1,0:T(8,128)(2,1)} %bitcast.21.returned_ref, f32[384,2048]{1,0:T(8,128)} %get-tuple-element.54.padded_ref, f32[2,256,2048]{2,1,0:T(8,128)} %get-tuple-element.56.local_ref, ...), custom_call_target="tpu_custom_call" | custom-call | tf_op jit(solution)/shard_map/final_value/pallas_call | solution.py:301
  786.7 0.7 copy-done.13
  787.5 18.3 %final_key.1 = (bf16[256,2048]{1,0:T(8,128)(2,1)}, bf16[256,2048]{1,0:T(8,128)(2,1)}, bf16[256,2048]{1,0:T(8,128)(2,1)}, f32[1,2048]{1,0:T(1,128)}) custom-call(s32[2]{0:T(128)} %pad_add_fusion.place_ref, s32[288]{0:T(512)} %reshape.194.index_ref.served_ref, bf16[288,64,128]{2,1,0:T(8,128)(2,1)} %bitcast.23.returned_ref, ...), custom_call_target="tpu_custom_call" | custom-call | tf_op jit(solution)/shard_map/final_key/pallas_call | solution.py:301
  805.8 0.8 broadcast_in_dim.67
  806.6 29.2 %all_to_all.41 = f32[32,1,2048]{2,1,0:T(1,128)S(1)} all-to-all(f32[32,1,2048]{2,1,0:T(1,128)S(1)} %broadcast_in_dim.67), channel_id=1, replica_groups=mesh['dp'=1,'seq'=32] {'seq'}, dimensions={0} | all-to-all | bytes 524288 | tf_op jit(solution)/shard_map/all_to_all | solution.py:361
  835.8 0.8 reduce_sum.62
  (86 shorter events, 7.6 us)
Async XLA Ops:
  9.1 28.1 %copy-start.15 = (s32[192]{0:T(256)}, s32[192]{0:T(256)S(1)}, u32[]{:S(2)}) copy-start(s32[192]{0:T(256)S(1)} %multiply_add_fusion.pos_ref) | copy-start | bytes 2308
  10.0 14.4 %all-to-all-start = ((s32[32,1,9]{2,1,0:T(1,128)}), s32[32,1,9]{2,1,0:T(1,128)S(1)}, u32[]{:S(2)}, u32[]{:S(2)}) async-start(s32[32,1,9]{2,1,0:T(1,128)} %bitcast.2), calls=%async_computation | async-start | bytes 32768 | tf_op jit(solution)/shard_map/all_to_all | solution.py:350
  37.2 3.8 copy-start.2
  37.2 197.7 %all-to-all-start.2 = ((bf16[32,9,64,128]{3,2,1,0:T(8,128)(2,1)}), bf16[32,9,64,128]{3,2,1,0:T(8,128)(2,1)}, u32[]{:S(2)}, u32[]{:S(2)}) async-start(bf16[32,9,64,128]{3,2,1,0:T(8,128)(2,1)} %bitcast.92), calls=%async_computation.2 | async-start | bytes 9437184 | tf_op jit(solution)/shard_map/all_to_all | solution.py:356
  40.9 1.4 copy-start
  40.9 177.9 %all-reduce.6.cloned.1.call-start = ((), (), s32[]{:S(2)}) async-start(), calls=%async_computation.8 | async-start | bytes 4194304 | tf_op jit(solution)/shard_map/psum | solution.py:364
  41.0 1.5 slice-start.1
  41.0 1.6 slice-start.2
  41.9 1.2 copy-start.10
  234.9 31.1 %all-to-all-start.1 = ((f32[32,4,2176]{2,1,0:T(4,128)}), f32[32,4,2176]{2,1,0:T(4,128)S(1)}, u32[]{:S(2)}, u32[]{:S(2)}) async-start(f32[32,4,2176]{2,1,0:T(4,128)} %reshape.195), calls=%async_computation.1 | async-start | bytes 2228224 | tf_op jit(solution)/shard_map/all_to_all | solution.py:393
  266.0 1.0 copy-start.6
  267.0 3.8 copy-start.3
  267.0 3.8 copy-start.1
  267.0 109.7 %all-to-all-start.4 = ((bf16[32,9,64,128]{3,2,1,0:T(8,128)(2,1)}), bf16[32,9,64,128]{3,2,1,0:T(8,128)(2,1)}, u32[]{:S(2)}, u32[]{:S(2)}) async-start(bf16[32,9,64,128]{3,2,1,0:T(8,128)(2,1)} %bitcast.89), calls=%async_computation.4 | async-start | bytes 9437184 | tf_op jit(solution)/shard_map/all_to_all | solution.py:356
  270.9 4.4 slice-start
  271.0 4.3 collective-permute-start
  273.3 4.9 collective-permute-start.1
  275.3 3.0 copy-start.8
  278.2 0.8 copy-start.9
  279.0 27.6 %copy-start.7 = (f32[32,4,2176]{2,1,0:T(4,128)S(1)}, f32[32,4,2176]{2,1,0:T(4,128)}, u32[]{:S(2)}) copy-start(f32[32,4,2176]{2,1,0:T(4,128)} %copy-done.6) | copy-start | bytes 3342340
  376.7 46.3 %all-to-all-start.3 = ((f32[32,1,192]{2,1,0:T(1,128)}), f32[32,1,192]{2,1,0:T(1,128)S(1)}, u32[]{:S(2)}, u32[]{:S(2)}) async-start(f32[32,1,192]{2,1,0:T(1,128)} %reshape.219), calls=%async_computation.3 | async-start | bytes 65536 | tf_op jit(solution)/shard_map/all_to_all | solution.py:361
  423.0 219.4 %all-to-all-start.5 = ((bf16[32,9,64,128]{3,2,1,0:T(8,128)(2,1)}), bf16[32,9,64,128]{3,2,1,0:T(8,128)(2,1)}, u32[]{:S(2)}, u32[]{:S(2)}) async-start(bf16[32,9,64,128]{3,2,1,0:T(8,128)(2,1)} %bitcast.91), calls=%async_computation.5 | async-start | bytes 9437184 | tf_op jit(solution)/shard_map/all_to_all | solution.py:356
  426.6 215.8 %all-reduce.8.cloned.1.call-start = ((), (), s32[]{:S(2)}) async-start(), calls=%async_computation.9 | async-start | bytes 6291456 | tf_op jit(solution)/shard_map/psum | solution.py:416
  642.4 3.9 copy-start.4
  642.4 144.2 %all-to-all-start.6 = ((bf16[32,9,64,128]{3,2,1,0:T(8,128)(2,1)}), bf16[32,9,64,128]{3,2,1,0:T(8,128)(2,1)}, u32[]{:S(2)}, u32[]{:S(2)}) async-start(bf16[32,9,64,128]{3,2,1,0:T(8,128)(2,1)} %bitcast.90), calls=%async_computation.6 | async-start | bytes 9437184 | tf_op jit(solution)/shard_map/all_to_all | solution.py:356
  646.4 4.8 copy-start.5
  646.6 122.2 %collective-permute-start.2 = (bf16[64,2048]{1,0:T(8,128)(2,1)S(1)}, bf16[64,2048]{1,0:T(8,128)(2,1)S(1)}, u32[]{:S(2)}, u32[]{:S(2)}) collective-permute-start(bf16[64,2048]{1,0:T(8,128)(2,1)S(1)} %get-tuple-element.77), channel_id=1, source_target_pairs={{1,0},{2,1},{3,2},{4,3},{5,4},{6,5},{7,6},{8,7},{9,8},{10,9},{11,1... | collective-permute-start | bytes 786440 | tf_op jit(solution)/shard_map/ppermute | solution.py:38
  648.1 120.8 %collective-permute-start.3 = (bf16[64,2048]{1,0:T(8,128)(2,1)S(1)}, bf16[64,2048]{1,0:T(8,128)(2,1)S(1)}, u32[]{:S(2)}, u32[]{:S(2)}) collective-permute-start(bf16[64,2048]{1,0:T(8,128)(2,1)S(1)} %get-tuple-element.76), channel_id=1, source_target_pairs={{0,1},{1,2},{2,3},{3,4},{4,5},{5,6},{6,7},{7,8},{8,9},{9,10},{10,1... | collective-permute-start | bytes 786440 | tf_op jit(solution)/shard_map/ppermute | solution.py:38
  651.4 135.3 %collective-permute-start.4 = (bf16[64,2048]{1,0:T(8,128)(2,1)S(1)}, bf16[64,2048]{1,0:T(8,128)(2,1)S(1)}, u32[]{:S(2)}, u32[]{:S(2)}) collective-permute-start(bf16[64,2048]{1,0:T(8,128)(2,1)S(1)} %get-tuple-element.75), channel_id=1, source_target_pairs={{1,0},{2,1},{3,2},{4,3},{5,4},{6,5},{7,6},{8,7},{9,8},{10,9},{11,1... | collective-permute-start | bytes 786440 | tf_op jit(solution)/shard_map/ppermute | solution.py:38
  652.7 134.0 %collective-permute-start.5 = (bf16[64,2048]{1,0:T(8,128)(2,1)S(1)}, bf16[64,2048]{1,0:T(8,128)(2,1)S(1)}, u32[]{:S(2)}, u32[]{:S(2)}) collective-permute-start(bf16[64,2048]{1,0:T(8,128)(2,1)S(1)} %get-tuple-element.74), channel_id=1, source_target_pairs={{0,1},{1,2},{2,3},{3,4},{4,5},{5,6},{6,7},{7,8},{8,9},{9,10},{10,1... | collective-permute-start | bytes 786440 | tf_op jit(solution)/shard_map/ppermute | solution.py:38
  768.8 0.7 copy-start.11
  768.8 0.8 copy-start.12
  786.7 0.7 copy-start.13
  786.7 0.8 copy-start.14
Sparse Core Ops, SparseCore 0:
  47.1 171.6 all-reduce.5
  488.9 153.5 all-reduce.7

commit v3 on v2

--- a/solution.py
+++ b/solution.py
@@ -36,6 +36,143 @@
     length = lax.axis_size(axis)
     pairs = [(i, i + by) for i in range(length) if 0 <= i + by < length]
     return lax.ppermute(array, axis, pairs)
+
+
+def on(device):
+    return dict(device_id={"seq": device}, device_id_type=pl.DeviceIdType.MESH)
+
+
+def spread_kernel(count, in_ref, out_ref, send_sem, recv_sem):
+    me = lax.axis_index("seq")
+    children = (
+        ((lax.rem(me, 8) == 0) & (me + 8 < count), 8),
+        (lax.rem(me, 8) == 0, 4),
+        (lax.rem(me, 4) == 0, 2),
+        (lax.rem(me, 2) == 0, 1),
+    )
+    near = jnp.where(lax.rem(me, 4) == 2, me - 2, jnp.where(lax.rem(me, 8) == 4, me - 4, me - 8))
+    parent = jnp.where(lax.rem(me, 2) == 1, me - 1, near)
+    barrier = pltpu.get_barrier_semaphore()
+    greeted = jnp.where(me > 0, 1, 0)
+    for there, step in children:
+        greeted = greeted + jnp.where(there, 1, 0)
+
+        @pl.when(there)
+        def _():
+            pl.semaphore_signal(barrier, inc=1, **on(me + step))
+
+    @pl.when(me > 0)
+    def _():
+        pl.semaphore_signal(barrier, inc=1, **on(parent))
+
+    pl.semaphore_wait(barrier, greeted)
+
+    @pl.when(me == 0)
+    def _():
+        out_ref[...] = in_ref[...]
+
+    def copy(c, i, device):
+        return pltpu.make_async_remote_copy(
+            src_ref=out_ref.at[c],
+            dst_ref=out_ref.at[c],
+            send_sem=send_sem.at[i, c],
+            recv_sem=recv_sem.at[c],
+            **on(device),
+        )
+
+    def forward(c, carry):
+        @pl.when(me > 0)
+        def _():
+            copy(c, 0, parent).wait_recv()
+
+        for i, (there, step) in enumerate(children):
+
+            @pl.when(there)
+            def _():
+                copy(c, i, me + step).start()
+
+        return carry
+
+    def finish(c, carry):
+        for i, (there, step) in enumerate(children):
+
+            @pl.when(there)
+            def _():
+                copy(c, i, me + step).wait_send()
+
+        return carry
+
+    lax.fori_loop(0, out_ref.shape[0], forward, 0)
+    lax.fori_loop(0, out_ref.shape[0], finish, 0)
+
+
+def spread(array, count):
+    chunks = array.shape[0]
+    return pl.pallas_call(
+        functools.partial(spread_kernel, count),
+        in_specs=[WHOLE],
+        out_specs=WHOLE,
+        out_shape=jax.ShapeDtypeStruct(array.shape, array.dtype),
+        scratch_shapes=[
+            pltpu.SemaphoreType.DMA((4, chunks)),
+            pltpu.SemaphoreType.DMA((chunks,)),
+        ],
+        compiler_params=pltpu.CompilerParams(
+            collective_id=0, has_side_effects=True, vmem_limit_bytes=32 * 1024 * 1024
+        ),
+        name="spread",
+    )(array)
+
+
+def collect_kernel(count, in_ref, out_ref, send_sem, recv_sem):
+    me = lax.axis_index("seq")
+    barrier = pltpu.get_barrier_semaphore()
+
+    def copy(device):
+        return pltpu.make_async_remote_copy(
+            src_ref=in_ref,
+            dst_ref=out_ref.at[device],
+            send_sem=send_sem,
+            recv_sem=recv_sem.at[device],
+            **on(0),
+        )
+
+    @pl.when(me == 0)
+    def _():
+        def greet(d, carry):
+            pl.semaphore_signal(barrier, inc=1, **on(d))
+            return carry
+
+        lax.fori_loop(1, count, greet, 0)
+        pl.semaphore_wait(barrier, count - 1)
+        out_ref[0] = in_ref[...]
+
+        def receive(d, carry):
+            copy(d).wait_recv()
+            return carry
+
+        lax.fori_loop(1, count, receive, 0)
+
+    @pl.when(me > 0)
+    def _():
+        pl.semaphore_signal(barrier, inc=1, **on(0))
+        pl.semaphore_wait(barrier, 1)
+        copy(me).start()
+        copy(me).wait_send()
+
+
+def collect(piece, count):
+    return pl.pallas_call(
+        functools.partial(collect_kernel, count),
+        in_specs=[WHOLE],
+        out_specs=WHOLE,
+        out_shape=jax.ShapeDtypeStruct((count,) + piece.shape, piece.dtype),
+        scratch_shapes=[pltpu.SemaphoreType.DMA, pltpu.SemaphoreType.DMA((count,))],
+        compiler_params=pltpu.CompilerParams(
+            collective_id=1, has_side_effects=True, vmem_limit_bytes=32 * 1024 * 1024
+        ),
+        name="collect",
+    )(piece)
 
 
 def pick_kernel(per_dev, slots, index_ref, key_ref, value_ref, key_out, value_out):
@@ -214,8 +351,8 @@
 
 
 def sum_terms(
-    per_dev, place_ref, served_ref, returned_ref, padded_ref, local_ref, next_ref, prev_ref,
-    global_ref, acc_ref,
+    per_dev, capacity, place_ref, served_ref, returned_ref, padded_ref, local_ref, next_ref,
+    prev_ref, global_ref, acc_ref,
 ):
     head = pl.program_id(0)
 
@@ -228,11 +365,12 @@
 
             @pl.when(table >= 0)
             def _():
-                acc_ref[table] += returned_ref[s].astype(jnp.float32)
+                block = returned_ref[lax.div(s, capacity), lax.rem(s, capacity)]
+                acc_ref[table] += block.astype(jnp.float32)
 
             return carry
 
-        lax.fori_loop(0, returned_ref.shape[0], step, 0)
+        lax.fori_loop(0, returned_ref.shape[0] * capacity, step, 0)
 
     sums = []
     for p in range(per_dev):
@@ -243,32 +381,33 @@
             term = term + next_ref[...].astype(jnp.float32)
         if p == 0:
             term = term + prev_ref[...].astype(jnp.float32)
-        if p < NG:
-            term = term + jnp.where(place_ref[0] == 0, global_ref[rows, :], 0.0)
+        if global_ref is not None and p < NG:
+            whole = global_ref[rows, :].astype(jnp.float32)
+            term = term + jnp.where(place_ref[0] == 0, whole, 0.0)
         sums.append(term)
     return sums
 
 
 def final_value_kernel(
-    per_dev, place_ref, served_ref, returned_ref, padded_ref, local_ref, next_ref, prev_ref,
-    global_ref, dv_out, acc_ref,
+    per_dev, capacity, place_ref, served_ref, returned_ref, padded_ref, local_ref, next_ref,
+    prev_ref, dv_out, acc_ref,
 ):
     sums = sum_terms(
-        per_dev, place_ref, served_ref, returned_ref, padded_ref, local_ref, next_ref, prev_ref,
-        global_ref, acc_ref,
+        per_dev, capacity, place_ref, served_ref, returned_ref, padded_ref, local_ref, next_ref,
+        prev_ref, None, acc_ref,
     )
     for p in range(per_dev):
-        dv_out[p * BLOCK : (p + 1) * BLOCK, :] = sums[p].astype(jnp.bfloat16)
+        dv_out[p * BLOCK : (p + 1) * BLOCK, :] = sums[p]
 
 
 def final_key_kernel(
-    per_dev, place_ref, served_ref, returned_ref, padded_ref, local_ref, next_ref, prev_ref,
-    global_ref, keys_ref, gain_ref, edq_ref, eout_ref, att_ref, dq_ref,
-    dk_out, att_out, dq_out, gain_out, acc_ref,
+    per_dev, capacity, place_ref, served_ref, returned_ref, padded_ref, local_ref, next_ref,
+    prev_ref, gk_ref, gv_ref, edq_ref, eout_ref, keys_ref, gain_ref, att_ref, dq_ref, dv_ref,
+    dk_out, att_out, dq_out, dv_out, gain_out, acc_ref,
 ):
     sums = sum_terms(
-        per_dev, place_ref, served_ref, returned_ref, padded_ref, local_ref, next_ref, prev_ref,
-        global_ref, acc_ref,
+        per_dev, capacity, place_ref, served_ref, returned_ref, padded_ref, local_ref, next_ref,
+        prev_ref, gk_ref, acc_ref,
     )
     is_edge = place_ref[0] == 0
     gain_sum = jnp.zeros((1, HD), jnp.float32)
@@ -280,26 +419,26 @@
         )
         if p < NG:
             att_out[rows, :] = jnp.where(is_edge, eout_ref[rows, :], att_ref[rows, :])
-            dq_out[rows, :] = jnp.where(
-                is_edge, edq_ref[rows, :].astype(jnp.bfloat16), dq_ref[rows, :]
-            )
+            dq_out[rows, :] = jnp.where(is_edge, edq_ref[rows, :], dq_ref[rows, :])
+            whole = jnp.where(is_edge, gv_ref[rows, :].astype(jnp.float32), 0.0)
+            dv_out[rows, :] = (dv_ref[rows, :] + whole).astype(jnp.bfloat16)
         else:
+            dv_out[rows, :] = dv_ref[rows, :].astype(jnp.bfloat16)
             att_out[rows, :] = att_ref[rows, :]
             dq_out[rows, :] = dq_ref[rows, :]
     gain_out[...] = gain_sum
 
 
-def final(kernel, part, place, served, inputs, more, per_dev, name):
+def final(kernel, part, capacity, place, served, inputs, more, per_dev, name):
     tok = inputs[2].shape[1]
     width = inputs[2].shape[2]
-    more_specs = [
-        head_spec(tok), head_spec(1), head_spec(EDGE), head_spec(EDGE), head_spec(tok),
-        head_spec(tok),
-    ]
-    full = jax.ShapeDtypeStruct((tok, width), jnp.bfloat16)
-    outs = [full] if not more else [full] * 3 + [jax.ShapeDtypeStruct((1, width), jnp.float32)]
+    more_specs = [head_spec(x.shape[0]) for x in more]
+    outs = [jax.ShapeDtypeStruct((tok, width), jnp.float32)]
+    if more:
+        outs = [jax.ShapeDtypeStruct((tok, width), jnp.bfloat16)] * 4
+        outs = outs + [jax.ShapeDtypeStruct((1, width), jnp.float32)]
     return pl.pallas_call(
-        functools.partial(kernel, per_dev),
+        functools.partial(kernel, per_dev, capacity),
         grid_spec=pltpu.PrefetchScalarGridSpec(
             num_scalar_prefetch=2,
             grid=(HEADS,),
@@ -309,9 +448,8 @@
                 pl.BlockSpec((1, tok, HD), lambda h, *_: (part, 0, h)),
                 head_spec(BLOCK),
                 head_spec(BLOCK),
-                head_spec(EDGE),
             ]
-            + more_specs[: len(more)],
+            + more_specs,
             out_specs=[head_spec(x.shape[0]) for x in outs],
             scratch_shapes=[pltpu.VMEM((HEADS * per_dev, BLOCK, HD), jnp.float32)],
         ),
@@ -351,24 +489,28 @@
     served = served.reshape(owners * capacity)
     picked_k, picked_v = pick(served, key_eff, v, per_dev)
 
-    def exchange(slots):
-        shaped = slots.reshape(owners, capacity, BLOCK, HD)
-        moved = lax.all_to_all(shaped, "seq", split_axis=0, concat_axis=0, tiled=True)
-        return moved.reshape(owners * capacity, BLOCK, HD)
+    def exchange(slots, *extra):
+        parts = [slots.reshape(owners, capacity, BLOCK, HD)]
+        for rows in extra:
+            parts.append(rows.astype(jnp.bfloat16).reshape(owners, -1, BLOCK, HD))
+        shaped = jnp.concatenate(parts, axis=1) if extra else parts[0]
+        return lax.all_to_all(shaped, "seq", split_axis=0, concat_axis=0, tiled=True)
+
+    def fetch(slots):
+        return exchange(slots).reshape(owners * capacity, BLOCK, HD)
 
     def to_all(array):
         spread = jnp.broadcast_to(array[None], (owners,) + array.shape)
         return lax.all_to_all(spread, "seq", split_axis=0, concat_axis=0, tiled=True)
 
     edge = jnp.stack([q[:EDGE], key_eff[:EDGE], v[:EDGE], g[:EDGE]])
-    edge = lax.psum(jnp.where(seq_place == 0, edge, jnp.zeros_like(edge)), "seq")
+    edge = spread(edge.reshape(16, 4 * EDGE // 16, width), owners).reshape(4, EDGE, width)
+    picked_k, edge = lax.optimization_barrier((picked_k, edge))
     tails = jnp.stack([key_eff[tok - BLOCK :], v[tok - BLOCK :]])
     heads = jnp.stack([key_eff[:BLOCK], v[:BLOCK]])
     left = passed_along(tails, "seq", 1)
     right = passed_along(heads, "seq", -1)
-    arrived_k = exchange(picked_k)
-    picked_v, arrived_k = lax.optimization_barrier((picked_v, arrived_k))
-    arrived_v = exchange(picked_v)
+    arrived_k = fetch(picked_k)
 
     stat = (HEADS, 1, EDGE)
     edge_in = head_spec_3(4, EDGE)
@@ -385,13 +527,14 @@
     stats = jnp.pad(stats, ((0, 0), (0, HD - 2 * HEADS)))
     parts = jnp.concatenate([numer, stats], axis=1).reshape(owners, share, width + HD)
 
+    picked_v, arrived_k, parts = lax.optimization_barrier((picked_v, arrived_k, parts))
+    arrived_v = fetch(picked_v)
     base = [q, g, key_eff, left, right, edge, arrived_k]
     value_global, value_padded, send_v = sparse(
         value_kernel, place, position, base, [], per_dev, 0, "value_terms"
     )
 
     parts = lax.all_to_all(parts, "seq", split_axis=0, concat_axis=0, tiled=True)
-    parts, send_v = lax.optimization_barrier((parts, send_v))
     tops = parts[:, :, width : width + HEADS]
     top_row = jnp.max(tops, axis=0)
     factor = jnp.exp(tops - top_row[None])
@@ -405,15 +548,12 @@
     delta_row = jnp.sum(grad_row * out_row.astype(jnp.float32), axis=2)
     row_stats = to_all(jnp.concatenate([top_row, total_row, delta_row], axis=1))
     row_stats = row_stats.reshape(EDGE, 3, HEADS).transpose(1, 2, 0)[:, :, None]
-    edge_out = lax.all_gather(out_row.reshape(share, width), "seq", axis=0, tiled=True)
-
-    arrived_v, send_v = lax.optimization_barrier((arrived_v, send_v))
-    returned_v = exchange(send_v)
+
+    arrived_v, send_v, row_stats = lax.optimization_barrier((arrived_v, send_v, row_stats))
+    returned_v = exchange(send_v, value_global)
     key_global, key_padded, send_k, att, dq = sparse(
         key_kernel, place, position, base, [v, arrived_v], per_dev, 2, "key_terms"
     )
-    row_stats, send_k = lax.optimization_barrier((row_stats, send_k))
-    value_global = lax.psum(value_global, "seq")
     edge_dq, local = edge_call(
         edge_grad_kernel,
         (edge, key_eff, v, row_stats[0], row_stats[1], row_stats[2]),
@@ -422,25 +562,43 @@
         [head_spec(EDGE), head_spec_3(2, tok)],
         "grads",
     )
-    send_k, returned_v, value_global = lax.optimization_barrier((send_k, returned_v, value_global))
-    returned_k = exchange(send_k)
 
     def neighbours(padded):
         nxt = passed_along(padded[:BLOCK].astype(jnp.bfloat16), "seq", -1)
         prev = passed_along(padded[tok + BLOCK :].astype(jnp.bfloat16), "seq", 1)
         return nxt, prev
 
-    edge_dq, key_global = lax.psum((edge_dq, key_global), "seq")
+    near_v = neighbours(value_padded)
+    near_k = neighbours(key_padded)
+    send_k, edge_dq, returned_v = lax.optimization_barrier((send_k, edge_dq, returned_v))
+    returned_k = exchange(send_k, key_global, edge_dq)
     (dv,) = final(
-        final_value_kernel, 1, place, served,
-        (returned_v, value_padded, local, *neighbours(value_padded), value_global), (),
-        per_dev, "final_value",
+        final_value_kernel, 1, capacity, place, served,
+        (returned_v, value_padded, local, *near_v), (), per_dev, "final_value",
     )
     returned_k, dv = lax.optimization_barrier((returned_k, dv))
-    dk, att, dq, gain_term = final(
-        final_key_kernel, 0, place, served,
-        (returned_k, key_padded, local, *neighbours(key_padded), key_global),
-        (keys[0], key_gain[None], edge_dq, edge_out, att, dq), per_dev, "final_key",
+
+    def summed(block):
+        return jnp.sum(block.astype(jnp.float32), axis=0).astype(jnp.bfloat16).reshape(share, width)
+
+    piece = jnp.concatenate(
+        [
+            summed(returned_k[:, capacity]),
+            summed(returned_v[:, capacity]),
+            summed(returned_k[:, capacity + 1]),
+            out_row.reshape(share, width),
+        ]
+    )
+    collected = collect(piece, owners).reshape(owners, 4, share, width)
+    collected = collected.transpose(1, 0, 2, 3).reshape(4, EDGE, width)
+    dk, att, dq, dv, gain_term = final(
+        final_key_kernel, 0, capacity, place, served,
+        (returned_k, key_padded, local, *near_k),
+        (
+            collected[0], collected[1], collected[2], collected[3], keys[0], key_gain[None], att,
+            dq, dv,
+        ),
+        per_dev, "final_key",
     )
     gain_grad = lax.psum(jnp.sum(to_all(gain_term), axis=(0, 1)), "dp")
     return att[None], dq[None], dk[None], dv[None], gain_grad

time: 845 us -> 713 us (0.84)
  blocking collectives: 140 us -> 23 us
  waiting for transfers between devices: 438 us -> 340 us
  Pallas kernels: 146 us -> 204 us
  starting transfers between devices: 78.1 us -> 92.4 us
  other arithmetic: 11 us -> 24.7 us
  between operations: 14.5 us -> 1.25 us
  local copies, waits for them, and re-layouts: 14.8 us -> 25.9 us
    psum x2 -> x0, waiting for transfers between devices: 328 us -> none  [the longest x1 174 us: shards(): lax.psum(jnp.where(seq_place == 0, edge, jnp.zeros_like(edge)), 'seq')]
    all_to_all x4, waiting for transfers between devices: 68 us -> 310 us  [exchange(): lax.all_to_all(shaped, 'seq', split_axis=0, concat_axis=0, tiled=True)]
    all_gather x1 -> x0, blocking collectives: 111 us -> none  [shards(): lax.all_gather(out_row.reshape(share, width), 'seq', axis=0, tiled=True)]
    pallas_call x2 -> x4, Pallas kernels: 35.3 us -> 92.6 us  [the longest x2 40 us: final(): pl.pallas_call(functools.partial(kernel, per_dev, capacity), grid_spec=pl...]
    all_to_all x4, starting transfers between devices: 14.9 us -> 69.1 us  [exchange(): lax.all_to_all(shaped, 'seq', split_axis=0, concat_axis=0, tiled=True)]
    all_to_all x1 -> x0, starting transfers between devices: 39 us -> none  [to_all(): lax.all_to_all(spread, 'seq', split_axis=0, concat_axis=0, tiled=True)]
    concatenate x0 -> x3, other arithmetic: none -> 10.9 us  [the longest x2 10.9 us: exchange(): shaped = jnp.concatenate(parts, axis=1) if extra else parts[0]]
    all_to_all x1 -> x2, blocking collectives: 29.2 us -> 23 us  [to_all(): lax.all_to_all(spread, 'seq', split_axis=0, concat_axis=0, tiled=True)]
  transfers between devices with their start and end apart: 15 -> 12, of which waited for: 7 -> 6; matrix products, arithmetic and copies ran while one was open for 2% -> 4% of each run, Pallas kernels for 14% -> 24%
where the time goes in v3:
time: 713 us; the launch traced here: 711 us
  waiting for transfers between devices  340 us (48%)
  Pallas kernels  204 us (29%)
  starting transfers between devices  92.4 us (13%)
  local copies, waits for them, and re-layouts  25.9 us (4%)
  other arithmetic  24.7 us (3%)
  blocking collectives  23 us (3%)
    all_to_all x4, waiting for transfers between devices, exchange(): lax.all_to_all(shaped, 'seq', split_axis=0, concat_axis=0, tiled=True)  310 us
    pallas_call x2, Pallas kernels, sparse(): pl.pallas_call(functools.partial(kernel, per_dev), grid_spec=pltpu.Prefet...  73.6 us
    all_to_all x4, starting transfers between devices, exchange(): lax.all_to_all(shaped, 'seq', split_axis=0, concat_axis=0, tiled=True)  69.1 us
    pallas_call x2, Pallas kernels, final(): pl.pallas_call(functools.partial(kernel, per_dev, capacity), grid_spec=pl...  40 us
    all_to_all x1, waiting for transfers between devices, shards(): lax.all_to_all(parts, 'seq', split_axis=0, concat_axis=0, tiled=True)  26.5 us
    pallas_call x1, Pallas kernels, collect(): pl.pallas_call(functools.partial(collect_kernel, count), in_specs=[WHOLE]...  26.4 us
    pallas_call x2, Pallas kernels, edge_call(): pl.pallas_call(kernel, grid=(HEADS,), in_specs=specs, out_specs=out_specs...  26.4 us
    pallas_call x1, Pallas kernels, spread(): pl.pallas_call(functools.partial(spread_kernel, count), in_specs=[WHOLE],...  26.2 us
  transfers between devices with their start and end apart: 12, of which 6 were waited for; matrix products, arithmetic and copies ran while one was open for 4% of the time, Pallas kernels for 24%

profile of v3, /device:TPU:0, one launch (start us, length us, event | category | flops | bytes accessed | tf_op | source)
XLA Modules:
  0.0 710.6 jit_solution(18005383817390691846)
XLA Ops:
  3.5 7.3 %all-to-all-start = ((s32[32,1,9]{2,1,0:T(1,128)}), s32[32,1,9]{2,1,0:T(1,128)S(1)}, u32[]{:S(2)}, u32[]{:S(2)}) async-start(s32[32,1,9]{2,1,0:T(1,128)} %bitcast.2), calls=%async_computation | async-start | bytes 32768 | tf_op jit(solution)/shard_map/all_to_all | solution.py:488
  10.8 1.2 copy-done.6
  13.2 26.2 %spread.1 = bf16[16,32,2048]{2,1,0:T(8,128)(2,1)S(1)} custom-call(bf16[16,32,2048]{2,1,0:T(8,128)(2,1)S(1)} %bitcast.85), custom_call_target="tpu_custom_call" | custom-call | tf_op jit(solution)/shard_map/spread/pallas_call | solution.py:111
  39.4 1.3 copy-done
  42.6 10.9 %pick.1 = (bf16[288,64,128]{2,1,0:T(8,128)(2,1)}, bf16[288,64,128]{2,1,0:T(8,128)(2,1)}) custom-call(s32[288]{0:T(512)} %reshape.224.index_ref.served_ref, bf16[256,2048]{1,0:T(8,128)(2,1)} %copy-done.1, bf16[256,2048]{1,0:T(8,128)(2,1)} %bitcast.86), custom_call_target="tpu_custom_call" | custom-call | tf_op jit(solution)/shard_map/pick/pallas_call | solution.py:192
  53.5 21.6 %all-to-all-start.1 = ((bf16[32,9,64,128]{3,2,1,0:T(8,128)(2,1)}), bf16[32,9,64,128]{3,2,1,0:T(8,128)(2,1)}, u32[]{:S(2)}, u32[]{:S(2)}) async-start(bf16[32,9,64,128]{3,2,1,0:T(8,128)(2,1)} %bitcast.98), calls=%async_computation.1 | async-start | bytes 9437184 | tf_op jit(solution)/shard_map/all_to_all | solution.py:497
  75.1 12.6 %sums.1 = (f32[16,1,128]{2,1,0:T(1,128)}, f32[16,1,128]{2,1,0:T(1,128)}, f32[128,2048]{1,0:T(8,128)}) custom-call(bf16[4,128,2048]{2,1,0:T(8,128)(2,1)} %bitcast.80, bf16[256,2048]{1,0:T(8,128)(2,1)} %copy-done.1, bf16[256,2048]{1,0:T(8,128)(2,1)} %bitcast.87), custom_call_target="tpu_custom_call" | custom-call | tf_op jit(solution)/shard_map/sums/pallas_call | solution.py:342
  88.5 1.3 select_maximum_fusion
  89.8 1.3 reshape.229
  91.1 89.3 %all-to-all-done.1 = bf16[32,9,64,128]{3,2,1,0:T(8,128)(2,1)} async-done(((bf16[32,9,64,128]{3,2,1,0:T(8,128)(2,1)}), bf16[32,9,64,128]{3,2,1,0:T(8,128)(2,1)}, u32[]{:S(2)}, u32[]{:S(2)}) %all-to-all-start.1) | async-done | bytes 4718624 | tf_op jit(solution)/shard_map/all_to_all | solution.py:497
  180.4 3.8 all-to-all-start.3
  184.2 1.1 slice.113
  185.3 26.5 %all-to-all-done.3 = f32[32,4,2176]{2,1,0:T(4,128)S(1)} async-done(((f32[32,4,2176]{2,1,0:T(4,128)}), f32[32,4,2176]{2,1,0:T(4,128)S(1)}, u32[]{:S(2)}, u32[]{:S(2)}) %all-to-all-start.3) | async-done | bytes 1114144 | tf_op jit(solution)/shard_map/all_to_all | solution.py:537
  213.3 10.7 %all_to_all.41 = f32[32,1,192]{2,1,0:T(1,128)S(1)} all-to-all(f32[32,1,192]{2,1,0:T(1,128)S(1)} %reshape.254), channel_id=1, replica_groups=mesh['dp'=1,'seq'=32] {'seq'}, dimensions={0} | all-to-all | bytes 49152 | tf_op jit(solution)/shard_map/all_to_all | solution.py:504
  224.0 3.7 all-to-all-start.2
  227.9 2.0 collective-permute-start
  230.0 1.3 collective-permute-start.1
  231.9 3.0 collective-permute-done.1.right_ref
  235.7 27.4 %value_terms.1 = (f32[128,2048]{1,0:T(8,128)}, f32[384,2048]{1,0:T(8,128)}, bf16[288,64,128]{2,1,0:T(8,128)(2,1)}) custom-call(s32[2]{0:T(128)} %pad_add_fusion.place_ref, s32[192]{0:T(256)} %copy-done.14, bf16[256,2048]{1,0:T(8,128)(2,1)} %bitcast.93, bf16[256,2048]{1,0:T(8,128)(2,1)} %bitcast.91, bf16[256,2048]{1,0:T(8,128)(2,1)} %copy-done.1, ...), custom_call_target="tpu_custom_call" | custom-call | tf_op jit(solution)/shard_map/value_terms/pallas_call | solution.py:298
  263.1 1.3 convert_element_type.65
  266.2 67.4 %all-to-all-done.2 = bf16[32,9,64,128]{3,2,1,0:T(8,128)(2,1)} async-done(((bf16[32,9,64,128]{3,2,1,0:T(8,128)(2,1)}), bf16[32,9,64,128]{3,2,1,0:T(8,128)(2,1)}, u32[]{:S(2)}, u32[]{:S(2)}) %all-to-all-start.2) | async-done | bytes 4718624 | tf_op jit(solution)/shard_map/all_to_all | solution.py:497
  333.7 5.1 pad_maximum_fusion.1
  338.8 39.9 %all-to-all-start.5 = ((bf16[32,10,64,128]{3,2,1,0:T(8,128)(2,1)}), bf16[32,10,64,128]{3,2,1,0:T(8,128)(2,1)}, u32[]{:S(2)}, u32[]{:S(2)}) async-start(bf16[32,10,64,128]{3,2,1,0:T(8,128)(2,1)} %pad_maximum_fusion.1), calls=%async_computation.5 | async-start | bytes 10485760 | tf_op jit(solution)/shard_map/all_to_all | solution.py:497
  378.7 46.2 %key_terms.1 = (f32[128,2048]{1,0:T(8,128)}, f32[384,2048]{1,0:T(8,128)}, bf16[288,64,128]{2,1,0:T(8,128)(2,1)}, bf16[256,2048]{1,0:T(8,128)(2,1)}, bf16[256,2048]{1,0:T(8,128)(2,1)}) custom-call(s32[2]{0:T(128)} %pad_add_fusion.place_ref, s32[192]{0:T(256)} %copy-done.14, bf16[256,2048]{1,0:T(8,128)(2,1)} %bitcast.94, bf16[256,2048]{1,0:T(8,128)(2,1)} %bitcast.92, ...), custom_call_target="tpu_custom_call" | custom-call | tf_op jit(solution)/shard_map/key_terms/pallas_call | solution.py:298
  424.9 1.3 convert_element_type.66
  427.0 13.8 %grads.1 = (f32[128,2048]{1,0:T(8,128)}, f32[2,256,2048]{2,1,0:T(8,128)}) custom-call(bf16[4,128,2048]{2,1,0:T(8,128)(2,1)} %bitcast.84, bf16[256,2048]{1,0:T(8,128)(2,1)} %copy-done.1, bf16[256,2048]{1,0:T(8,128)(2,1)} %bitcast.89, f32[16,1,128]{2,1,0:T(1,128)} %bitcast.105, f32[16,1,128]{2,1,0:T(1,128)} %bitcast.104, f32[16,1,128]{2,1,0:T(1,128)} %bitcast.103), custom_call_target="tpu_custom_call" | custom-call | tf_op jit(solution)/shard_map/grads/pallas_call | solution.py:342
  440.8 54.5 %all-to-all-done.5.returned_ref = bf16[32,10,64,128]{3,2,1,0:T(8,128)(2,1)} async-done(((bf16[32,10,64,128]{3,2,1,0:T(8,128)(2,1)}), bf16[32,10,64,128]{3,2,1,0:T(8,128)(2,1)}, u32[]{:S(2)}, u32[]{:S(2)}) %all-to-all-start.5) | async-done | bytes 5242912 | tf_op jit(solution)/shard_map/all_to_all | solution.py:497
  495.4 1.3 convert_element_type.67
  496.9 5.8 pad_maximum_fusion
  502.7 3.9 all-to-all-start.6
  506.9 2.1 collective-permute-start.3
  509.0 1.3 collective-permute-start.2
  511.4 4.2 collective-permute-start.5
  515.5 1.5 collective-permute-start.4
  517.0 1.1 slice_reduce_fusion.1
  519.0 18.9 %final_value.1.dv_ref = f32[256,2048]{1,0:T(8,128)} custom-call(s32[2]{0:T(128)} %pad_add_fusion.place_ref, s32[288]{0:T(512)} %reshape.224.index_ref.served_ref, bf16[32,10,64,128]{3,2,1,0:T(8,128)(2,1)} %all-to-all-done.5.returned_ref, f32[384,2048]{1,0:T(8,128)} %get-tuple-element.59.padded_ref, f32[2,256,2048]{2,1,0:T(8,128)} %get-tuple-element.60.local_ref, ...), custom_call_target="tpu_custom_call" | custom-call | tf_op jit(solution)/shard_map/final_value/pallas_call | solution.py:440
  537.9 98.9 %all-to-all-done.6.returned_ref = bf16[32,11,64,128]{3,2,1,0:T(8,128)(2,1)} async-done(((bf16[32,11,64,128]{3,2,1,0:T(8,128)(2,1)}), bf16[32,11,64,128]{3,2,1,0:T(8,128)(2,1)}, u32[]{:S(2)}, u32[]{:S(2)}) %all-to-all-start.6) | async-done | bytes 5767200 | tf_op jit(solution)/shard_map/all_to_all | solution.py:497
  636.8 1.4 slice_reduce_fusion.2
  638.3 26.4 %collect.1 = bf16[32,16,2048]{2,1,0:T(8,128)(2,1)S(1)} custom-call(bf16[16,2048]{1,0:T(8,128)(2,1)S(1)} %pad_maximum_fusion.5.in_ref), custom_call_target="tpu_custom_call" | custom-call | tf_op jit(solution)/shard_map/collect/pallas_call | solution.py:165
  664.7 2.3 reshape.241
  667.0 2.9 copy.70
  669.9 1.1 fusion.10
  671.0 1.0 squeeze.56.eout_ref
  672.0 0.9 squeeze.55.edq_ref
  672.9 0.9 squeeze.54.gv_ref
  673.8 0.9 squeeze.53.gk_ref
  675.6 21.1 %final_key.1 = (bf16[256,2048]{1,0:T(8,128)(2,1)}, bf16[256,2048]{1,0:T(8,128)(2,1)}, bf16[256,2048]{1,0:T(8,128)(2,1)}, bf16[256,2048]{1,0:T(8,128)(2,1)}, f32[1,2048]{1,0:T(1,128)}) custom-call(s32[2]{0:T(128)} %pad_add_fusion.place_ref, s32[288]{0:T(512)} %reshape.224.index_ref.served_ref, bf16[32,11,64,128]{3,2,1,0:T(8,128)(2,1)} %all-to-all-done.6.returned_ref, ...), custom_call_target="tpu_custom_call" | custom-call | tf_op jit(solution)/shard_map/final_key/pallas_call | solution.py:440
  697.5 12.3 %all_to_all.42 = f32[32,1,2048]{2,1,0:T(1,128)S(1)} all-to-all(f32[32,1,2048]{2,1,0:T(1,128)S(1)} %broadcast_in_dim.63), channel_id=1, replica_groups=mesh['dp'=1,'seq'=32] {'seq'}, dimensions={0} | all-to-all | bytes 524288 | tf_op jit(solution)/shard_map/all_to_all | solution.py:504
  (98 shorter events, 17.2 us)
Async XLA Ops:
  0.6 10.2 %copy-start.13 = (f32[2048]{0:T(1024)S(1)}, f32[2048]{0:T(1024)}, u32[]{:S(2)}) copy-start(f32[2048]{0:T(1024)} %param.9) | copy-start | bytes 24580
  2.6 9.6 %copy-start.14 = (s32[192]{0:T(256)}, s32[192]{0:T(256)S(1)}, u32[]{:S(2)}) copy-start(s32[192]{0:T(256)S(1)} %multiply_add_fusion.pos_ref) | copy-start | bytes 2308
  3.5 37.2 %all-to-all-start = ((s32[32,1,9]{2,1,0:T(1,128)}), s32[32,1,9]{2,1,0:T(1,128)S(1)}, u32[]{:S(2)}, u32[]{:S(2)}) async-start(s32[32,1,9]{2,1,0:T(1,128)} %bitcast.2), calls=%async_computation | async-start | bytes 32768 | tf_op jit(solution)/shard_map/all_to_all | solution.py:488
  10.8 1.2 copy-start.6
  10.8 1.5 slice-start
  10.8 1.5 slice-start.1
  10.8 1.6 slice-start.2
  12.2 1.0 copy-start.1
  39.4 1.3 copy-start
  53.5 126.9 %all-to-all-start.1 = ((bf16[32,9,64,128]{3,2,1,0:T(8,128)(2,1)}), bf16[32,9,64,128]{3,2,1,0:T(8,128)(2,1)}, u32[]{:S(2)}, u32[]{:S(2)}) async-start(bf16[32,9,64,128]{3,2,1,0:T(8,128)(2,1)} %bitcast.98), calls=%async_computation.1 | async-start | bytes 9437184 | tf_op jit(solution)/shard_map/all_to_all | solution.py:497
  180.4 31.4 %all-to-all-start.3 = ((f32[32,4,2176]{2,1,0:T(4,128)}), f32[32,4,2176]{2,1,0:T(4,128)S(1)}, u32[]{:S(2)}, u32[]{:S(2)}) async-start(f32[32,4,2176]{2,1,0:T(4,128)} %reshape.229), calls=%async_computation.3 | async-start | bytes 2228224 | tf_op jit(solution)/shard_map/all_to_all | solution.py:537
  224.0 3.7 copy-start.3
  224.0 3.8 copy-start.2
  224.0 109.6 %all-to-all-start.2 = ((bf16[32,9,64,128]{3,2,1,0:T(8,128)(2,1)}), bf16[32,9,64,128]{3,2,1,0:T(8,128)(2,1)}, u32[]{:S(2)}, u32[]{:S(2)}) async-start(bf16[32,9,64,128]{3,2,1,0:T(8,128)(2,1)} %bitcast.95), calls=%async_computation.2 | async-start | bytes 9437184 | tf_op jit(solution)/shard_map/all_to_all | solution.py:497
  227.9 3.9 collective-permute-start
  230.0 4.9 collective-permute-start.1
  231.9 3.0 copy-start.7
  234.9 0.8 copy-start.8
  338.8 156.6 %all-to-all-start.5 = ((bf16[32,10,64,128]{3,2,1,0:T(8,128)(2,1)}), bf16[32,10,64,128]{3,2,1,0:T(8,128)(2,1)}, u32[]{:S(2)}, u32[]{:S(2)}) async-start(bf16[32,10,64,128]{3,2,1,0:T(8,128)(2,1)} %pad_maximum_fusion.1), calls=%async_computation.5 | async-start | bytes 10485760 | tf_op jit(solution)/shard_map/all_to_all | solution.py:497
  502.7 3.9 copy-start.4
  502.7 134.1 %all-to-all-start.6 = ((bf16[32,11,64,128]{3,2,1,0:T(8,128)(2,1)}), bf16[32,11,64,128]{3,2,1,0:T(8,128)(2,1)}, u32[]{:S(2)}, u32[]{:S(2)}) async-start(bf16[32,11,64,128]{3,2,1,0:T(8,128)(2,1)} %pad_maximum_fusion), calls=%async_computation.6 | async-start | bytes 11534336 | tf_op jit(solution)/shard_map/all_to_all | solution.py:497
  506.6 3.7 copy-start.5
  506.9 11.2 %collective-permute-start.3 = (bf16[64,2048]{1,0:T(8,128)(2,1)S(1)}, bf16[64,2048]{1,0:T(8,128)(2,1)S(1)}, u32[]{:S(2)}, u32[]{:S(2)}) collective-permute-start(bf16[64,2048]{1,0:T(8,128)(2,1)S(1)} %get-tuple-element.81), channel_id=1, source_target_pairs={{0,1},{1,2},{2,3},{3,4},{4,5},{5,6},{6,7},{7,8},{8,9},{9,10},{10,1... | collective-permute-start | bytes 786440 | tf_op jit(solution)/shard_map/ppermute | solution.py:38
  509.0 9.1 %collective-permute-start.2 = (bf16[64,2048]{1,0:T(8,128)(2,1)S(1)}, bf16[64,2048]{1,0:T(8,128)(2,1)S(1)}, u32[]{:S(2)}, u32[]{:S(2)}) collective-permute-start(bf16[64,2048]{1,0:T(8,128)(2,1)S(1)} %get-tuple-element.82), channel_id=1, source_target_pairs={{1,0},{2,1},{3,2},{4,3},{5,4},{6,5},{7,6},{8,7},{9,8},{10,9},{11,1... | collective-permute-start | bytes 786440 | tf_op jit(solution)/shard_map/ppermute | solution.py:38
  511.4 163.4 %collective-permute-start.5 = (bf16[64,2048]{1,0:T(8,128)(2,1)}, bf16[64,2048]{1,0:T(8,128)(2,1)S(1)}, u32[]{:S(2)}, u32[]{:S(2)}) collective-permute-start(bf16[64,2048]{1,0:T(8,128)(2,1)} %get-tuple-element.79), channel_id=1, source_target_pairs={{0,1},{1,2},{2,3},{3,4},{4,5},{5,6},{6,7},{7,8},{8,9},{9,10},{10,1... | collective-permute-start | bytes 786440 | tf_op jit(solution)/shard_map/ppermute | solution.py:38
  515.5 159.3 %collective-permute-start.4 = (bf16[64,2048]{1,0:T(8,128)(2,1)S(1)}, bf16[64,2048]{1,0:T(8,128)(2,1)S(1)}, u32[]{:S(2)}, u32[]{:S(2)}) collective-permute-start(bf16[64,2048]{1,0:T(8,128)(2,1)S(1)} %get-tuple-element.80), channel_id=1, source_target_pairs={{1,0},{2,1},{3,2},{4,3},{5,4},{6,5},{7,6},{8,7},{9,8},{10,9},{11,1... | collective-permute-start | bytes 786440 | tf_op jit(solution)/shard_map/ppermute | solution.py:38
  518.2 0.7 copy-start.11
  518.2 0.8 copy-start.12
  674.8 0.7 copy-start.9
  674.8 0.8 copy-start.10

commit v4 on v3

--- a/solution.py
+++ b/solution.py
@@ -161,7 +161,7 @@
         copy(me).wait_send()
 
 
-def collect(piece, count):
+def collect(piece, count, number):
     return pl.pallas_call(
         functools.partial(collect_kernel, count),
         in_specs=[WHOLE],
@@ -169,40 +169,68 @@
         out_shape=jax.ShapeDtypeStruct((count,) + piece.shape, piece.dtype),
         scratch_shapes=[pltpu.SemaphoreType.DMA, pltpu.SemaphoreType.DMA((count,))],
         compiler_params=pltpu.CompilerParams(
-            collective_id=1, has_side_effects=True, vmem_limit_bytes=32 * 1024 * 1024
+            collective_id=number, has_side_effects=True, vmem_limit_bytes=32 * 1024 * 1024
         ),
-        name="collect",
+        name=f"collect_{number}",
     )(piece)
 
 
-def pick_kernel(per_dev, slots, index_ref, key_ref, value_ref, key_out, value_out):
+def slot_rows(slot, capacity):
+    start = pl.multiple_of(lax.rem(slot, capacity) * BLOCK, BLOCK)
+    return lax.div(slot, capacity), pl.ds(start, BLOCK)
+
+
+def pick_kernel(
+    per_dev, capacity, index_ref, key_ref, value_ref, extra_ref, key_out, value_out
+):
+    filled = capacity * BLOCK
+    key_out[:, filled:, :] = extra_ref[...]
+    value_out[:, filled:, :] = jnp.zeros_like(value_out[:, filled:, :])
+
     def step(s, carry):
         table = jnp.maximum(index_ref[s], 0)
         rows = pl.ds(pl.multiple_of(lax.rem(table, per_dev) * BLOCK, BLOCK), BLOCK)
         cols = pl.ds(pl.multiple_of(lax.div(table, per_dev) * HD, HD), HD)
-        key_out[s] = key_ref[rows, cols]
-        value_out[s] = value_ref[rows, cols]
+        owner, place = slot_rows(s, capacity)
+        key_out[owner, place, :] = key_ref[rows, cols]
+        value_out[owner, place, :] = value_ref[rows, cols]
         return carry
 
-    lax.fori_loop(0, slots, step, 0)
-
-
-def pick(index, key_eff, values, per_dev):
-    slots = index.shape[0]
+    lax.fori_loop(0, key_out.shape[0] * capacity, step, 0)
+
+
+def pick(index, key_eff, values, extra, more, per_dev, capacity):
+    owners = extra.shape[0]
+    filled = capacity * BLOCK
     return pl.pallas_call(
-        functools.partial(pick_kernel, per_dev, slots),
+        functools.partial(pick_kernel, per_dev, capacity),
         grid_spec=pltpu.PrefetchScalarGridSpec(
-            num_scalar_prefetch=1, grid=(), in_specs=[WHOLE, WHOLE], out_specs=[WHOLE, WHOLE]
+            num_scalar_prefetch=1, grid=(), in_specs=[WHOLE] * 3, out_specs=[WHOLE, WHOLE]
         ),
-        out_shape=[jax.ShapeDtypeStruct((slots, BLOCK, HD), jnp.bfloat16)] * 2,
+        out_shape=[
+            jax.ShapeDtypeStruct((owners, filled + extra.shape[1], HD), jnp.bfloat16),
+            jax.ShapeDtypeStruct((owners, filled + more, HD), jnp.bfloat16),
+        ],
         compiler_params=VMEM,
         name="pick",
-    )(index, key_eff, values)
+    )(index, key_eff, values, extra)
+
+
+def in_parts(x):
+    high = lax.reduce_precision(x, 8, 7)
+    middle = lax.reduce_precision(x - high, 8, 7)
+    return jnp.stack([high, middle, x - high - middle]).astype(jnp.bfloat16)
+
+
+def from_parts(parts, axis):
+    parts = parts.astype(jnp.float32)
+    low = [lax.index_in_dim(parts, i, axis, keepdims=False) for i in range(3)]
+    return low[0] + (low[1] + low[2])
 
 
 def listed_rows(edge_rows, window_rows, p, arrived_ref, slots):
     window = window_rows[p * BLOCK : (p + 3) * BLOCK]
-    return jnp.concatenate([edge_rows, window] + [arrived_ref[s] for s in slots], axis=0)
+    return jnp.concatenate([edge_rows, window] + [arrived_ref[s[0], s[1], :] for s in slots], axis=0)
 
 
 def softmax_parts(q, keys, block, total_blocks):
@@ -223,7 +251,7 @@
     padded_ref[p * BLOCK : (p + 3) * BLOCK, :] += terms[EDGE : EDGE + 3 * BLOCK]
     for r in range(NR):
         start = EDGE + (3 + r) * BLOCK
-        send_ref[slots[r]] = terms[start : start + BLOCK].astype(jnp.bfloat16)
+        send_ref[slots[r][0], slots[r][1], :] = terms[start : start + BLOCK].astype(jnp.bfloat16)
 
 
 def clear(head, global_ref, padded_ref, send_ref):
@@ -236,7 +264,7 @@
 
 
 def value_kernel(
-    per_dev, place_ref, pos_ref, q_ref, g_ref, k_ref, left_ref, right_ref, edge_ref,
+    per_dev, capacity, place_ref, pos_ref, q_ref, g_ref, k_ref, left_ref, right_ref, edge_ref,
     arrived_ref, global_ref, padded_ref, send_ref,
 ):
     head = pl.program_id(0)
@@ -244,7 +272,9 @@
     k_window = jnp.concatenate([left_ref[0], k_ref[...], right_ref[0]], axis=0)
     for p in range(per_dev):
         rows = slice(p * BLOCK, (p + 1) * BLOCK)
-        slots = [pos_ref[(head * per_dev + p) * NR + r] for r in range(NR)]
+        slots = [
+            slot_rows(pos_ref[(head * per_dev + p) * NR + r], capacity) for r in range(NR)
+        ]
         keys = listed_rows(edge_ref[1], k_window, p, arrived_ref, slots)
         _, _, weights = softmax_parts(q_ref[rows, :], keys, place_ref[0] + p, place_ref[1])
         terms = dot_tn(weights.astype(jnp.bfloat16), g_ref[rows, :])
@@ -252,7 +282,7 @@
 
 
 def key_kernel(
-    per_dev, place_ref, pos_ref, q_ref, g_ref, k_ref, left_ref, right_ref, edge_ref,
+    per_dev, capacity, place_ref, pos_ref, q_ref, g_ref, k_ref, left_ref, right_ref, edge_ref,
     arrived_ref, v_ref, arrived_v_ref, global_ref, padded_ref, send_ref, att_ref, dq_ref,
 ):
     head = pl.program_id(0)
@@ -261,7 +291,9 @@
     v_window = jnp.concatenate([left_ref[1], v_ref[...], right_ref[1]], axis=0)
     for p in range(per_dev):
         rows = slice(p * BLOCK, (p + 1) * BLOCK)
-        slots = [pos_ref[(head * per_dev + p) * NR + r] for r in range(NR)]
+        slots = [
+            slot_rows(pos_ref[(head * per_dev + p) * NR + r], capacity) for r in range(NR)
+        ]
         keys = listed_rows(edge_ref[1], k_window, p, arrived_ref, slots)
         values = listed_rows(edge_ref[2], v_window, p, arrived_v_ref, slots)
         q = q_ref[rows, :]
@@ -289,14 +321,14 @@
     return pl.BlockSpec((1, 1, EDGE), lambda h, *_: (h, 0, 0))
 
 
-def sparse(kernel, place, position, inputs, more, per_dev, outs, name):
+def sparse(kernel, place, position, inputs, more, per_dev, capacity, extra, outs, name):
     q = inputs[0]
     tok = q.shape[0]
     width = q.shape[1]
     wide = tok + 2 * BLOCK
-    slots = inputs[6].shape
+    slots = (inputs[6].shape[0], capacity * BLOCK + extra, HD)
     return pl.pallas_call(
-        functools.partial(kernel, per_dev),
+        functools.partial(kernel, per_dev, capacity),
         grid_spec=pltpu.PrefetchScalarGridSpec(
             num_scalar_prefetch=2,
             grid=(HEADS,),
@@ -365,8 +397,8 @@
 
             @pl.when(table >= 0)
             def _():
-                block = returned_ref[lax.div(s, capacity), lax.rem(s, capacity)]
-                acc_ref[table] += block.astype(jnp.float32)
+                owner, rows = slot_rows(s, capacity)
+                acc_ref[table] += returned_ref[owner, rows, :].astype(jnp.float32)
 
             return carry
 
@@ -487,30 +519,28 @@
     ).reshape(owners, capacity)
     served = lax.all_to_all(outgoing, "seq", split_axis=0, concat_axis=0, tiled=True)
     served = served.reshape(owners * capacity)
-    picked_k, picked_v = pick(served, key_eff, v, per_dev)
-
-    def exchange(slots, *extra):
-        parts = [slots.reshape(owners, capacity, BLOCK, HD)]
-        for rows in extra:
-            parts.append(rows.astype(jnp.bfloat16).reshape(owners, -1, BLOCK, HD))
-        shaped = jnp.concatenate(parts, axis=1) if extra else parts[0]
-        return lax.all_to_all(shaped, "seq", split_axis=0, concat_axis=0, tiled=True)
-
-    def fetch(slots):
-        return exchange(slots).reshape(owners * capacity, BLOCK, HD)
+    filled = capacity * BLOCK
+
+    def exchange(slots):
+        return lax.all_to_all(slots, "seq", split_axis=0, concat_axis=0, tiled=True)
 
     def to_all(array):
-        spread = jnp.broadcast_to(array[None], (owners,) + array.shape)
-        return lax.all_to_all(spread, "seq", split_axis=0, concat_axis=0, tiled=True)
+        spread_out = jnp.broadcast_to(array[None], (owners,) + array.shape)
+        return lax.all_to_all(spread_out, "seq", split_axis=0, concat_axis=0, tiled=True)
+
+    def pieces(rows):
+        return rows.astype(jnp.bfloat16).reshape(owners, -1, HD)
+
+    def padded_rows(flat, count):
+        flat = jnp.pad(flat, ((0, 0), (0, count * HD - flat.shape[1])))
+        return flat.reshape(flat.shape[0], count, HD)
 
     edge = jnp.stack([q[:EDGE], key_eff[:EDGE], v[:EDGE], g[:EDGE]])
     edge = spread(edge.reshape(16, 4 * EDGE // 16, width), owners).reshape(4, EDGE, width)
-    picked_k, edge = lax.optimization_barrier((picked_k, edge))
     tails = jnp.stack([key_eff[tok - BLOCK :], v[tok - BLOCK :]])
     heads = jnp.stack([key_eff[:BLOCK], v[:BLOCK]])
     left = passed_along(tails, "seq", 1)
     right = passed_along(heads, "seq", -1)
-    arrived_k = fetch(picked_k)
 
     stat = (HEADS, 1, EDGE)
     edge_in = head_spec_3(4, EDGE)
@@ -523,36 +553,44 @@
         "sums",
     )
     share = EDGE // owners
-    stats = jnp.concatenate([top[:, 0].T, total[:, 0].T], axis=1)
-    stats = jnp.pad(stats, ((0, 0), (0, HD - 2 * HEADS)))
-    parts = jnp.concatenate([numer, stats], axis=1).reshape(owners, share, width + HD)
-
-    picked_v, arrived_k, parts = lax.optimization_barrier((picked_v, arrived_k, parts))
-    arrived_v = fetch(picked_v)
-    base = [q, g, key_eff, left, right, edge, arrived_k]
-    value_global, value_padded, send_v = sparse(
-        value_kernel, place, position, base, [], per_dev, 0, "value_terms"
-    )
-
-    parts = lax.all_to_all(parts, "seq", split_axis=0, concat_axis=0, tiled=True)
-    tops = parts[:, :, width : width + HEADS]
+    stats = in_parts(jnp.concatenate([top[:, 0], total[:, 0]])).transpose(2, 0, 1)
+    stats = padded_rows(stats.reshape(owners, share * 6 * HEADS), 16)
+    extra = jnp.concatenate([pieces(numer), stats], axis=1)
+    picked_k, picked_v = pick(served, key_eff, v, extra, 16, per_dev, capacity)
+    picked_k, left, right = lax.optimization_barrier((picked_k, left, right))
+    arrived_k = exchange(picked_k)
+    parts = arrived_k[:, filled : filled + share * width // HD]
+    parts = parts.reshape(owners, share, HEADS, HD).astype(jnp.float32)
+    stats = arrived_k[:, filled + share * width // HD :].reshape(owners, -1)
+    stats = stats[:, : share * 6 * HEADS].reshape(owners, share, 3, 2 * HEADS)
+    stats = from_parts(stats, 2)
+    tops = stats[:, :, :HEADS]
     top_row = jnp.max(tops, axis=0)
     factor = jnp.exp(tops - top_row[None])
-    total_row = jnp.sum(factor * parts[:, :, width + HEADS : width + 2 * HEADS], axis=0)
-    numer_row = jnp.sum(
-        parts[:, :, :width].reshape(owners, share, HEADS, HD) * factor[..., None], axis=0
-    )
+    total_row = jnp.sum(factor * stats[:, :, HEADS:], axis=0)
+    numer_row = jnp.sum(parts * factor[..., None], axis=0)
     out_row = (numer_row / total_row[..., None]).astype(jnp.bfloat16)
     grad_row = lax.dynamic_slice_in_dim(edge[3], seq_place * share, share, axis=0)
     grad_row = grad_row.reshape(share, HEADS, HD).astype(jnp.float32)
     delta_row = jnp.sum(grad_row * out_row.astype(jnp.float32), axis=2)
-    row_stats = to_all(jnp.concatenate([top_row, total_row, delta_row], axis=1))
-    row_stats = row_stats.reshape(EDGE, 3, HEADS).transpose(1, 2, 0)[:, :, None]
-
-    arrived_v, send_v, row_stats = lax.optimization_barrier((arrived_v, send_v, row_stats))
-    returned_v = exchange(send_v, value_global)
+    row_stats = in_parts(jnp.stack([top_row, total_row, delta_row]))
+    row_stats = padded_rows(row_stats.reshape(1, 9 * share * HEADS), 16)
+    picked_v = picked_v.at[:, filled:].set(jnp.broadcast_to(row_stats, (owners, 16, HD)))
+    arrived_v = exchange(picked_v)
+
+    base = [q, g, key_eff, left, right, edge, arrived_k]
+    value_global, value_padded, send_v = sparse(
+        value_kernel, place, position, base, [], per_dev, capacity, share * width // HD, 0,
+        "value_terms",
+    )
+    arrived_v, send_v, value_global = lax.optimization_barrier((arrived_v, send_v, value_global))
+    row_stats = arrived_v[:, filled:].reshape(owners, -1)[:, : 9 * share * HEADS]
+    row_stats = from_parts(row_stats.reshape(owners, 3, 3, share, HEADS), 1)
+    row_stats = row_stats.transpose(1, 3, 0, 2).reshape(3, HEADS, 1, EDGE)
+    returned_v = exchange(send_v.at[:, filled:].set(pieces(value_global)))
     key_global, key_padded, send_k, att, dq = sparse(
-        key_kernel, place, position, base, [v, arrived_v], per_dev, 2, "key_terms"
+        key_kernel, place, position, base, [v, arrived_v], per_dev, capacity,
+        2 * share * width // HD, 2, "key_terms",
     )
     edge_dq, local = edge_call(
         edge_grad_kernel,
@@ -570,33 +608,35 @@
 
     near_v = neighbours(value_padded)
     near_k = neighbours(key_padded)
-    send_k, edge_dq, returned_v = lax.optimization_barrier((send_k, edge_dq, returned_v))
-    returned_k = exchange(send_k, key_global, edge_dq)
+    extra = jnp.concatenate([pieces(key_global), pieces(edge_dq)], axis=1)
+    send_k = send_k.at[:, filled:].set(extra)
+    send_k, returned_v = lax.optimization_barrier((send_k, returned_v))
+    returned_k = exchange(send_k)
     (dv,) = final(
         final_value_kernel, 1, capacity, place, served,
         (returned_v, value_padded, local, *near_v), (), per_dev, "final_value",
     )
-    returned_k, dv = lax.optimization_barrier((returned_k, dv))
 
     def summed(block):
         return jnp.sum(block.astype(jnp.float32), axis=0).astype(jnp.bfloat16).reshape(share, width)
 
-    piece = jnp.concatenate(
-        [
-            summed(returned_k[:, capacity]),
-            summed(returned_v[:, capacity]),
-            summed(returned_k[:, capacity + 1]),
-            out_row.reshape(share, width),
-        ]
-    )
-    collected = collect(piece, owners).reshape(owners, 4, share, width)
-    collected = collected.transpose(1, 0, 2, 3).reshape(4, EDGE, width)
+    def collected(first, second, number):
+        got = collect(jnp.concatenate([first, second]).reshape(16, -1), owners, number)
+        return got.reshape(owners, 2, share, width).transpose(1, 0, 2, 3).reshape(2, EDGE, width)
+
+    global_v, edge_out = collected(summed(returned_v[:, filled:]), out_row.reshape(share, width), 1)
+    returned_k, dv, global_v, edge_out = lax.optimization_barrier(
+        (returned_k, dv, global_v, edge_out)
+    )
+    count = share * width // HD
+    global_k, edge_dq = collected(
+        summed(returned_k[:, filled : filled + count]), summed(returned_k[:, filled + count :]), 2
+    )
     dk, att, dq, dv, gain_term = final(
         final_key_kernel, 0, capacity, place, served,
         (returned_k, key_padded, local, *near_k),
         (
-            collected[0], collected[1], collected[2], collected[3], keys[0], key_gain[None], att,
-            dq, dv,
+            global_k, global_v, edge_dq, edge_out, keys[0], key_gain[None], att, dq, dv,
         ),
         per_dev, "final_key",
     )

time: 713 us -> 678 us (0.951)
  Pallas kernels: 204 us -> 322 us
  waiting for transfers between devices: 340 us -> 246 us
  starting transfers between devices: 92.4 us -> 47.8 us
  blocking collectives: 23 us -> 12.3 us
    pallas_call x1 -> x2, Pallas kernels: 26.4 us -> 135 us  [collect(): pl.pallas_call(functools.partial(collect_kernel, count), in_specs=[WHOLE]...]
    all_to_all x5 -> x4, waiting for transfers between devices: 337 us -> 246 us  [exchange(): return lax.all_to_all(slots, 'seq', split_axis=0, concat_axis=0, tiled=True)]
    all_to_all x5 -> x4, starting transfers between devices: 72.8 us -> 28 us  [exchange(): return lax.all_to_all(slots, 'seq', split_axis=0, concat_axis=0, tiled=True)]
    concatenate x6 -> x3, other arithmetic: 13 us -> 0.93 us  [the longest x1 0.88 us: shards(): extra = jnp.concatenate([pieces(numer), stats], axis=1)]
    all_to_all x2 -> x1, blocking collectives: 23 us -> 12.3 us  [to_all(): lax.all_to_all(spread_out, 'seq', split_axis=0, concat_axis=0, tiled=True)]
    pallas_call x1, Pallas kernels: 26.2 us -> 34.8 us  [spread(): pl.pallas_call(functools.partial(spread_kernel, count), in_specs=[WHOLE],...]
  transfers between devices with their start and end apart: 12 -> 11, of which waited for: 6 -> 3; matrix products, arithmetic and copies ran while one was open for 4% -> 5% of each run, Pallas kernels for 24% -> 45%
where the time goes in v4:
time: 678 us; the launch traced here: 676 us
  Pallas kernels  322 us (47%)
  waiting for transfers between devices  246 us (36%)
  starting transfers between devices  47.8 us (7%)
  local copies, waits for them, and re-layouts  26.4 us (4%)
  other arithmetic  19.3 us (3%)
  blocking collectives  12.3 us (2%)
    all_to_all x4, waiting for transfers between devices, exchange(): return lax.all_to_all(slots, 'seq', split_axis=0, concat_axis=0, tiled=True)  246 us
    pallas_call x2, Pallas kernels, collect(): pl.pallas_call(functools.partial(collect_kernel, count), in_specs=[WHOLE]...  135 us
    pallas_call x2, Pallas kernels, sparse(): pl.pallas_call(functools.partial(kernel, per_dev, capacity), grid_spec=pl...  75.1 us
    pallas_call x2, Pallas kernels, final(): pl.pallas_call(functools.partial(kernel, per_dev, capacity), grid_spec=pl...  40.1 us
    pallas_call x1, Pallas kernels, spread(): pl.pallas_call(functools.partial(spread_kernel, count), in_specs=[WHOLE],...  34.8 us
    all_to_all x4, starting transfers between devices, exchange(): return lax.all_to_all(slots, 'seq', split_axis=0, concat_axis=0, tiled=True)  28 us
    pallas_call x2, Pallas kernels, edge_call(): pl.pallas_call(kernel, grid=(HEADS,), in_specs=specs, out_specs=out_specs...  26.3 us
  transfers between devices with their start and end apart: 11, of which 3 were waited for; matrix products, arithmetic and copies ran while one was open for 5% of the time, Pallas kernels for 45%

profile of v4, /device:TPU:0, one launch (start us, length us, event | category | flops | bytes accessed | tf_op | source)
XLA Modules:
  0.0 675.6 jit_solution(15078701809500899801)
XLA Ops:
  3.4 7.3 %all-to-all-start = ((s32[32,1,9]{2,1,0:T(1,128)}), s32[32,1,9]{2,1,0:T(1,128)S(1)}, u32[]{:S(2)}, u32[]{:S(2)}) async-start(s32[32,1,9]{2,1,0:T(1,128)} %bitcast.2), calls=%async_computation | async-start | bytes 32768 | tf_op jit(solution)/shard_map/all_to_all | solution.py:520
  10.7 1.1 fusion.17
  11.8 1.5 multiply_convert_fusion.k_ref.key_ref
  13.4 0.8 pad_maximum_fusion.2
  14.2 2.3 collective-permute-start
  16.5 0.8 pad_maximum_fusion.3
  17.4 1.3 collective-permute-start.1
  19.0 34.8 %spread.1 = bf16[16,32,2048]{2,1,0:T(8,128)(2,1)S(1)} custom-call(bf16[16,32,2048]{2,1,0:T(8,128)(2,1)S(1)} %bitcast.84), custom_call_target="tpu_custom_call" | custom-call | tf_op jit(solution)/shard_map/spread/pallas_call | solution.py:111
  53.9 1.3 copy-done
  55.1 12.5 %sums.1 = (f32[16,1,128]{2,1,0:T(1,128)}, f32[16,1,128]{2,1,0:T(1,128)}, f32[128,2048]{1,0:T(8,128)}) custom-call(bf16[4,128,2048]{2,1,0:T(8,128)(2,1)} %bitcast.80, bf16[256,2048]{1,0:T(8,128)(2,1)} %copy-done.1, bf16[256,2048]{1,0:T(8,128)(2,1)} %bitcast.85), custom_call_target="tpu_custom_call" | custom-call | tf_op jit(solution)/shard_map/sums/pallas_call | solution.py:374
  67.7 1.3 convert_element_type.82
  70.3 0.9 pad_maximum_fusion.1.extra_ref
  73.1 11.5 %pick.1 = (bf16[32,656,128]{2,1,0:T(8,128)(2,1)}, bf16[32,592,128]{2,1,0:T(8,128)(2,1)}) custom-call(s32[288]{0:T(512)} %reshape.597.index_ref.served_ref, bf16[256,2048]{1,0:T(8,128)(2,1)} %copy-done.1, bf16[256,2048]{1,0:T(8,128)(2,1)} %bitcast.86, bf16[32,80,128]{2,1,0:T(8,128)(2,1)} %pad_maximum_fusion.1.extra_ref), custom_call_target="tpu_custom_call" | custom-call | tf_op jit(solution)/shard_map/pick/pallas_call | solution.py:205
  85.4 16.9 %all-to-all-start.1 = ((bf16[32,656,128]{2,1,0:T(8,128)(2,1)}), bf16[32,656,128]{2,1,0:T(8,128)(2,1)}, u32[]{:S(2)}, u32[]{:S(2)}) async-start(bf16[32,656,128]{2,1,0:T(8,128)(2,1)} %get-tuple-element.79), calls=%async_computation.1 | async-start | bytes 10747904 | tf_op jit(solution)/shard_map/all_to_all | solution.py:525
  102.2 1.1 slice.206
  103.3 118.6 %all-to-all-done.1.arrived_ref = bf16[32,656,128]{2,1,0:T(8,128)(2,1)} async-done(((bf16[32,656,128]{2,1,0:T(8,128)(2,1)}), bf16[32,656,128]{2,1,0:T(8,128)(2,1)}, u32[]{:S(2)}, u32[]{:S(2)}) %all-to-all-start.1) | async-done | bytes 5373984 | tf_op jit(solution)/shard_map/all_to_all | solution.py:525
  221.9 0.9 slice.228
  223.5 1.4 multiply_reduce_fusion
  225.9 3.6 all-to-all-start.2
  230.1 27.9 %value_terms.1 = (f32[128,2048]{1,0:T(8,128)}, f32[384,2048]{1,0:T(8,128)}, bf16[32,640,128]{2,1,0:T(8,128)(2,1)}) custom-call(s32[2]{0:T(128)} %pad_add_fusion.place_ref, s32[192]{0:T(256)} %copy-done.9, bf16[256,2048]{1,0:T(8,128)(2,1)} %bitcast.89, bf16[256,2048]{1,0:T(8,128)(2,1)} %bitcast.91, bf16[256,2048]{1,0:T(8,128)(2,1)} %copy-done.1, ...), custom_call_target="tpu_custom_call" | custom-call | tf_op jit(solution)/shard_map/value_terms/pallas_call | solution.py:330
  258.0 79.6 %all-to-all-done.2.arrived_v_ref = bf16[32,592,128]{2,1,0:T(8,128)(2,1)} async-done(((bf16[32,592,128]{2,1,0:T(8,128)(2,1)}), bf16[32,592,128]{2,1,0:T(8,128)(2,1)}, u32[]{:S(2)}, u32[]{:S(2)}) %all-to-all-start.2) | async-done | bytes 4849696 | tf_op jit(solution)/shard_map/all_to_all | solution.py:525
  337.6 1.3 convert_element_type.95
  339.2 0.9 constant_dynamic-update-slice_fusion
  340.1 3.9 all-to-all-start.3
  344.0 0.9 slice.208
  347.6 47.2 %key_terms.1 = (f32[128,2048]{1,0:T(8,128)}, f32[384,2048]{1,0:T(8,128)}, bf16[32,704,128]{2,1,0:T(8,128)(2,1)}, bf16[256,2048]{1,0:T(8,128)(2,1)}, bf16[256,2048]{1,0:T(8,128)(2,1)}) custom-call(s32[2]{0:T(128)} %pad_add_fusion.place_ref, s32[192]{0:T(256)} %copy-done.9, bf16[256,2048]{1,0:T(8,128)(2,1)} %bitcast.90, bf16[256,2048]{1,0:T(8,128)(2,1)} %bitcast.92, ...), custom_call_target="tpu_custom_call" | custom-call | tf_op jit(solution)/shard_map/key_terms/pallas_call | solution.py:330
  394.8 1.3 convert_element_type.91
  396.3 13.8 %grads.1 = (f32[128,2048]{1,0:T(8,128)}, f32[2,256,2048]{2,1,0:T(8,128)}) custom-call(bf16[4,128,2048]{2,1,0:T(8,128)(2,1)} %bitcast.83, bf16[256,2048]{1,0:T(8,128)(2,1)} %copy-done.1, bf16[256,2048]{1,0:T(8,128)(2,1)} %bitcast.88, f32[16,1,128]{2,1,0:T(1,128)} %copy.74.top_ref, f32[16,1,128]{2,1,0:T(1,128)} %copy.75.total_ref, f32[16,1,128]{2,1,0:T(1,128)} %copy.76.delta_ref), custom_call_target="tpu_custom_call" | custom-call | tf_op jit(solution)/shard_map/grads/pallas_call | solution.py:374
  410.1 1.3 convert_element_type.94
  411.7 1.2 maximum_dynamic-update-slice_fusion
  412.9 47.8 %all-to-all-done.3.returned_ref = bf16[32,640,128]{2,1,0:T(8,128)(2,1)} async-done(((bf16[32,640,128]{2,1,0:T(8,128)(2,1)}), bf16[32,640,128]{2,1,0:T(8,128)(2,1)}, u32[]{:S(2)}, u32[]{:S(2)}) %all-to-all-start.3) | async-done | bytes 5242912 | tf_op jit(solution)/shard_map/all_to_all | solution.py:525
  460.7 3.6 all-to-all-start.4
  465.5 2.2 collective-permute-start.3
  467.7 1.3 collective-permute-start.2
  470.0 4.2 collective-permute-start.5
  474.2 1.3 collective-permute-start.4
  475.5 1.1 slice_reduce_fusion.2
  476.7 125.5 %collect_1.1 = bf16[32,16,1024]{2,1,0:T(8,128)(2,1)S(1)} custom-call(bf16[16,1024]{1,0:T(8,128)(2,1)S(1)} %reshape.609.in_ref), custom_call_target="tpu_custom_call" | custom-call | tf_op jit(solution)/shard_map/collect_1/pallas_call | solution.py:165
  603.9 0.9 unstack.27.eout_ref
  604.8 0.9 unstack.25.gv_ref
  606.5 19.0 %final_value.1.dv_ref = f32[256,2048]{1,0:T(8,128)} custom-call(s32[2]{0:T(128)} %pad_add_fusion.place_ref, s32[288]{0:T(512)} %reshape.597.index_ref.served_ref, bf16[32,640,128]{2,1,0:T(8,128)(2,1)} %all-to-all-done.3.returned_ref, f32[384,2048]{1,0:T(8,128)} %get-tuple-element.91.padded_ref, f32[2,256,2048]{2,1,0:T(8,128)} %get-tuple-element.92.local_ref, ...), custom_call_target="tpu_custom_call" | custom-call | tf_op jit(solution)/shard_map/final_value/pallas_call | solution.py:472
  625.5 1.4 slice_reduce_fusion.1
  627.0 9.2 %collect_2.1 = bf16[32,16,1024]{2,1,0:T(8,128)(2,1)S(1)} custom-call(bf16[16,1024]{1,0:T(8,128)(2,1)S(1)} %reshape.613.in_ref), custom_call_target="tpu_custom_call" | custom-call | tf_op jit(solution)/shard_map/collect_2/pallas_call | solution.py:165
  637.9 0.9 unstack.31.edq_ref
  638.9 0.9 unstack.29.gk_ref
  640.6 21.1 %final_key.1 = (bf16[256,2048]{1,0:T(8,128)(2,1)}, bf16[256,2048]{1,0:T(8,128)(2,1)}, bf16[256,2048]{1,0:T(8,128)(2,1)}, bf16[256,2048]{1,0:T(8,128)(2,1)}, f32[1,2048]{1,0:T(1,128)}) custom-call(s32[2]{0:T(128)} %pad_add_fusion.place_ref, s32[288]{0:T(512)} %reshape.597.index_ref.served_ref, bf16[32,704,128]{2,1,0:T(8,128)(2,1)} %all-to-all-done.4.returned_ref, ...), custom_call_target="tpu_custom_call" | custom-call | tf_op jit(solution)/shard_map/final_key/pallas_call | solution.py:472
  661.7 0.8 broadcast_in_dim.58
  662.5 12.3 %all_to_all.31 = f32[32,1,2048]{2,1,0:T(1,128)S(1)} all-to-all(f32[32,1,2048]{2,1,0:T(1,128)S(1)} %broadcast_in_dim.58), channel_id=1, replica_groups=mesh['dp'=1,'seq'=32] {'seq'}, dimensions={0} | all-to-all | bytes 524288 | tf_op jit(solution)/shard_map/all_to_all | solution.py:529
  (111 shorter events, 20.7 us)
Async XLA Ops:
  2.6 14.8 %copy-start.9 = (s32[192]{0:T(256)}, s32[192]{0:T(256)S(1)}, u32[]{:S(2)}) copy-start(s32[192]{0:T(256)S(1)} %multiply_add_fusion.pos_ref) | copy-start | bytes 2308
  3.4 67.7 %all-to-all-start = ((s32[32,1,9]{2,1,0:T(1,128)}), s32[32,1,9]{2,1,0:T(1,128)S(1)}, u32[]{:S(2)}, u32[]{:S(2)}) async-start(s32[32,1,9]{2,1,0:T(1,128)} %bitcast.2), calls=%async_computation | async-start | bytes 32768 | tf_op jit(solution)/shard_map/all_to_all | solution.py:520
  13.3 5.4 copy-start.1
  13.4 5.4 slice-start
  13.4 5.4 slice-start.1
  13.4 5.4 slice-start.2
  14.2 70.3 %collective-permute-start = (bf16[2,64,2048]{2,1,0:T(8,128)(2,1)}, bf16[2,64,2048]{2,1,0:T(8,128)(2,1)S(1)}, u32[]{:S(2)}, u32[]{:S(2)}) collective-permute-start(bf16[2,64,2048]{2,1,0:T(8,128)(2,1)} %pad_maximum_fusion.2), channel_id=1, source_target_pairs={{0,1},{1,2},{2,3},{3,4},{4,5},{5,6},{6,7},{7,8},{8,9},{9,10},{10,1... | collective-permute-start | bytes 1572872 | tf_op jit(solution)/shard_map/ppermute | solution.py:38
  17.4 67.2 %collective-permute-start.1 = (bf16[2,64,2048]{2,1,0:T(8,128)(2,1)}, bf16[2,64,2048]{2,1,0:T(8,128)(2,1)}, u32[]{:S(2)}, u32[]{:S(2)}) collective-permute-start(bf16[2,64,2048]{2,1,0:T(8,128)(2,1)} %pad_maximum_fusion.3), channel_id=1, source_target_pairs={{1,0},{2,1},{3,2},{4,3},{5,4},{6,5},{7,6},{8,7},{9,8},{10,9},{11,1... | collective-permute-start | bytes 1572872 | tf_op jit(solution)/shard_map/ppermute | solution.py:38
  53.9 1.3 copy-start
  84.6 0.8 copy-start.4
  85.4 136.5 %all-to-all-start.1 = ((bf16[32,656,128]{2,1,0:T(8,128)(2,1)}), bf16[32,656,128]{2,1,0:T(8,128)(2,1)}, u32[]{:S(2)}, u32[]{:S(2)}) async-start(bf16[32,656,128]{2,1,0:T(8,128)(2,1)} %get-tuple-element.79), calls=%async_computation.1 | async-start | bytes 10747904 | tf_op jit(solution)/shard_map/all_to_all | solution.py:525
  225.9 111.7 %all-to-all-start.2 = ((bf16[32,592,128]{2,1,0:T(8,128)(2,1)}), bf16[32,592,128]{2,1,0:T(8,128)(2,1)}, u32[]{:S(2)}, u32[]{:S(2)}) async-start(bf16[32,592,128]{2,1,0:T(8,128)(2,1)} %broadcast_dynamic-update-slice_fusion), calls=%async_computation.2 | async-start | bytes 9699328 | tf_op jit(solution)/shard_map/all_to_all | solution.py:525
  340.1 120.6 %all-to-all-start.3 = ((bf16[32,640,128]{2,1,0:T(8,128)(2,1)}), bf16[32,640,128]{2,1,0:T(8,128)(2,1)}, u32[]{:S(2)}, u32[]{:S(2)}) async-start(bf16[32,640,128]{2,1,0:T(8,128)(2,1)} %constant_dynamic-update-slice_fusion), calls=%async_computation.3 | async-start | bytes 10485760 | tf_op jit(solution)/shard_map/all_to_all | solution.py:525
  412.9 51.5 %copy-start.2 = (f32[384,2048]{1,0:T(8,128)S(1)}, f32[384,2048]{1,0:T(8,128)}, u32[]{:S(2)}) copy-start(f32[384,2048]{1,0:T(8,128)} %get-tuple-element.91.padded_ref) | copy-start | bytes 9437188
  460.7 164.8 %all-to-all-start.4 = ((bf16[32,704,128]{2,1,0:T(8,128)(2,1)}), bf16[32,704,128]{2,1,0:T(8,128)(2,1)}, u32[]{:S(2)}, u32[]{:S(2)}) async-start(bf16[32,704,128]{2,1,0:T(8,128)(2,1)} %maximum_dynamic-update-slice_fusion), calls=%async_computation.4 | async-start | bytes 11534336 | tf_op jit(solution)/shard_map/all_to_all | solution.py:525
  464.4 4.6 copy-start.3
  465.5 140.3 %collective-permute-start.3 = (bf16[64,2048]{1,0:T(8,128)(2,1)}, bf16[64,2048]{1,0:T(8,128)(2,1)S(1)}, u32[]{:S(2)}, u32[]{:S(2)}) collective-permute-start(bf16[64,2048]{1,0:T(8,128)(2,1)} %get-tuple-element.111), channel_id=1, source_target_pairs={{0,1},{1,2},{2,3},{3,4},{4,5},{5,6},{6,7},{7,8},{8,9},{9,10},{10,1... | collective-permute-start | bytes 786440 | tf_op jit(solution)/shard_map/ppermute | solution.py:38
  467.7 138.1 %collective-permute-start.2 = (bf16[64,2048]{1,0:T(8,128)(2,1)}, bf16[64,2048]{1,0:T(8,128)(2,1)S(1)}, u32[]{:S(2)}, u32[]{:S(2)}) collective-permute-start(bf16[64,2048]{1,0:T(8,128)(2,1)} %get-tuple-element.112), channel_id=1, source_target_pairs={{1,0},{2,1},{3,2},{4,3},{5,4},{6,5},{7,6},{8,7},{9,8},{10,9},{11,1... | collective-permute-start | bytes 786440 | tf_op jit(solution)/shard_map/ppermute | solution.py:38
  470.0 169.8 %collective-permute-start.5 = (bf16[64,2048]{1,0:T(8,128)(2,1)}, bf16[64,2048]{1,0:T(8,128)(2,1)S(1)}, u32[]{:S(2)}, u32[]{:S(2)}) collective-permute-start(bf16[64,2048]{1,0:T(8,128)(2,1)} %get-tuple-element.109), channel_id=1, source_target_pairs={{0,1},{1,2},{2,3},{3,4},{4,5},{5,6},{6,7},{7,8},{8,9},{9,10},{10,1... | collective-permute-start | bytes 786440 | tf_op jit(solution)/shard_map/ppermute | solution.py:38
  474.2 165.6 %collective-permute-start.4 = (bf16[64,2048]{1,0:T(8,128)(2,1)S(1)}, bf16[64,2048]{1,0:T(8,128)(2,1)S(1)}, u32[]{:S(2)}, u32[]{:S(2)}) collective-permute-start(bf16[64,2048]{1,0:T(8,128)(2,1)S(1)} %get-tuple-element.110), channel_id=1, source_target_pairs={{1,0},{2,1},{3,2},{4,3},{5,4},{6,5},{7,6},{8,7},{9,8},{10,9},{11,1... | collective-permute-start | bytes 786440 | tf_op jit(solution)/shard_map/ppermute | solution.py:38
  605.8 0.7 copy-start.7
  605.8 0.8 copy-start.8
  639.8 0.7 copy-start.5
  639.8 0.8 copy-start.6

commit v5 on v4

--- a/solution.py
+++ b/solution.py
@@ -196,7 +196,7 @@
         value_out[owner, place, :] = value_ref[rows, cols]
         return carry
 
-    lax.fori_loop(0, key_out.shape[0] * capacity, step, 0)
+    lax.fori_loop(0, key_out.shape[0] * capacity, step, 0, unroll=4)
 
 
 def pick(index, key_eff, values, extra, more, per_dev, capacity):
@@ -536,7 +536,7 @@
         return flat.reshape(flat.shape[0], count, HD)
 
     edge = jnp.stack([q[:EDGE], key_eff[:EDGE], v[:EDGE], g[:EDGE]])
-    edge = spread(edge.reshape(16, 4 * EDGE // 16, width), owners).reshape(4, EDGE, width)
+    edge = spread(edge.reshape(32, 4 * EDGE // 32, width), owners).reshape(4, EDGE, width)
     tails = jnp.stack([key_eff[tok - BLOCK :], v[tok - BLOCK :]])
     heads = jnp.stack([key_eff[:BLOCK], v[:BLOCK]])
     left = passed_along(tails, "seq", 1)
@@ -624,6 +624,7 @@
         got = collect(jnp.concatenate([first, second]).reshape(16, -1), owners, number)
         return got.reshape(owners, 2, share, width).transpose(1, 0, 2, 3).reshape(2, EDGE, width)
 
+    returned_v, dv = lax.optimization_barrier((returned_v, dv))
     global_v, edge_out = collected(summed(returned_v[:, filled:]), out_row.reshape(share, width), 1)
     returned_k, dv, global_v, edge_out = lax.optimization_barrier(
         (returned_k, dv, global_v, edge_out)

time: 678 us -> 676 us (level)
  transfers between devices with their start and end apart: 11 -> 11, of which waited for: 3 -> 3; matrix products, arithmetic and copies ran while one was open for 5% -> 4% of each run, Pallas kernels for 45% -> 45%
where the time goes in v5:
time: 676 us; the launch traced here: 674 us
  Pallas kernels  325 us (48%)
  waiting for transfers between devices  246 us (36%)
  starting transfers between devices  45.1 us (7%)
  local copies, waits for them, and re-layouts  24.9 us (4%)
  other arithmetic  19.2 us (3%)
  blocking collectives  12.3 us (2%)
    all_to_all x4, waiting for transfers between devices, exchange(): return lax.all_to_all(slots, 'seq', split_axis=0, concat_axis=0, tiled=True)  246 us
    pallas_call x2, Pallas kernels, collect(): pl.pallas_call(functools.partial(collect_kernel, count), in_specs=[WHOLE]...  137 us
    pallas_call x2, Pallas kernels, sparse(): pl.pallas_call(functools.partial(kernel, per_dev, capacity), grid_spec=pl...  75.1 us
    pallas_call x2, Pallas kernels, final(): pl.pallas_call(functools.partial(kernel, per_dev, capacity), grid_spec=pl...  40 us
    pallas_call x1, Pallas kernels, spread(): pl.pallas_call(functools.partial(spread_kernel, count), in_specs=[WHOLE],...  35.5 us
    pallas_call x2, Pallas kernels, edge_call(): pl.pallas_call(kernel, grid=(HEADS,), in_specs=specs, out_specs=out_specs...  26.3 us
    all_to_all x4, starting transfers between devices, exchange(): return lax.all_to_all(slots, 'seq', split_axis=0, concat_axis=0, tiled=True)  25 us
  transfers between devices with their start and end apart: 11, of which 3 were waited for; matrix products, arithmetic and copies ran while one was open for 4% of the time, Pallas kernels for 45%

profile of v5, /device:TPU:0, one launch (start us, length us, event | category | flops | bytes accessed | tf_op | source)
XLA Modules:
  0.0 674.1 jit_solution(6425599388585297586)
XLA Ops:
  3.4 7.3 %all-to-all-start = ((s32[32,1,9]{2,1,0:T(1,128)}), s32[32,1,9]{2,1,0:T(1,128)S(1)}, u32[]{:S(2)}, u32[]{:S(2)}) async-start(s32[32,1,9]{2,1,0:T(1,128)} %bitcast.2), calls=%async_computation | async-start | bytes 32768 | tf_op jit(solution)/shard_map/all_to_all | solution.py:520
  10.7 1.1 fusion.17
  11.8 1.5 multiply_convert_fusion.k_ref.key_ref
  13.4 0.8 pad_maximum_fusion.2
  14.2 2.3 collective-permute-start
  16.5 0.8 pad_maximum_fusion.3
  17.4 1.3 collective-permute-start.1
  19.0 35.5 %spread.1 = bf16[32,16,2048]{2,1,0:T(8,128)(2,1)S(1)} custom-call(bf16[32,16,2048]{2,1,0:T(8,128)(2,1)S(1)} %bitcast.84), custom_call_target="tpu_custom_call" | custom-call | tf_op jit(solution)/shard_map/spread/pallas_call | solution.py:111
  54.6 1.3 copy-done
  55.9 12.5 %sums.1 = (f32[16,1,128]{2,1,0:T(1,128)}, f32[16,1,128]{2,1,0:T(1,128)}, f32[128,2048]{1,0:T(8,128)}) custom-call(bf16[4,128,2048]{2,1,0:T(8,128)(2,1)} %bitcast.80, bf16[256,2048]{1,0:T(8,128)(2,1)} %copy-done.1, bf16[256,2048]{1,0:T(8,128)(2,1)} %bitcast.85), custom_call_target="tpu_custom_call" | custom-call | tf_op jit(solution)/shard_map/sums/pallas_call | solution.py:374
  68.4 1.3 convert_element_type.82
  71.0 0.9 pad_maximum_fusion.1.extra_ref
  73.8 11.0 %pick.1 = (bf16[32,656,128]{2,1,0:T(8,128)(2,1)}, bf16[32,592,128]{2,1,0:T(8,128)(2,1)}) custom-call(s32[288]{0:T(512)} %reshape.597.index_ref.served_ref, bf16[256,2048]{1,0:T(8,128)(2,1)} %copy-done.1, bf16[256,2048]{1,0:T(8,128)(2,1)} %bitcast.86, bf16[32,80,128]{2,1,0:T(8,128)(2,1)} %pad_maximum_fusion.1.extra_ref), custom_call_target="tpu_custom_call" | custom-call | tf_op jit(solution)/shard_map/pick/pallas_call | solution.py:205
  85.6 14.0 %all-to-all-start.1 = ((bf16[32,656,128]{2,1,0:T(8,128)(2,1)}), bf16[32,656,128]{2,1,0:T(8,128)(2,1)}, u32[]{:S(2)}, u32[]{:S(2)}) async-start(bf16[32,656,128]{2,1,0:T(8,128)(2,1)} %get-tuple-element.81), calls=%async_computation.1 | async-start | bytes 10747904 | tf_op jit(solution)/shard_map/all_to_all | solution.py:525
  99.6 1.1 slice.206
  100.7 118.6 %all-to-all-done.1.arrived_ref = bf16[32,656,128]{2,1,0:T(8,128)(2,1)} async-done(((bf16[32,656,128]{2,1,0:T(8,128)(2,1)}), bf16[32,656,128]{2,1,0:T(8,128)(2,1)}, u32[]{:S(2)}, u32[]{:S(2)}) %all-to-all-start.1) | async-done | bytes 5373984 | tf_op jit(solution)/shard_map/all_to_all | solution.py:525
  219.3 0.9 slice.228
  220.8 1.4 multiply_reduce_fusion
  223.3 3.6 all-to-all-start.2
  227.5 27.9 %value_terms.1 = (f32[128,2048]{1,0:T(8,128)}, f32[384,2048]{1,0:T(8,128)}, bf16[32,640,128]{2,1,0:T(8,128)(2,1)}) custom-call(s32[2]{0:T(128)} %pad_add_fusion.place_ref, s32[192]{0:T(256)} %copy-done.9, bf16[256,2048]{1,0:T(8,128)(2,1)} %bitcast.89, bf16[256,2048]{1,0:T(8,128)(2,1)} %bitcast.91, bf16[256,2048]{1,0:T(8,128)(2,1)} %copy-done.1, ...), custom_call_target="tpu_custom_call" | custom-call | tf_op jit(solution)/shard_map/value_terms/pallas_call | solution.py:330
  255.4 79.6 %all-to-all-done.2.arrived_v_ref = bf16[32,592,128]{2,1,0:T(8,128)(2,1)} async-done(((bf16[32,592,128]{2,1,0:T(8,128)(2,1)}), bf16[32,592,128]{2,1,0:T(8,128)(2,1)}, u32[]{:S(2)}, u32[]{:S(2)}) %all-to-all-start.2) | async-done | bytes 4849696 | tf_op jit(solution)/shard_map/all_to_all | solution.py:525
  335.0 1.3 convert_element_type.95
  336.5 0.9 constant_dynamic-update-slice_fusion
  337.4 3.9 all-to-all-start.3
  341.3 0.9 slice.208
  344.9 47.2 %key_terms.1 = (f32[128,2048]{1,0:T(8,128)}, f32[384,2048]{1,0:T(8,128)}, bf16[32,704,128]{2,1,0:T(8,128)(2,1)}, bf16[256,2048]{1,0:T(8,128)(2,1)}, bf16[256,2048]{1,0:T(8,128)(2,1)}) custom-call(s32[2]{0:T(128)} %pad_add_fusion.place_ref, s32[192]{0:T(256)} %copy-done.9, bf16[256,2048]{1,0:T(8,128)(2,1)} %bitcast.90, bf16[256,2048]{1,0:T(8,128)(2,1)} %bitcast.92, ...), custom_call_target="tpu_custom_call" | custom-call | tf_op jit(solution)/shard_map/key_terms/pallas_call | solution.py:330
  392.1 1.3 convert_element_type.91
  393.7 13.8 %grads.1 = (f32[128,2048]{1,0:T(8,128)}, f32[2,256,2048]{2,1,0:T(8,128)}) custom-call(bf16[4,128,2048]{2,1,0:T(8,128)(2,1)} %bitcast.83, bf16[256,2048]{1,0:T(8,128)(2,1)} %copy-done.1, bf16[256,2048]{1,0:T(8,128)(2,1)} %bitcast.88, f32[16,1,128]{2,1,0:T(1,128)} %copy.74.top_ref, f32[16,1,128]{2,1,0:T(1,128)} %copy.75.total_ref, f32[16,1,128]{2,1,0:T(1,128)} %copy.76.delta_ref), custom_call_target="tpu_custom_call" | custom-call | tf_op jit(solution)/shard_map/grads/pallas_call | solution.py:374
  407.5 1.3 convert_element_type.94
  409.0 1.2 maximum_dynamic-update-slice_fusion
  410.2 47.8 %all-to-all-done.3.returned_ref = bf16[32,640,128]{2,1,0:T(8,128)(2,1)} async-done(((bf16[32,640,128]{2,1,0:T(8,128)(2,1)}), bf16[32,640,128]{2,1,0:T(8,128)(2,1)}, u32[]{:S(2)}, u32[]{:S(2)}) %all-to-all-start.3) | async-done | bytes 5242912 | tf_op jit(solution)/shard_map/all_to_all | solution.py:525
  458.1 3.6 all-to-all-start.4
  462.0 2.2 collective-permute-start.3
  464.3 1.3 collective-permute-start.2
  465.9 4.2 collective-permute-start.5
  470.1 1.5 collective-permute-start.4
  472.3 18.9 %final_value.1.dv_ref = f32[256,2048]{1,0:T(8,128)} custom-call(s32[2]{0:T(128)} %pad_add_fusion.place_ref, s32[288]{0:T(512)} %reshape.597.index_ref.served_ref, bf16[32,640,128]{2,1,0:T(8,128)(2,1)} %all-to-all-done.3.returned_ref, f32[384,2048]{1,0:T(8,128)} %get-tuple-element.93.padded_ref, f32[2,256,2048]{2,1,0:T(8,128)} %get-tuple-element.94.local_ref, ...), custom_call_target="tpu_custom_call" | custom-call | tf_op jit(solution)/shard_map/final_value/pallas_call | solution.py:472
  491.3 1.1 slice_reduce_fusion.2
  492.5 128.0 %collect_1.1 = bf16[32,16,1024]{2,1,0:T(8,128)(2,1)S(1)} custom-call(bf16[16,1024]{1,0:T(8,128)(2,1)S(1)} %reshape.609.in_ref), custom_call_target="tpu_custom_call" | custom-call | tf_op jit(solution)/shard_map/collect_1/pallas_call | solution.py:165
  622.3 0.9 unstack.27.eout_ref
  623.2 0.9 unstack.25.gv_ref
  624.1 1.4 slice_reduce_fusion.1
  625.5 9.2 %collect_2.1 = bf16[32,16,1024]{2,1,0:T(8,128)(2,1)S(1)} custom-call(bf16[16,1024]{1,0:T(8,128)(2,1)S(1)} %reshape.613.in_ref), custom_call_target="tpu_custom_call" | custom-call | tf_op jit(solution)/shard_map/collect_2/pallas_call | solution.py:165
  636.5 0.9 unstack.31.edq_ref
  637.4 0.9 unstack.29.gk_ref
  639.1 21.1 %final_key.1 = (bf16[256,2048]{1,0:T(8,128)(2,1)}, bf16[256,2048]{1,0:T(8,128)(2,1)}, bf16[256,2048]{1,0:T(8,128)(2,1)}, bf16[256,2048]{1,0:T(8,128)(2,1)}, f32[1,2048]{1,0:T(1,128)}) custom-call(s32[2]{0:T(128)} %pad_add_fusion.place_ref, s32[288]{0:T(512)} %reshape.597.index_ref.served_ref, bf16[32,704,128]{2,1,0:T(8,128)(2,1)} %all-to-all-done.4.returned_ref, ...), custom_call_target="tpu_custom_call" | custom-call | tf_op jit(solution)/shard_map/final_key/pallas_call | solution.py:472
  660.2 0.8 broadcast_in_dim.58
  661.0 12.3 %all_to_all.31 = f32[32,1,2048]{2,1,0:T(1,128)S(1)} all-to-all(f32[32,1,2048]{2,1,0:T(1,128)S(1)} %broadcast_in_dim.58), channel_id=1, replica_groups=mesh['dp'=1,'seq'=32] {'seq'}, dimensions={0} | all-to-all | bytes 524288 | tf_op jit(solution)/shard_map/all_to_all | solution.py:529
  (111 shorter events, 19.2 us)
Async XLA Ops:
  2.6 14.8 %copy-start.9 = (s32[192]{0:T(256)}, s32[192]{0:T(256)S(1)}, u32[]{:S(2)}) copy-start(s32[192]{0:T(256)S(1)} %multiply_add_fusion.pos_ref) | copy-start | bytes 2308
  3.4 68.5 %all-to-all-start = ((s32[32,1,9]{2,1,0:T(1,128)}), s32[32,1,9]{2,1,0:T(1,128)S(1)}, u32[]{:S(2)}, u32[]{:S(2)}) async-start(s32[32,1,9]{2,1,0:T(1,128)} %bitcast.2), calls=%async_computation | async-start | bytes 32768 | tf_op jit(solution)/shard_map/all_to_all | solution.py:520
  13.3 5.4 copy-start.1
  13.4 5.4 slice-start
  13.4 5.4 slice-start.1
  13.4 5.4 slice-start.2
  14.2 70.6 %collective-permute-start = (bf16[2,64,2048]{2,1,0:T(8,128)(2,1)}, bf16[2,64,2048]{2,1,0:T(8,128)(2,1)S(1)}, u32[]{:S(2)}, u32[]{:S(2)}) collective-permute-start(bf16[2,64,2048]{2,1,0:T(8,128)(2,1)} %pad_maximum_fusion.2), channel_id=1, source_target_pairs={{0,1},{1,2},{2,3},{3,4},{4,5},{5,6},{6,7},{7,8},{8,9},{9,10},{10,1... | collective-permute-start | bytes 1572872 | tf_op jit(solution)/shard_map/ppermute | solution.py:38
  17.4 67.4 %collective-permute-start.1 = (bf16[2,64,2048]{2,1,0:T(8,128)(2,1)}, bf16[2,64,2048]{2,1,0:T(8,128)(2,1)}, u32[]{:S(2)}, u32[]{:S(2)}) collective-permute-start(bf16[2,64,2048]{2,1,0:T(8,128)(2,1)} %pad_maximum_fusion.3), channel_id=1, source_target_pairs={{1,0},{2,1},{3,2},{4,3},{5,4},{6,5},{7,6},{8,7},{9,8},{10,9},{11,1... | collective-permute-start | bytes 1572872 | tf_op jit(solution)/shard_map/ppermute | solution.py:38
  54.6 1.3 copy-start
  84.8 0.8 copy-start.4
  85.6 133.6 %all-to-all-start.1 = ((bf16[32,656,128]{2,1,0:T(8,128)(2,1)}), bf16[32,656,128]{2,1,0:T(8,128)(2,1)}, u32[]{:S(2)}, u32[]{:S(2)}) async-start(bf16[32,656,128]{2,1,0:T(8,128)(2,1)} %get-tuple-element.81), calls=%async_computation.1 | async-start | bytes 10747904 | tf_op jit(solution)/shard_map/all_to_all | solution.py:525
  223.3 111.7 %all-to-all-start.2 = ((bf16[32,592,128]{2,1,0:T(8,128)(2,1)}), bf16[32,592,128]{2,1,0:T(8,128)(2,1)}, u32[]{:S(2)}, u32[]{:S(2)}) async-start(bf16[32,592,128]{2,1,0:T(8,128)(2,1)} %broadcast_dynamic-update-slice_fusion), calls=%async_computation.2 | async-start | bytes 9699328 | tf_op jit(solution)/shard_map/all_to_all | solution.py:525
  337.4 120.6 %all-to-all-start.3 = ((bf16[32,640,128]{2,1,0:T(8,128)(2,1)}), bf16[32,640,128]{2,1,0:T(8,128)(2,1)}, u32[]{:S(2)}, u32[]{:S(2)}) async-start(bf16[32,640,128]{2,1,0:T(8,128)(2,1)} %constant_dynamic-update-slice_fusion), calls=%async_computation.3 | async-start | bytes 10485760 | tf_op jit(solution)/shard_map/all_to_all | solution.py:525
  410.2 51.5 %copy-start.2 = (f32[384,2048]{1,0:T(8,128)S(1)}, f32[384,2048]{1,0:T(8,128)}, u32[]{:S(2)}) copy-start(f32[384,2048]{1,0:T(8,128)} %get-tuple-element.93.padded_ref) | copy-start | bytes 9437188
  458.1 166.0 %all-to-all-start.4 = ((bf16[32,704,128]{2,1,0:T(8,128)(2,1)}), bf16[32,704,128]{2,1,0:T(8,128)(2,1)}, u32[]{:S(2)}, u32[]{:S(2)}) async-start(bf16[32,704,128]{2,1,0:T(8,128)(2,1)} %maximum_dynamic-update-slice_fusion), calls=%async_computation.4 | async-start | bytes 11534336 | tf_op jit(solution)/shard_map/all_to_all | solution.py:525
  461.7 3.9 copy-start.3
  462.0 9.5 %collective-permute-start.3 = (bf16[64,2048]{1,0:T(8,128)(2,1)S(1)}, bf16[64,2048]{1,0:T(8,128)(2,1)S(1)}, u32[]{:S(2)}, u32[]{:S(2)}) collective-permute-start(bf16[64,2048]{1,0:T(8,128)(2,1)S(1)} %get-tuple-element.115), channel_id=1, source_target_pairs={{0,1},{1,2},{2,3},{3,4},{4,5},{5,6},{6,7},{7,8},{8,9},{9,10},{10,1... | collective-permute-start | bytes 786440 | tf_op jit(solution)/shard_map/ppermute | solution.py:38
  464.3 7.3 %collective-permute-start.2 = (bf16[64,2048]{1,0:T(8,128)(2,1)S(1)}, bf16[64,2048]{1,0:T(8,128)(2,1)S(1)}, u32[]{:S(2)}, u32[]{:S(2)}) collective-permute-start(bf16[64,2048]{1,0:T(8,128)(2,1)S(1)} %get-tuple-element.116), channel_id=1, source_target_pairs={{1,0},{2,1},{3,2},{4,3},{5,4},{6,5},{7,6},{8,7},{9,8},{10,9},{11,1... | collective-permute-start | bytes 786440 | tf_op jit(solution)/shard_map/ppermute | solution.py:38
  465.9 172.4 %collective-permute-start.5 = (bf16[64,2048]{1,0:T(8,128)(2,1)S(1)}, bf16[64,2048]{1,0:T(8,128)(2,1)S(1)}, u32[]{:S(2)}, u32[]{:S(2)}) collective-permute-start(bf16[64,2048]{1,0:T(8,128)(2,1)S(1)} %get-tuple-element.113), channel_id=1, source_target_pairs={{0,1},{1,2},{2,3},{3,4},{4,5},{5,6},{6,7},{7,8},{8,9},{9,10},{10,1... | collective-permute-start | bytes 786440 | tf_op jit(solution)/shard_map/ppermute | solution.py:38
  470.1 168.3 %collective-permute-start.4 = (bf16[64,2048]{1,0:T(8,128)(2,1)S(1)}, bf16[64,2048]{1,0:T(8,128)(2,1)S(1)}, u32[]{:S(2)}, u32[]{:S(2)}) collective-permute-start(bf16[64,2048]{1,0:T(8,128)(2,1)S(1)} %get-tuple-element.114), channel_id=1, source_target_pairs={{1,0},{2,1},{3,2},{4,3},{5,4},{6,5},{7,6},{8,7},{9,8},{10,9},{11,1... | collective-permute-start | bytes 786440 | tf_op jit(solution)/shard_map/ppermute | solution.py:38
  471.6 0.7 copy-start.7
  471.6 0.8 copy-start.8
  638.3 0.7 copy-start.5
  638.3 0.8 copy-start.6

commit v6 on v5

--- a/solution.py
+++ b/solution.py
@@ -620,19 +620,18 @@
     def summed(block):
         return jnp.sum(block.astype(jnp.float32), axis=0).astype(jnp.bfloat16).reshape(share, width)
 
-    def collected(first, second, number):
-        got = collect(jnp.concatenate([first, second]).reshape(16, -1), owners, number)
-        return got.reshape(owners, 2, share, width).transpose(1, 0, 2, 3).reshape(2, EDGE, width)
-
-    returned_v, dv = lax.optimization_barrier((returned_v, dv))
-    global_v, edge_out = collected(summed(returned_v[:, filled:]), out_row.reshape(share, width), 1)
-    returned_k, dv, global_v, edge_out = lax.optimization_barrier(
-        (returned_k, dv, global_v, edge_out)
-    )
+    returned_k, dv = lax.optimization_barrier((returned_k, dv))
     count = share * width // HD
-    global_k, edge_dq = collected(
-        summed(returned_k[:, filled : filled + count]), summed(returned_k[:, filled + count :]), 2
-    )
+    piece = jnp.concatenate(
+        [
+            summed(returned_k[:, filled : filled + count]),
+            summed(returned_v[:, filled:]),
+            summed(returned_k[:, filled + count :]),
+            out_row.reshape(share, width),
+        ]
+    )
+    got = collect(piece, owners, 1).reshape(owners, 4, share, width)
+    global_k, global_v, edge_dq, edge_out = got.transpose(1, 0, 2, 3).reshape(4, EDGE, width)
     dk, att, dq, dv, gain_term = final(
         final_key_kernel, 0, capacity, place, served,
         (returned_k, key_padded, local, *near_k),

time: 676 us -> 667 us (0.987)
  Pallas kernels: 325 us -> 214 us
  waiting for transfers between devices: 246 us -> 346 us
    pallas_call x2 -> x1, Pallas kernels: 137 us -> 26.5 us  [collect(): pl.pallas_call(functools.partial(collect_kernel, count), in_specs=[WHOLE]...]
    all_to_all x4, waiting for transfers between devices: 246 us -> 346 us  [exchange(): return lax.all_to_all(slots, 'seq', split_axis=0, concat_axis=0, tiled=True)]
  transfers between devices with their start and end apart: 11 -> 11, of which waited for: 3 -> 4; matrix products, arithmetic and copies ran while one was open for 4% -> 5% of each run, Pallas kernels for 45% -> 29%
where the time goes in v6:
time: 667 us; the launch traced here: 665 us
  waiting for transfers between devices  346 us (52%)
  Pallas kernels  214 us (32%)
  starting transfers between devices  45.2 us (7%)
  local copies, waits for them, and re-layouts  27.5 us (4%)
  other arithmetic  18.2 us (3%)
  blocking collectives  12.3 us (2%)
    all_to_all x4, waiting for transfers between devices, exchange(): return lax.all_to_all(slots, 'seq', split_axis=0, concat_axis=0, tiled=True)  346 us
    pallas_call x2, Pallas kernels, sparse(): pl.pallas_call(functools.partial(kernel, per_dev, capacity), grid_spec=pl...  75.1 us
    pallas_call x2, Pallas kernels, final(): pl.pallas_call(functools.partial(kernel, per_dev, capacity), grid_spec=pl...  40.1 us
    pallas_call x1, Pallas kernels, spread(): pl.pallas_call(functools.partial(spread_kernel, count), in_specs=[WHOLE],...  35.5 us
    pallas_call x1, Pallas kernels, collect(): pl.pallas_call(functools.partial(collect_kernel, count), in_specs=[WHOLE]...  26.5 us
    pallas_call x2, Pallas kernels, edge_call(): pl.pallas_call(kernel, grid=(HEADS,), in_specs=specs, out_specs=out_specs...  26.3 us
    all_to_all x4, starting transfers between devices, exchange(): return lax.all_to_all(slots, 'seq', split_axis=0, concat_axis=0, tiled=True)  25.3 us
  transfers between devices with their start and end apart: 11, of which 4 were waited for; matrix products, arithmetic and copies ran while one was open for 5% of the time, Pallas kernels for 29%

profile of v6, /device:TPU:0, one launch (start us, length us, event | category | flops | bytes accessed | tf_op | source)
XLA Modules:
  0.0 664.7 jit_solution(1477318914022572343)
XLA Ops:
  3.5 7.3 %all-to-all-start = ((s32[32,1,9]{2,1,0:T(1,128)}), s32[32,1,9]{2,1,0:T(1,128)S(1)}, u32[]{:S(2)}, u32[]{:S(2)}) async-start(s32[32,1,9]{2,1,0:T(1,128)} %bitcast.2), calls=%async_computation | async-start | bytes 32768 | tf_op jit(solution)/shard_map/all_to_all | solution.py:520
  10.8 1.1 fusion.16
  11.9 0.9 multiply_convert_fusion.k_ref.key_ref
  12.9 1.0 pad_maximum_fusion.2
  13.9 2.2 collective-permute-start
  16.9 1.4 collective-permute-start.1
  18.7 35.5 %spread.1 = bf16[32,16,2048]{2,1,0:T(8,128)(2,1)S(1)} custom-call(bf16[32,16,2048]{2,1,0:T(8,128)(2,1)S(1)} %bitcast.81), custom_call_target="tpu_custom_call" | custom-call | tf_op jit(solution)/shard_map/spread/pallas_call | solution.py:111
  54.2 1.3 copy-done
  55.5 12.5 %sums.1 = (f32[16,1,128]{2,1,0:T(1,128)}, f32[16,1,128]{2,1,0:T(1,128)}, f32[128,2048]{1,0:T(8,128)}) custom-call(bf16[4,128,2048]{2,1,0:T(8,128)(2,1)} %bitcast.77, bf16[256,2048]{1,0:T(8,128)(2,1)} %copy-done.1, bf16[256,2048]{1,0:T(8,128)(2,1)} %bitcast.82), custom_call_target="tpu_custom_call" | custom-call | tf_op jit(solution)/shard_map/sums/pallas_call | solution.py:374
  68.1 1.3 convert_element_type.82
  72.7 11.0 %pick.1 = (bf16[32,656,128]{2,1,0:T(8,128)(2,1)}, bf16[32,592,128]{2,1,0:T(8,128)(2,1)}) custom-call(s32[288]{0:T(512)} %reshape.587.index_ref.served_ref, bf16[256,2048]{1,0:T(8,128)(2,1)} %copy-done.1, bf16[256,2048]{1,0:T(8,128)(2,1)} %bitcast.83, bf16[32,80,128]{2,1,0:T(8,128)(2,1)} %pad_maximum_fusion.1.extra_ref), custom_call_target="tpu_custom_call" | custom-call | tf_op jit(solution)/shard_map/pick/pallas_call | solution.py:205
  84.6 14.0 %all-to-all-start.1 = ((bf16[32,656,128]{2,1,0:T(8,128)(2,1)}), bf16[32,656,128]{2,1,0:T(8,128)(2,1)}, u32[]{:S(2)}, u32[]{:S(2)}) async-start(bf16[32,656,128]{2,1,0:T(8,128)(2,1)} %get-tuple-element.77), calls=%async_computation.1 | async-start | bytes 10747904 | tf_op jit(solution)/shard_map/all_to_all | solution.py:525
  98.5 1.1 slice.206
  99.6 118.6 %all-to-all-done.1.arrived_ref = bf16[32,656,128]{2,1,0:T(8,128)(2,1)} async-done(((bf16[32,656,128]{2,1,0:T(8,128)(2,1)}), bf16[32,656,128]{2,1,0:T(8,128)(2,1)}, u32[]{:S(2)}, u32[]{:S(2)}) %all-to-all-start.1) | async-done | bytes 5373984 | tf_op jit(solution)/shard_map/all_to_all | solution.py:525
  218.2 0.9 slice.228
  219.8 1.4 multiply_reduce_fusion
  222.2 3.6 all-to-all-start.2
  226.4 27.9 %value_terms.1 = (f32[128,2048]{1,0:T(8,128)}, f32[384,2048]{1,0:T(8,128)}, bf16[32,640,128]{2,1,0:T(8,128)(2,1)}) custom-call(s32[2]{0:T(128)} %pad_add_fusion.place_ref, s32[192]{0:T(256)} %copy-done.10, bf16[256,2048]{1,0:T(8,128)(2,1)} %bitcast.87, bf16[256,2048]{1,0:T(8,128)(2,1)} %bitcast.89, bf16[256,2048]{1,0:T(8,128)(2,1)} %copy-done.1, ...), custom_call_target="tpu_custom_call" | custom-call | tf_op jit(solution)/shard_map/value_terms/pallas_call | solution.py:330
  254.2 79.7 %all-to-all-done.2.arrived_v_ref = bf16[32,592,128]{2,1,0:T(8,128)(2,1)} async-done(((bf16[32,592,128]{2,1,0:T(8,128)(2,1)}), bf16[32,592,128]{2,1,0:T(8,128)(2,1)}, u32[]{:S(2)}, u32[]{:S(2)}) %all-to-all-start.2) | async-done | bytes 4849696 | tf_op jit(solution)/shard_map/all_to_all | solution.py:525
  333.9 1.3 convert_element_type.95
  335.4 0.9 constant_dynamic-update-slice_fusion
  336.3 3.9 all-to-all-start.3
  340.2 0.9 slice.208
  343.8 47.2 %key_terms.1 = (f32[128,2048]{1,0:T(8,128)}, f32[384,2048]{1,0:T(8,128)}, bf16[32,704,128]{2,1,0:T(8,128)(2,1)}, bf16[256,2048]{1,0:T(8,128)(2,1)}, bf16[256,2048]{1,0:T(8,128)(2,1)}) custom-call(s32[2]{0:T(128)} %pad_add_fusion.place_ref, s32[192]{0:T(256)} %copy-done.10, bf16[256,2048]{1,0:T(8,128)(2,1)} %bitcast.88, bf16[256,2048]{1,0:T(8,128)(2,1)} %bitcast.90, ...), custom_call_target="tpu_custom_call" | custom-call | tf_op jit(solution)/shard_map/key_terms/pallas_call | solution.py:330
  391.0 1.3 convert_element_type.91
  392.6 13.8 %grads.1 = (f32[128,2048]{1,0:T(8,128)}, f32[2,256,2048]{2,1,0:T(8,128)}) custom-call(bf16[4,128,2048]{2,1,0:T(8,128)(2,1)} %bitcast.80, bf16[256,2048]{1,0:T(8,128)(2,1)} %copy-done.1, bf16[256,2048]{1,0:T(8,128)(2,1)} %bitcast.85, f32[16,1,128]{2,1,0:T(1,128)} %copy.70.top_ref, f32[16,1,128]{2,1,0:T(1,128)} %copy.71.total_ref, f32[16,1,128]{2,1,0:T(1,128)} %copy.72.delta_ref), custom_call_target="tpu_custom_call" | custom-call | tf_op jit(solution)/shard_map/grads/pallas_call | solution.py:374
  406.4 1.3 convert_element_type.94
  407.9 1.3 maximum_dynamic-update-slice_fusion
  409.2 47.8 %all-to-all-done.3.returned_ref = bf16[32,640,128]{2,1,0:T(8,128)(2,1)} async-done(((bf16[32,640,128]{2,1,0:T(8,128)(2,1)}), bf16[32,640,128]{2,1,0:T(8,128)(2,1)}, u32[]{:S(2)}, u32[]{:S(2)}) %all-to-all-start.3) | async-done | bytes 5242912 | tf_op jit(solution)/shard_map/all_to_all | solution.py:525
  456.9 3.9 all-to-all-start.4
  461.2 2.1 collective-permute-start.3
  463.3 1.3 collective-permute-start.2
  464.9 4.2 collective-permute-start.5
  469.1 1.5 collective-permute-start.4
  470.6 1.1 slice_reduce_fusion.1
  472.5 19.0 %final_value.1.dv_ref = f32[256,2048]{1,0:T(8,128)} custom-call(s32[2]{0:T(128)} %pad_add_fusion.place_ref, s32[288]{0:T(512)} %reshape.587.index_ref.served_ref, bf16[32,640,128]{2,1,0:T(8,128)(2,1)} %all-to-all-done.3.returned_ref, f32[384,2048]{1,0:T(8,128)} %get-tuple-element.89.padded_ref, f32[2,256,2048]{2,1,0:T(8,128)} %get-tuple-element.90.local_ref, ...), custom_call_target="tpu_custom_call" | custom-call | tf_op jit(solution)/shard_map/final_value/pallas_call | solution.py:472
  491.5 99.6 %all-to-all-done.4.returned_ref = bf16[32,704,128]{2,1,0:T(8,128)(2,1)} async-done(((bf16[32,704,128]{2,1,0:T(8,128)(2,1)}), bf16[32,704,128]{2,1,0:T(8,128)(2,1)}, u32[]{:S(2)}, u32[]{:S(2)}) %all-to-all-start.4) | async-done | bytes 5767200 | tf_op jit(solution)/shard_map/all_to_all | solution.py:525
  591.1 1.4 slice_reduce_fusion.2
  592.5 26.5 %collect_1.1 = bf16[32,16,2048]{2,1,0:T(8,128)(2,1)S(1)} custom-call(bf16[16,2048]{1,0:T(8,128)(2,1)S(1)} %pad_maximum_fusion.4.in_ref), custom_call_target="tpu_custom_call" | custom-call | tf_op jit(solution)/shard_map/collect_1/pallas_call | solution.py:165
  619.0 2.2 reshape.601
  621.2 2.9 copy.91
  624.1 1.1 fusion.13
  625.2 0.9 unstack.31.eout_ref
  626.1 0.9 unstack.29.edq_ref
  627.0 0.9 unstack.27.gv_ref
  628.0 0.9 unstack.25.gk_ref
  629.7 21.1 %final_key.1 = (bf16[256,2048]{1,0:T(8,128)(2,1)}, bf16[256,2048]{1,0:T(8,128)(2,1)}, bf16[256,2048]{1,0:T(8,128)(2,1)}, bf16[256,2048]{1,0:T(8,128)(2,1)}, f32[1,2048]{1,0:T(1,128)}) custom-call(s32[2]{0:T(128)} %pad_add_fusion.place_ref, s32[288]{0:T(512)} %reshape.587.index_ref.served_ref, bf16[32,704,128]{2,1,0:T(8,128)(2,1)} %all-to-all-done.4.returned_ref, ...), custom_call_target="tpu_custom_call" | custom-call | tf_op jit(solution)/shard_map/final_key/pallas_call | solution.py:472
  651.6 12.3 %all_to_all.31 = f32[32,1,2048]{2,1,0:T(1,128)S(1)} all-to-all(f32[32,1,2048]{2,1,0:T(1,128)S(1)} %broadcast_in_dim.58), channel_id=1, replica_groups=mesh['dp'=1,'seq'=32] {'seq'}, dimensions={0} | all-to-all | bytes 524288 | tf_op jit(solution)/shard_map/all_to_all | solution.py:529
  (110 shorter events, 17.5 us)
Async XLA Ops:
  0.6 11.3 %copy-start.4 = (bf16[1,256,2048]{2,1,0:T(8,128)(2,1)S(1)}, bf16[1,256,2048]{2,1,0:T(8,128)(2,1)}, u32[]{:S(2)}) copy-start(bf16[1,256,2048]{2,1,0:T(8,128)(2,1)} %param.13) | copy-start | bytes 3145732
  2.7 10.2 %copy-start.10 = (s32[192]{0:T(256)}, s32[192]{0:T(256)S(1)}, u32[]{:S(2)}) copy-start(s32[192]{0:T(256)S(1)} %multiply_add_fusion.pos_ref) | copy-start | bytes 2308
  3.5 67.4 %all-to-all-start = ((s32[32,1,9]{2,1,0:T(1,128)}), s32[32,1,9]{2,1,0:T(1,128)S(1)}, u32[]{:S(2)}, u32[]{:S(2)}) async-start(s32[32,1,9]{2,1,0:T(1,128)} %bitcast.2), calls=%async_computation | async-start | bytes 32768 | tf_op jit(solution)/shard_map/all_to_all | solution.py:520
  12.8 5.5 copy-start.1
  13.9 69.9 %collective-permute-start = (bf16[2,64,2048]{2,1,0:T(8,128)(2,1)}, bf16[2,64,2048]{2,1,0:T(8,128)(2,1)S(1)}, u32[]{:S(2)}, u32[]{:S(2)}) collective-permute-start(bf16[2,64,2048]{2,1,0:T(8,128)(2,1)} %pad_maximum_fusion.2), channel_id=1, source_target_pairs={{0,1},{1,2},{2,3},{3,4},{4,5},{5,6},{6,7},{7,8},{8,9},{9,10},{10,1... | collective-permute-start | bytes 1572872 | tf_op jit(solution)/shard_map/ppermute | solution.py:38
  16.9 1.5 slice-start
  16.9 1.5 slice-start.1
  16.9 1.5 slice-start.2
  16.9 66.9 %collective-permute-start.1 = (bf16[2,64,2048]{2,1,0:T(8,128)(2,1)}, bf16[2,64,2048]{2,1,0:T(8,128)(2,1)}, u32[]{:S(2)}, u32[]{:S(2)}) collective-permute-start(bf16[2,64,2048]{2,1,0:T(8,128)(2,1)} %pad_maximum_fusion.3), channel_id=1, source_target_pairs={{1,0},{2,1},{3,2},{4,3},{5,4},{6,5},{7,6},{8,7},{9,8},{10,9},{11,1... | collective-permute-start | bytes 1572872 | tf_op jit(solution)/shard_map/ppermute | solution.py:38
  54.2 1.3 copy-start
  68.1 1.6 copy-start.11
  68.1 1.6 copy-start.12
  83.8 0.8 copy-start.5
  84.6 133.6 %all-to-all-start.1 = ((bf16[32,656,128]{2,1,0:T(8,128)(2,1)}), bf16[32,656,128]{2,1,0:T(8,128)(2,1)}, u32[]{:S(2)}, u32[]{:S(2)}) async-start(bf16[32,656,128]{2,1,0:T(8,128)(2,1)} %get-tuple-element.77), calls=%async_computation.1 | async-start | bytes 10747904 | tf_op jit(solution)/shard_map/all_to_all | solution.py:525
  222.2 111.7 %all-to-all-start.2 = ((bf16[32,592,128]{2,1,0:T(8,128)(2,1)}), bf16[32,592,128]{2,1,0:T(8,128)(2,1)}, u32[]{:S(2)}, u32[]{:S(2)}) async-start(bf16[32,592,128]{2,1,0:T(8,128)(2,1)} %broadcast_dynamic-update-slice_fusion), calls=%async_computation.2 | async-start | bytes 9699328 | tf_op jit(solution)/shard_map/all_to_all | solution.py:525
  336.3 120.6 %all-to-all-start.3 = ((bf16[32,640,128]{2,1,0:T(8,128)(2,1)}), bf16[32,640,128]{2,1,0:T(8,128)(2,1)}, u32[]{:S(2)}, u32[]{:S(2)}) async-start(bf16[32,640,128]{2,1,0:T(8,128)(2,1)} %constant_dynamic-update-slice_fusion), calls=%async_computation.3 | async-start | bytes 10485760 | tf_op jit(solution)/shard_map/all_to_all | solution.py:525
  456.9 3.9 copy-start.2
  456.9 134.1 %all-to-all-start.4 = ((bf16[32,704,128]{2,1,0:T(8,128)(2,1)}), bf16[32,704,128]{2,1,0:T(8,128)(2,1)}, u32[]{:S(2)}, u32[]{:S(2)}) async-start(bf16[32,704,128]{2,1,0:T(8,128)(2,1)} %maximum_dynamic-update-slice_fusion), calls=%async_computation.4 | async-start | bytes 11534336 | tf_op jit(solution)/shard_map/all_to_all | solution.py:525
  460.9 3.7 copy-start.3
  461.2 10.5 %collective-permute-start.3 = (bf16[64,2048]{1,0:T(8,128)(2,1)S(1)}, bf16[64,2048]{1,0:T(8,128)(2,1)S(1)}, u32[]{:S(2)}, u32[]{:S(2)}) collective-permute-start(bf16[64,2048]{1,0:T(8,128)(2,1)S(1)} %get-tuple-element.111), channel_id=1, source_target_pairs={{0,1},{1,2},{2,3},{3,4},{4,5},{5,6},{6,7},{7,8},{8,9},{9,10},{10,1... | collective-permute-start | bytes 786440 | tf_op jit(solution)/shard_map/ppermute | solution.py:38
  463.3 8.5 %collective-permute-start.2 = (bf16[64,2048]{1,0:T(8,128)(2,1)S(1)}, bf16[64,2048]{1,0:T(8,128)(2,1)S(1)}, u32[]{:S(2)}, u32[]{:S(2)}) collective-permute-start(bf16[64,2048]{1,0:T(8,128)(2,1)S(1)} %get-tuple-element.112), channel_id=1, source_target_pairs={{1,0},{2,1},{3,2},{4,3},{5,4},{6,5},{7,6},{8,7},{9,8},{10,9},{11,1... | collective-permute-start | bytes 786440 | tf_op jit(solution)/shard_map/ppermute | solution.py:38
  464.9 164.0 %collective-permute-start.5 = (bf16[64,2048]{1,0:T(8,128)(2,1)S(1)}, bf16[64,2048]{1,0:T(8,128)(2,1)S(1)}, u32[]{:S(2)}, u32[]{:S(2)}) collective-permute-start(bf16[64,2048]{1,0:T(8,128)(2,1)S(1)} %get-tuple-element.109), channel_id=1, source_target_pairs={{0,1},{1,2},{2,3},{3,4},{4,5},{5,6},{6,7},{7,8},{8,9},{9,10},{10,1... | collective-permute-start | bytes 786440 | tf_op jit(solution)/shard_map/ppermute | solution.py:38
  469.1 159.8 %collective-permute-start.4 = (bf16[64,2048]{1,0:T(8,128)(2,1)S(1)}, bf16[64,2048]{1,0:T(8,128)(2,1)S(1)}, u32[]{:S(2)}, u32[]{:S(2)}) collective-permute-start(bf16[64,2048]{1,0:T(8,128)(2,1)S(1)} %get-tuple-element.110), channel_id=1, source_target_pairs={{1,0},{2,1},{3,2},{4,3},{5,4},{6,5},{7,6},{8,7},{9,8},{10,9},{11,1... | collective-permute-start | bytes 786440 | tf_op jit(solution)/shard_map/ppermute | solution.py:38
  471.7 0.7 copy-start.8
  471.8 0.8 copy-start.9
  628.9 0.7 copy-start.6
  628.9 0.8 copy-start.7
